TPU v7x, 512 devices: a whole 4x8x8 slice. The times are simulated.
512 devices in a mesh: dp: 32 (over z, y_hi), seq: 16 (over x, y_lo, core).
Axes of the slice: x: 4, y: 8 (y_hi: 4, y_lo: 2; y = y_hi * 2 + y_lo), z: 8, core: 2. Of those that a mesh axis runs over, the one named last changes fastest.
Arguments:
- latents: bfloat16 [32, 16, 128, 1152], P('dp', 'seq'), may hold values from -6 to 6
- targets: bfloat16 [32, 16, 128, 1152], P('dp', 'seq'), may hold values from -6 to 6
- modulation: float32 [32, 2, 3, 1152], P('dp'), may hold values from -3 to 3
- query_key_value_weight: bfloat16 [2, 1152, 1728], P(None, 'dp'), may hold values from -0.1875 to 0.1875
- output_projection_weight: bfloat16 [2, 576, 1152], P(None, 'dp'), may hold values from -0.25 to 0.25
- adapter_down_weight: float32 [2, 1152, 64], replicated, may hold values from -0.1875 to 0.1875
- adapter_up_weight: float32 [2, 64, 1728], replicated, may hold values from -0.75 to 0.75
Outputs:
- grad_down: float32 [2, 1152, 64], replicated
- grad_up: float32 [2, 64, 1728], replicated
All inputs are finite; a program needn't handle non-finite values.
Results may differ from a plain program's by a relative error of at most 0.0027.
Values may be sent and summed in bfloat16 or wider, within the bound.
No kernel may reach another device: no remote copies, remote signals or barrier semaphores. Data moves between devices by JAX's collectives and lax.ppermute only.
A program may use at most 128 MiB of HBM per device.

v0:
```python
import math

import jax
import jax.numpy as jnp
from jax import lax
from jax.sharding import PartitionSpec as P

MODEL_WIDTH = 1152
HEADS = 8
HEAD = 72


def layer_norm(values):
    average = jnp.mean(values, -1, keepdims=True)
    centred = values - average
    spread = jnp.mean(centred * centred, -1, keepdims=True)
    return centred * lax.rsqrt(spread + 1e-06)


def head_norm(values):
    return values * lax.rsqrt(jnp.mean(values * values, -1, keepdims=True) + 1e-06)


def rotary(values, count):
    half_head = HEAD // 2
    position = jnp.arange(count).astype(jnp.float32)
    frequency = jnp.exp(
        jnp.arange(half_head).astype(jnp.float32) * (-2.0 * math.log(10000.0) / HEAD)
    )
    angles = position[:, None] * frequency[None, :]
    cosine = jnp.cos(angles)[:, None, None, :]
    sine_part = jnp.sin(angles)[:, None, None, :]
    first = values[..., :half_head]
    second = values[..., half_head:]
    return jnp.concatenate(
        [first * cosine - second * sine_part, second * cosine + first * sine_part], -1
    )


def block(
    hidden,
    apply_modulation,
    query_key_value_weight,
    output_projection_weight,
    low_down,
    low_up,
    temporal_block,
):
    in_shape = hidden.shape
    normed = layer_norm(hidden.reshape(-1, MODEL_WIDTH).astype(jnp.float32))
    modded = (normed * (1.0 + apply_modulation[1]) + apply_modulation[0]).astype(jnp.bfloat16)
    frozen_part = jnp.dot(modded, query_key_value_weight, preferred_element_type=jnp.float32)
    reduced = jnp.dot(modded.astype(jnp.float32), low_down, precision=lax.Precision.HIGHEST)
    projected = frozen_part + jnp.dot(reduced, low_up, precision=lax.Precision.HIGHEST)
    projected = projected.reshape(in_shape[0], in_shape[1], 3, HEADS, HEAD)
    queries = head_norm(projected[:, :, 0])
    key_vecs = head_norm(projected[:, :, 1])
    if temporal_block:
        queries = rotary(queries, in_shape[0])
        key_vecs = rotary(key_vecs, in_shape[0])
    queries = queries.astype(jnp.bfloat16)
    key_vecs = key_vecs.astype(jnp.bfloat16)
    value_vecs = projected[:, :, 2].astype(jnp.bfloat16)
    if temporal_block:
        scores = jnp.einsum(
            "frhe,grhe->rhfg", queries, key_vecs, preferred_element_type=jnp.float32
        )
    else:
        scores = jnp.einsum(
            "fshe,fthe->fhst", queries, key_vecs, preferred_element_type=jnp.float32
        )
    scores = scores * (1.0 / math.sqrt(HEAD))
    weights = jnp.exp(scores)
    weights = (weights / jnp.sum(weights, -1, keepdims=True)).astype(jnp.bfloat16)
    if temporal_block:
        attended = jnp.einsum(
            "rhfg,grhe->frhe", weights, value_vecs, preferred_element_type=jnp.float32
        )
    else:
        attended = jnp.einsum(
            "fhst,fthe->fshe", weights, value_vecs, preferred_element_type=jnp.float32
        )
    attended = attended.astype(jnp.bfloat16).reshape(-1, HEADS * HEAD)
    mixed = jnp.dot(attended, output_projection_weight, preferred_element_type=jnp.float32)
    updated = hidden.reshape(-1, MODEL_WIDTH).astype(jnp.float32) + apply_modulation[2] * mixed
    return updated.astype(jnp.bfloat16).reshape(in_shape)


def on_device(
    latents,
    targets,
    modulation,
    query_key_value_weight,
    output_projection_weight,
    adapter_down_weight,
    adapter_up_weight,
):
    hidden = latents[0]
    apply_modulation = modulation[0]
    qkv_whole, out_whole = (
        lax.all_gather(query_key_value_weight, "dp", axis=1, tiled=True),
        lax.all_gather(output_projection_weight, "dp", axis=1, tiled=True),
    )
    qkv_first, out_first = (qkv_whole[0], out_whole[0])

    def spatial_block(low_down, low_up):
        return block(hidden, apply_modulation[0], qkv_first, out_first, low_down, low_up, False)

    middle_state, spatial_block_backward = jax.vjp(
        spatial_block, adapter_down_weight[0], adapter_up_weight[0]
    )
    token_row_layout = lax.all_to_all(middle_state, "seq", split_axis=1, concat_axis=0, tiled=True)
    qkv_second, out_second = (qkv_whole[1], out_whole[1])

    def temporal_block(row_input, low_down, low_up):
        return block(row_input, apply_modulation[1], qkv_second, out_second, low_down, low_up, True)

    produced_output, temporal_block_backward = jax.vjp(
        temporal_block, token_row_layout, adapter_down_weight[1], adapter_up_weight[1]
    )
    frame_out = lax.all_to_all(produced_output, "seq", split_axis=0, concat_axis=1, tiled=True)
    frame_error = (
        (frame_out.astype(jnp.float32) - targets[0].astype(jnp.float32)) / MODEL_WIDTH
    ).astype(jnp.bfloat16)
    error_grad = lax.all_to_all(frame_error, "seq", split_axis=1, concat_axis=0, tiled=True)
    row_grad, down_late, up_late = temporal_block_backward(error_grad)
    frame_grad = lax.all_to_all(row_grad, "seq", split_axis=0, concat_axis=1, tiled=True)
    down_early, up_early = spatial_block_backward(frame_grad)
    down_early, up_early, down_late, up_late = lax.psum(
        (down_early, up_early, down_late, up_late), ("dp", "seq")
    )
    return (jnp.stack([down_early, down_late]), jnp.stack([up_early, up_late]))


def solution(mesh):
    in_specs = (
        P("dp", "seq", None, None),
        P("dp", "seq", None, None),
        P("dp", None, None, None),
        P(None, "dp", None),
        P(None, "dp", None),
        P(),
        P(),
    )
    out_specs = (P(), P())
    return jax.shard_map(
        on_device, mesh=mesh, in_specs=in_specs, out_specs=out_specs, check_vma=False
    )
```

profile of v0, /device:TPU:1, one launch (start us, length us, event | category | flops | bytes accessed | tf_op | source)
XLA Modules:
  0.0 692.7 jit_solution(2233761080926237757)
XLA Ops:
  8.6 1.5 slice_reduce_fusion.1
  10.1 1.1 convert_reduce_fusion.1
  11.2 1.2 fusion.60
  12.4 1.6 fusion.112
  14.6 2.6 fusion.87
  17.2 86.5 %all-gather.5.cloned.1.call-done = bf16[2,576,1152]{2,0,1:T(2,128)(2,1)} async-done(((bf16[2,18,1152]{2,0,1:T(2,128)(2,1)}), bf16[2,576,1152]{2,0,1:T(2,128)(2,1)}) %all-gather.5.cloned.1.call-update) | async-done | bytes 2654224 | tf_op jit(solution)/shard_map/all_gather | solution.py:102
  103.8 8.5 %fusion.152 = (bf16[1,576,1152]{2,0,1:T(2,128)(2,1)}, bf16[1,576,1152]{2,0,1:T(2,128)(2,1)}) fusion(bf16[2,576,1152]{2,0,1:T(2,128)(2,1)} %all-gather.5.cloned.1.call-done), kind=kLoop, calls=%fused_computation.227 | loop fusion | bytes 5308416 | tf_op jit(solution)/shard_map/slice | solution.py:113
  112.3 131.3 %all-gather.3.cloned.1.call-done = bf16[2,1152,1728]{2,0,1:T(2,128)(2,1)} async-done(((bf16[2,36,1728]{2,0,1:T(2,128)(2,1)}), bf16[2,1152,1728]{2,0,1:T(2,128)(2,1)}) %all-gather.3.cloned.1.call-update) | async-done | bytes 7962640 | tf_op jit(solution)/shard_map/all_gather | solution.py:101
  243.5 17.0 %fusion.151 = (bf16[1,1152,1728]{2,0,1:T(2,128)(2,1)}, bf16[1,1152,1728]{2,0,1:T(2,128)(2,1)}) fusion(bf16[2,1152,1728]{2,0,1:T(2,128)(2,1)} %all-gather.3.cloned.1.call-done), kind=kLoop, calls=%fused_computation.226 | loop fusion | bytes 15925248 | tf_op jit(solution)/shard_map/slice | solution.py:113
  260.6 17.8 %copy.88 = bf16[1,1152,1728]{1,2,0:T(8,128)(2,1)} copy(bf16[1,1152,1728]{2,0,1:T(2,128)(2,1)} %get-tuple-element.19) | data formatting | bytes 7962624
  278.4 3.4 fusion.8
  285.1 2.4 reduce.25
  288.3 6.2 all-to-all-start
  294.7 17.8 %copy.90 = bf16[1,1152,1728]{1,2,0:T(8,128)(2,1)} copy(bf16[1,1152,1728]{2,0,1:T(2,128)(2,1)} %get-tuple-element.18) | data formatting | bytes 7962624
  313.7 1.5 fusion.104
  315.2 1.6 fusion.83
  316.8 4.4 fusion.11
  321.1 1.5 copy.64
  322.6 2.0 reshape.685
  324.6 1.3 fusion.153
  325.9 1.1 slice.120
  331.1 2.2 fusion.28
  333.3 12.9 %all_to_all.16 = bf16[16,8,1152]{2,1,0:T(8,128)(2,1)S(1)} all-to-all(bf16[16,8,1152]{2,1,0:T(8,128)(2,1)S(1)} %fusion.28), channel_id=1, replica_groups=mesh['dp'=32,'seq'=16] {'seq'}, dimensions={0} | all-to-all | bytes 589824 | tf_op jit(solution)/shard_map/all_to_all | solution.py:121
  346.2 1.4 reshape.696
  347.6 1.9 fusion.156
  349.5 2.4 reduce.26
  352.7 4.7 all-to-all-start.2
  358.0 6.8 all-to-all-done.2
  365.7 2.9 convolution_convert_fusion.12
  368.7 1.1 copy.72
  370.8 1.5 fusion.39
  372.3 1.7 multiply_reduce_fusion.3
  377.7 1.7 copy.76
  379.3 1.9 reshape.690
  381.3 2.1 fusion.81
  383.4 1.6 convolution_convert_fusion
  385.0 3.0 fusion.64
  388.4 1.0 fusion.98
  389.4 4.6 all-to-all-start.3
  394.4 1.1 convolution_bitcast_fusion
  395.5 1.4 convolution_bitcast_fusion.2
  396.9 4.6 all-to-all-done.3
  401.5 2.3 convolution_convert_fusion.11
  405.5 1.8 convolution_bitcast_fusion.3
  408.0 1.2 convolution_bitcast_fusion.1
  409.2 273.0 %all-reduce.13.cloned.1.call-done = (f32[1,1152,64]{1,2,0:T(8,128)}, f32[1,1152,64]{1,2,0:T(8,128)}, f32[1,64,1728]{2,1,0:T(8,128)}, f32[1,64,1728]{2,1,0:T(8,128)}) async-done(((f32[1,1152,64]{1,2,0:T(8,128)}, f32[1,1152,64]{1,2,0:T(8,128)}, f32[1,64,1728]{2,1,0:T(8,128)}, f32[1,64,1728]{2,1,0:T(8,128)}), (f32[1,1152,64]{1,2,0:T(8,128)}, f32[1,1152,64]{1,2,0:T(8,128)}, f32[1,64,1728]{2,1,0:T(8,128)}, ...) | async-done | bytes 1474576 | tf_op jit(solution)/shard_map/psum | solution.py:129
  682.2 2.1 pad_maximum_fusion
  684.3 1.9 pad_maximum_fusion.1
  (194 shorter events, 21.1 us)
Async XLA Ops:
  7.2 96.6 %all-gather.5.cloned.1.call-start = ((), (), s32[]{:S(2)}) async-start(), calls=%async_computation.5 | async-start | bytes 2737152 | tf_op jit(solution)/shard_map/all_gather | solution.py:102
  7.9 235.7 %all-gather.3.cloned.1.call-start = ((), (), s32[]{:S(2)}) async-start(), calls=%async_computation.4 | async-start | bytes 8515584 | tf_op jit(solution)/shard_map/all_gather | solution.py:101
  10.1 268.3 %copy-start.42 = (f32[1152]{0:T(1024)}, f32[1152]{0:T(1024)S(1)}, u32[]{:S(2)}) copy-start(f32[1152]{0:T(1024)S(1)} %get-tuple-element.8) | copy-start | bytes 13828
  10.1 268.3 %copy-start.44 = (f32[1152]{0:T(1024)}, f32[1152]{0:T(1024)S(1)}, u32[]{:S(2)}) copy-start(f32[1152]{0:T(1024)S(1)} %get-tuple-element.9) | copy-start | bytes 13828
  10.1 273.0 %copy-start.46 = (f32[1152]{0:T(1024)}, f32[1152]{0:T(1024)S(1)}, u32[]{:S(2)}) copy-start(f32[1152]{0:T(1024)S(1)} %get-tuple-element.7) | copy-start | bytes 13828
  10.1 306.6 %copy-start.48 = (f32[1152]{0:T(1024)}, f32[1152]{0:T(1024)S(1)}, u32[]{:S(2)}) copy-start(f32[1152]{0:T(1024)S(1)} %get-tuple-element.10) | copy-start | bytes 13828
  11.2 267.2 %copy-start.58 = (f32[128]{0:T(128)}, f32[128]{0:T(128)S(1)}, u32[]{:S(2)}) copy-start(f32[128]{0:T(128)S(1)} %broadcast_multiply_fusion.1) | copy-start | bytes 1540
  12.4 266.0 %copy-start.60 = (f32[128]{0:T(128)}, f32[128]{0:T(128)S(1)}, u32[]{:S(2)}) copy-start(f32[128]{0:T(128)S(1)} %add_rsqrt_fusion) | copy-start | bytes 1540
  260.6 17.8 %copy-start.1 = (bf16[1,1,128,1152]{3,2,1,0:T(8,128)(2,1)S(1)}, bf16[1,1,128,1152]{3,2,1,0:T(8,128)(2,1)}, u32[]{:S(2)}) copy-start(bf16[1,1,128,1152]{3,2,1,0:T(8,128)(2,1)} %param.7) | copy-start | bytes 884740
  281.8 1.8 copy-start
  282.8 4.6 copy-start.52
  288.3 24.1 %all-to-all-start = ((bf16[16,2,4608]{2,1,0:T(2,128)(2,1)}), bf16[16,2,4608]{2,1,0:T(2,128)(2,1)S(1)}, u32[]{:S(2)}, u32[]{:S(2)}) async-start(bf16[16,2,4608]{2,1,0:T(2,128)(2,1)} %reshape.706), calls=%async_computation | async-start | bytes 589824 | tf_op jit(solution)/shard_map/all_to_all | solution.py:112
  294.7 34.1 %copy-start.32 = (f32[16,36]{1,0:T(8,128)}, f32[16,36]{1,0:T(8,128)S(1)}, u32[]{:S(2)}) copy-start(f32[16,36]{1,0:T(8,128)S(1)} %get-tuple-element.39) | copy-start | bytes 6916
  312.4 2.7 copy-start.2
  312.8 8.3 %copy-start.54 = (f32[128]{0:T(128)}, f32[128]{0:T(128)S(1)}, u32[]{:S(2)}) copy-start(f32[128]{0:T(128)S(1)} %broadcast_multiply_fusion) | copy-start | bytes 1540
  313.1 8.1 %copy-start.56 = (f32[128]{0:T(128)}, f32[128]{0:T(128)S(1)}, u32[]{:S(2)}) copy-start(f32[128]{0:T(128)S(1)} %fusion.142) | copy-start | bytes 1540
  315.2 6.0 copy-start.27
  327.0 3.5 copy-start.16
  329.3 1.8 copy-start.50
  330.4 2.8 copy-start.4
  330.5 2.8 copy-start.29
  346.2 11.2 %copy-start.30 = (f32[8,8,16]{2,1,0:T(8,128)S(1)}, f32[8,8,16]{2,1,0:T(8,128)}, u32[]{:S(2)}) copy-start(f32[8,8,16]{2,1,0:T(8,128)} %copy-done.29) | copy-start | bytes 12292
  346.2 18.9 %copy-start.51 = (f32[1152]{0:T(1024)S(1)}, f32[1152]{0:T(1024)}, u32[]{:S(2)}) copy-start(f32[1152]{0:T(1024)} %get-tuple-element.6) | copy-start | bytes 13828
  352.7 12.1 %all-to-all-start.2 = ((bf16[16,2,4608]{2,1,0:T(2,128)(2,1)}), bf16[16,2,4608]{2,1,0:T(2,128)(2,1)S(1)}, u32[]{:S(2)}, u32[]{:S(2)}) async-start(bf16[16,2,4608]{2,1,0:T(2,128)(2,1)} %reshape.708), calls=%async_computation.2 | async-start | bytes 589824 | tf_op jit(solution)/shard_map/all_to_all | solution.py:125
  368.7 5.3 copy-start.13
  370.8 3.2 copy-start.5
  370.8 3.2 copy-start.15
  370.8 3.3 copy-start.31
  372.2 2.2 copy-start.9
  372.2 2.2 copy-start.11
  375.3 1.7 copy-start.22
  375.3 1.7 copy-start.18
  379.3 5.7 copy-start.55
  385.0 3.1 copy-start.63
  385.0 3.1 copy-start.57
  388.1 6.3 copy-start.53
  388.1 6.3 copy-start.49
  388.1 7.4 %copy-start.28 = (f32[128,64]{0,1:T(8,128)S(1)}, f32[128,64]{0,1:T(8,128)}, u32[]{:S(2)}) copy-start(f32[128,64]{0,1:T(8,128)} %copy-done.27) | copy-start | bytes 98308
  388.1 13.4 %copy-start.47 = (f32[1152]{0:T(1024)S(1)}, f32[1152]{0:T(1024)}, u32[]{:S(2)}) copy-start(f32[1152]{0:T(1024)} %copy-done.46) | copy-start | bytes 13828
  389.4 14.3 %copy-start.7 = (f32[8,128,128]{1,2,0:T(8,128)S(1)}, f32[8,128,128]{1,2,0:T(8,128)}, u32[]{:S(2)}) copy-start(f32[8,128,128]{1,2,0:T(8,128)} %copy-done.6) | copy-start | bytes 1572868
  389.4 12.0 %all-to-all-start.3 = ((bf16[16,8,1152]{2,1,0:T(8,128)(2,1)}), bf16[16,8,1152]{2,1,0:T(8,128)(2,1)S(1)}, u32[]{:S(2)}, u32[]{:S(2)}) async-start(bf16[16,8,1152]{2,1,0:T(8,128)(2,1)} %fusion.98), calls=%async_computation.3 | async-start | bytes 589824 | tf_op jit(solution)/shard_map/all_to_all | solution.py:127
  394.0 288.1 %all-reduce.13.cloned.1.call-start = ((), (), s32[]{:S(2)}) async-start(), calls=%async_computation.6 | async-start | bytes 3014656 | tf_op jit(solution)/shard_map/psum | solution.py:129
  396.9 7.6 %copy-start.37 = (f32[128,8]{0,1:T(8,128)S(1)}, f32[128,8]{0,1:T(8,128)}, u32[]{:S(2)}) copy-start(f32[128,8]{0,1:T(8,128)} %copy-done.36) | copy-start | bytes 12292
  405.0 2.2 copy-start.3
  405.1 2.9 copy-start.43
  405.1 2.9 copy-start.45
  405.1 2.9 copy-start.59
  405.1 2.9 copy-start.61
  (22 other events, 18.2 us)
Sparse Core Ops, SparseCore 0:
  11.2 92.5 all-gather.4
  106.9 136.5 all-gather.2
  409.3 272.8 all-reduce.12
where the time goes:
time: 695 us; the launch traced here: 693 us
  waiting for transfers between devices  504 us (73%)
  local copies, waits for them, and re-layouts  80.9 us (12%)
  matrix products  42.2 us (6%)
  other arithmetic  22.5 us (3%)
  starting transfers between devices  15.8 us (2%)
  between operations  14.8 us (2%)
  blocking collectives  12.9 us (2%)
    psum x1, waiting for transfers between devices, on_device(): lax.psum((down_early, up_early, down_late, up_late), ('dp', 'seq'))  273 us
    all_gather x1, waiting for transfers between devices, on_device(): lax.all_gather(query_key_value_weight, 'dp', axis=1, tiled=True)  131 us
    all_gather x1, waiting for transfers between devices, on_device(): lax.all_gather(output_projection_weight, 'dp', axis=1, tiled=True)  86.5 us
    unnamed x135, local copies, waits for them, and re-layouts  41.8 us
    slice x2, local copies, waits for them, and re-layouts, on_device(): qkv_second, out_second = (qkv_whole[1], out_whole[1])  25.5 us
  transfers between devices with their start and end apart: 6, of which 5 were waited for; matrix products, arithmetic and copies ran while one was open for 5% of the time, Pallas kernels for 0%

commit v1 on v0

v1 whole, which is shorter than its diff:
```python
import math

import jax
import jax.numpy as jnp
import numpy as np
from jax import lax
from jax.experimental import pallas as pl
from jax.experimental.pallas import tpu as pltpu
from jax.sharding import Mesh, PartitionSpec as P

WIDTH = 1152
HEADS = 8
HEAD = 72
RANK = 64
FEATURES = HEADS * HEAD
ROWS = 128
F32 = jnp.float32
BF16 = jnp.bfloat16
SCALE = 1.0 / math.sqrt(HEAD)
MIB = 1 << 20
DP = ("z", "h")
SEQ = ("x", "l", "c")


def call(kernel, out_shape, scratch=(), in_specs=None, limit=48):
    vmem = pl.BlockSpec(memory_space=pltpu.VMEM)

    def run(*operands):
        return pl.pallas_call(
            kernel,
            out_shape=out_shape,
            in_specs=in_specs or [vmem] * len(operands),
            out_specs=jax.tree.map(lambda _: vmem, out_shape),
            scratch_shapes=list(scratch),
            compiler_params=pltpu.CompilerParams(vmem_limit_bytes=limit * MIB),
        )(*operands)

    return run


def spec(space):
    return pl.BlockSpec(memory_space=space)


def dot(a, b, dims=((1,), (0,))):
    return lax.dot_general(a, b, (dims, ((), ())), preferred_element_type=F32)


NT = ((1,), (1,))
TN = ((0,), (0,))


def halves(values):
    high = values.astype(BF16)
    return high, (values - high.astype(F32)).astype(BF16)


def normalise(values):
    centred = values - jnp.mean(values, -1, keepdims=True)
    rate = lax.rsqrt(jnp.mean(centred * centred, -1, keepdims=True) + 1e-06)
    return centred * rate, rate


def lane_mask(width, dtype=F32):
    lanes = lax.broadcasted_iota(jnp.int32, (1, 128), 1)
    return (lanes < width).astype(dtype)


def split_heads(projected):
    keep = lane_mask(HEAD)
    q = projected[:, :128] * keep
    k = pltpu.roll(projected, 256 - HEAD, 1)[:, :128] * keep
    v = pltpu.roll(projected, 256 - 2 * HEAD, 1)[:, :128] * keep
    return q, k, v


def join_heads(q, k, v):
    zero = jnp.zeros_like(q)
    return (
        jnp.concatenate([q, zero], 1)
        + pltpu.roll(jnp.concatenate([k, zero], 1), HEAD, 1)
        + pltpu.roll(jnp.concatenate([v, zero], 1), 2 * HEAD, 1)
    )


def head_rate(values):
    return lax.rsqrt(jnp.sum(values * values, -1, keepdims=True) * (1.0 / HEAD) + 1e-06)


def head_norm_back(values, cotangent):
    rate = head_rate(values)
    inner = jnp.sum(cotangent * values, -1, keepdims=True) * (1.0 / HEAD)
    return rate * (cotangent - values * (rate * rate * inner))


def swap(values):
    lanes = lax.broadcasted_iota(jnp.int32, (1, 128), 1)
    return jnp.where(
        lanes < HEAD // 2,
        pltpu.roll(values, 128 - HEAD // 2, 1),
        pltpu.roll(values, HEAD // 2, 1),
    )


def softmax(scores, mask):
    weights = jnp.exp(scores * SCALE)
    if mask is not None:
        weights = weights * mask
    return weights / jnp.sum(weights, -1, keepdims=True)


def attention_back(weights, q, k, v, cotangent):
    rounded = weights.astype(BF16)
    d_v = dot(rounded, cotangent, TN).astype(BF16)
    d_weights = dot(cotangent, v, NT).astype(BF16).astype(F32)
    d_scores = weights * (d_weights - jnp.sum(d_weights * weights, -1, keepdims=True))
    d_scores = (d_scores * SCALE).astype(BF16)
    d_q = dot(d_scores, k).astype(BF16)
    d_k = dot(d_scores, q, TN).astype(BF16)
    return d_q.astype(F32), d_k.astype(F32), d_v.astype(F32)


def same_token():
    rows = lax.broadcasted_iota(jnp.int32, (ROWS, ROWS), 0)
    columns = lax.broadcasted_iota(jnp.int32, (ROWS, ROWS), 1)
    return ((rows & 7) == (columns & 7)).astype(F32)


def rotation_tables():
    row = np.arange(ROWS)
    frame = ((row // 16) % 4) * 4 + (row // 64) * 2 + (row // 8) % 2
    half = HEAD // 2
    frequency = np.exp(np.arange(half) * (-2.0 * math.log(10000.0) / HEAD))
    angle = frame[:, None] * frequency[None, :]
    cosine = np.zeros((ROWS, 128), np.float32)
    sine = np.zeros((ROWS, 128), np.float32)
    cosine[:, :half] = cosine[:, half:HEAD] = np.cos(angle)
    sine[:, :half] = -np.sin(angle)
    sine[:, half:HEAD] = np.sin(angle)
    return cosine, sine


def prologue_kernel(place, latents, modulation, qkv, out, modded, first_part, rest_part, rest):
    normed, _ = normalise(latents[...].astype(F32))
    modded[...] = (normed * (1.0 + modulation[0, 1:2]) + modulation[0, 0:1]).astype(BF16)
    rest[...] = jnp.zeros_like(rest)
    for head in range(HEADS):

        @pl.when(place[0] == head)
        def _():
            for part in range(3):
                columns = slice(part * FEATURES + head * HEAD, part * FEATURES + head * HEAD + HEAD)
                rest[0, :, part * HEAD : part * HEAD + HEAD] = qkv[0, :, columns].astype(F32)
                rest[1, :, part * HEAD : part * HEAD + HEAD] = qkv[1, :, columns].astype(F32)
            for block in range(2):
                rows = slice(18 * block, 18 * block + 18)
                rest[1, rows, 216:232] = out[block, :, 1024 + 16 * head : 1040 + 16 * head].astype(F32)
                rest[1, rows, 256:384] = out[block, :, 128 * head : 128 * head + 128].astype(F32)

    first = rest[0, :, :256].astype(BF16)
    tiles = jnp.concatenate([rest[1, :, 128 * t : 128 * t + 128] for t in range(3)], 0)
    lower, upper = tiles[:54].astype(BF16), tiles[54:].astype(BF16)
    mine = jnp.where(place[1] == 0, lower, upper)
    for copy in range(32):
        first_part[copy] = first
        rest_part[copy] = mine


def prologue(place, latents, modulation, qkv, out):
    smem, vmem = spec(pltpu.SMEM), spec(pltpu.VMEM)
    return call(
        prologue_kernel,
        (
            jax.ShapeDtypeStruct((ROWS, WIDTH), BF16),
            jax.ShapeDtypeStruct((32, 36, 256), BF16),
            jax.ShapeDtypeStruct((32, 54, 128), BF16),
        ),
        [pltpu.VMEM((2, 36, 384), F32)],
        [smem, vmem, vmem, vmem, vmem],
    )(place, latents, modulation, qkv, out)


def spatial_kernel(order, *refs):
    pieces = refs[:8]
    weight, down, up, attended, modded, projected, reduced, weights, merged, sems = refs[8:]
    copies = [
        pltpu.make_async_copy(piece, modded.at[order[i]], sems.at[i])
        for i, piece in enumerate(pieces)
    ]
    for copy in copies:
        copy.start()
    for chunk in range(32):
        merged[36 * chunk : 36 * chunk + 36, :256] = weight[chunk]
    merged[:, 256:] = down[...]
    for copy in copies:
        copy.wait()
    whole = dot(modded[...].reshape(8 * ROWS, WIDTH), merged[...])
    low = whole[:, 256:320] + whole[:, 320:384]
    high, rest = halves(low)
    reduced[...] = jnp.concatenate([high, rest], 1)
    projected[...] = whole[:, :256] + dot(jnp.concatenate([high, high, rest], 1), up[...])
    for pair in range(4):
        outs = []
        for frame in (2 * pair, 2 * pair + 1):
            q, k, v = split_heads(projected[frame * ROWS : frame * ROWS + ROWS])
            q = (q * head_rate(q)).astype(BF16)
            k = (k * head_rate(k)).astype(BF16)
            w = softmax(dot(q, k, NT), None)
            weights[frame] = w
            outs.append(dot(w.astype(BF16), v.astype(BF16)).reshape(16, 8, 128))
        rows = jnp.stack(outs, 1).reshape(16, 16, 128).astype(BF16)
        attended[:, 16 * pair : 16 * pair + 16, :] = rows


def spatial(order, pieces, weight, down, up):
    vmem = spec(pltpu.VMEM)
    return call(
        spatial_kernel,
        (
            jax.ShapeDtypeStruct((16, 64, 128), BF16),
            jax.ShapeDtypeStruct((8, ROWS, WIDTH), BF16),
            jax.ShapeDtypeStruct((8 * ROWS, 256), F32),
            jax.ShapeDtypeStruct((8 * ROWS, 128), BF16),
            jax.ShapeDtypeStruct((8, ROWS, ROWS), F32),
        ),
        [pltpu.VMEM((WIDTH, 384), BF16), pltpu.SemaphoreType.DMA((8,))],
        [spec(pltpu.SMEM)] + [spec(pl.ANY)] * 8 + [vmem] * 3,
    )(order, *pieces, weight, down, up)


def spatial_back_kernel(cotangent, modded, projected, reduced, weights, up, grad, d_projected):
    for pair in range(4):
        rows = cotangent[:, 16 * pair : 16 * pair + 16, :].astype(F32).reshape(16, 2, 8, 128)
        for side in range(2):
            frame = 2 * pair + side
            span = slice(frame * ROWS, frame * ROWS + ROWS)
            q, k, v = split_heads(projected[span])
            q_out = (q * head_rate(q)).astype(BF16)
            k_out = (k * head_rate(k)).astype(BF16)
            d_q, d_k, d_v = attention_back(
                weights[frame],
                q_out,
                k_out,
                v.astype(BF16),
                rows[:, side].reshape(ROWS, 128).astype(BF16),
            )
            d_projected[span] = join_heads(head_norm_back(q, d_q), head_norm_back(k, d_k), d_v)
    high, rest = halves(d_projected[...])
    both = dot(reduced[...], jnp.concatenate([high, rest], 1), TN)
    grad_up = both[:64, :256] + both[64:, :256] + both[:64, 256:] + both[64:, 256:]
    two = dot(high, up[:128], NT) + dot(rest, up[:128], NT)
    low_high, low_rest = halves(two[:, :64] + two[:, 64:])
    down = dot(
        jnp.concatenate([low_high, low_rest], 1), modded[...].reshape(8 * ROWS, WIDTH), TN
    )
    grad_down = down[:64] + down[64:]
    grad[:64, :640] = grad_down[:, :640]
    grad[:64, 640:] = grad_up[:, :128]
    grad[64:, :512] = grad_down[:, 640:]
    grad[64:, 512:640] = grad_up[:, 128:]
    grad[64:, 640:] = jnp.zeros((64, 128), F32)


def spatial_back(cotangent, modded, projected, reduced, weights, up):
    return call(
        spatial_back_kernel,
        jax.ShapeDtypeStruct((128, 768), F32),
        [pltpu.VMEM((8 * ROWS, 256), F32)],
    )(cotangent, modded, projected, reduced, weights, up)


def assemble_kernel(order, *refs):
    pieces = refs[:8]
    qkv, out_first, out_second, held, sems = refs[8:]
    copies = [
        pltpu.make_async_copy(piece, held.at[order[i]], sems.at[i])
        for i, piece in enumerate(pieces)
    ]
    for copy in copies:
        copy.start()
    for copy in copies:
        copy.wait()

    def step(head, _):
        for d in range(32):
            a, b = 36 * d, 18 * d
            qkv[head, a : a + 36, :128] = held[head, 0, d, 0:36]
            qkv[head, a : a + 18, 128:] = held[head, 0, d, 36:54]
            qkv[head, a + 18 : a + 36, 128:] = held[head, 1, d, 0:18]
        return 0

    lax.fori_loop(0, HEADS, step, 0)
    for head in range(HEADS):
        main = slice(128 * head, 128 * head + 128)
        tail = slice(1024 + 16 * head, 1040 + 16 * head)
        for d in range(32):
            rows = slice(18 * d, 18 * d + 18)
            out_first[rows, main] = held[head, 1, d, 18:36]
            out_second[rows, main] = held[head, 1, d, 36:54]
            out_first[rows, tail] = held[head, 0, d, 36:54, 88:104]
            out_second[rows, tail] = held[head, 1, d, 0:18, 88:104]


def assemble(order, pieces):
    return call(
        assemble_kernel,
        (
            jax.ShapeDtypeStruct((HEADS, WIDTH, 256), BF16),
            jax.ShapeDtypeStruct((FEATURES, WIDTH), BF16),
            jax.ShapeDtypeStruct((FEATURES, WIDTH), BF16),
        ),
        [pltpu.VMEM((8, 2, 32, 54, 128), BF16), pltpu.SemaphoreType.DMA((8,))],
        [spec(pltpu.SMEM)] + [spec(pl.ANY)] * 8,
    )(order, *pieces)


def by_rows(values):
    values = values.astype(F32)
    frames = [x * 4 + l * 2 + c for l in range(2) for x in range(4) for c in range(2)]
    return jnp.concatenate([values[f] for f in frames], 0)


def temporal_kernel(
    received,
    latents,
    targets,
    modulation,
    qkv,
    out_first,
    out_second,
    down,
    up,
    cosine,
    sine,
    sent,
    modded,
    reduced,
    d_projected,
    d_reduced,
    wide,
    projected,
    weights,
    q_all,
    k_all,
    v_all,
):
    for head in range(HEADS):
        x, c = head // 2, head % 2
        rows = jnp.concatenate([received[x * 4 + c], received[x * 4 + 2 + c]], 0).astype(F32)
        wide[:, HEAD * head : HEAD * head + HEAD] = rows[:, :HEAD]
    gate_first, gate_second = modulation[0, 2:3], modulation[1, 2:3]
    mixed = dot(wide[...].astype(BF16), out_first[...])
    middle = (by_rows(latents[...]) + gate_first * mixed).astype(BF16).astype(F32)
    normed, rate = normalise(middle)
    scale = 1.0 + modulation[1, 1:2]
    modded[...] = (normed * scale + modulation[1, 0:1]).astype(BF16)
    low = dot(modded[...], down[...])
    high, rest = halves(low[:, :64] + low[:, 64:])
    reduced[...] = jnp.concatenate([high, rest], 1)
    three = jnp.concatenate([high, high, rest], 1)
    mask = same_token()
    for head in range(HEADS):
        both = dot(modded[...], qkv[head]) + dot(three, up[head])
        projected[head] = both
        q, k, v = split_heads(both)
        q = q * head_rate(q)
        k = k * head_rate(k)
        q = (q * cosine[...] + swap(q) * sine[...]).astype(BF16)
        k = (k * cosine[...] + swap(k) * sine[...]).astype(BF16)
        v = v.astype(BF16)
        w = softmax(dot(q, k, NT), mask)
        q_all[head], k_all[head], v_all[head], weights[head] = q, k, v, w
        wide[:, HEAD * head : HEAD * head + HEAD] = dot(w.astype(BF16), v)[:, :HEAD]
    mixed = dot(wide[...].astype(BF16), out_second[...])
    produced = (middle + gate_second * mixed).astype(BF16).astype(F32)
    error = ((produced - by_rows(targets[...])) / WIDTH).astype(BF16).astype(F32)
    wide[...] = dot((gate_second * error).astype(BF16), out_second[...], NT)
    d_low = jnp.zeros((ROWS, 128), F32)
    d_modded = jnp.zeros((ROWS, WIDTH), F32)
    for head in range(HEADS):
        cotangent = wide[:, HEAD * head : HEAD * head + HEAD].astype(BF16)
        cotangent = jnp.concatenate([cotangent, jnp.zeros((ROWS, 128 - HEAD), BF16)], 1)
        d_q, d_k, d_v = attention_back(
            weights[head], q_all[head], k_all[head], v_all[head], cotangent
        )
        d_q = d_q * cosine[...] - swap(d_q) * sine[...]
        d_k = d_k * cosine[...] - swap(d_k) * sine[...]
        q, k, _ = split_heads(projected[head])
        joined = join_heads(head_norm_back(q, d_q), head_norm_back(k, d_k), d_v)
        d_projected[head] = joined
        high, rest = halves(joined)
        d_low += dot(high, up[head, :128], NT) + dot(rest, up[head, :128], NT)
        d_modded += dot(high, qkv[head], NT)
    d_low = d_low[:, :64] + d_low[:, 64:]
    high, rest = halves(d_low)
    d_reduced[...] = jnp.concatenate([high, rest], 1)
    through = dot(jnp.concatenate([high, high], 1), down[...], NT) + dot(
        rest, down[:, :64], NT
    )
    d_modded = (d_modded.astype(BF16) + through.astype(BF16)).astype(F32)
    d_normed = d_modded * scale
    inner = jnp.mean(d_normed * normed, -1, keepdims=True)
    d_middle = rate * (d_normed - jnp.mean(d_normed, -1, keepdims=True) - normed * inner)
    d_middle = (error.astype(BF16) + d_middle.astype(BF16)).astype(F32)
    wide[...] = dot((gate_first * d_middle).astype(BF16), out_first[...], NT)
    for head in range(HEADS):
        x, c = head // 2, head % 2
        rows = wide[:, HEAD * head : HEAD * head + HEAD].astype(BF16)
        rows = jnp.concatenate([rows, jnp.zeros((ROWS, 128 - HEAD), BF16)], 1)
        sent[x * 4 + c] = rows[:64]
        sent[x * 4 + 2 + c] = rows[64:]


def temporal(*operands):
    return call(
        temporal_kernel,
        (
            jax.ShapeDtypeStruct((16, 64, 128), BF16),
            jax.ShapeDtypeStruct((ROWS, WIDTH), BF16),
            jax.ShapeDtypeStruct((ROWS, 128), BF16),
            jax.ShapeDtypeStruct((HEADS, ROWS, 256), F32),
            jax.ShapeDtypeStruct((ROWS, 128), BF16),
        ),
        [
            pltpu.VMEM((ROWS, FEATURES), F32),
            pltpu.VMEM((HEADS, ROWS, 256), F32),
            pltpu.VMEM((HEADS, ROWS, ROWS), F32),
            pltpu.VMEM((HEADS, ROWS, 128), BF16),
            pltpu.VMEM((HEADS, ROWS, 128), BF16),
            pltpu.VMEM((HEADS, ROWS, 128), BF16),
        ],
    )(*operands)


def temporal_grad_kernel(modded, reduced, d_projected, d_reduced, grad, ups):
    for head in range(HEADS):
        high, rest = halves(d_projected[head])
        both = dot(reduced[...], jnp.concatenate([high, rest], 1), TN)
        part = both[:64, :256] + both[64:, :256] + both[:64, 256:] + both[64:, 256:]
        for k in range(3):
            start = k * FEATURES + head * HEAD
            ups[:, start : start + HEAD] = part[:, k * HEAD : k * HEAD + HEAD]
    down = dot(d_reduced[...], modded[...], TN)
    grad[:64, :WIDTH] = down[:64] + down[64:]
    grad[:64, WIDTH:] = ups[:, :384]
    grad[64:, :1280] = ups[:, 384:1664]
    grad[64:, 1280:1408] = jnp.concatenate([ups[:, 1664:], jnp.zeros((64, 64), F32)], 1)
    grad[64:, 1408:] = jnp.zeros((64, 128), F32)


def temporal_grad(*operands):
    return call(
        temporal_grad_kernel,
        jax.ShapeDtypeStruct((128, 1536), F32),
        [pltpu.VMEM((64, 3 * FEATURES), F32)],
    )(*operands)


def epilogue_kernel(spatial_sum, temporal_sum, grad_down, grad_up):
    first = spatial_sum[...].reshape(128, 1664)
    second = temporal_sum[...].reshape(128, 1536)
    down = jnp.concatenate([first[:64, :640], first[64:, :512]], 1)
    grad_down[0] = down.T
    grad_down[1] = second[:64, :WIDTH].T
    for head in range(HEADS):
        top = first[:64, 640 + 128 * head : 768 + 128 * head]
        bottom = first[64:, 640 + 128 * head : 768 + 128 * head]
        both = jnp.concatenate([top, bottom], 1)
        for k in range(3):
            start = k * FEATURES + head * HEAD
            grad_up[0, :, start : start + HEAD] = both[:, k * HEAD : k * HEAD + HEAD]
    grad_up[1, :, :384] = second[:64, WIDTH:]
    grad_up[1, :, 384:] = second[64:, :1344]


def epilogue(spatial_sum, temporal_sum):
    return call(
        epilogue_kernel,
        (
            jax.ShapeDtypeStruct((2, WIDTH, RANK), F32),
            jax.ShapeDtypeStruct((2, RANK, 3 * FEATURES), F32),
        ),
    )(spatial_sum, temporal_sum)


def exchange(values, axes):
    return lax.all_to_all(values, axes, 0, 0)


def spread(values, axes, count):
    return exchange(jnp.broadcast_to(values[None], (count,) + values.shape), axes)


def shift(values, axis, count, by):
    return lax.ppermute(values, axis, [(i, (i + by) % count) for i in range(count)])


def two_parts(values):
    high = lax.reduce_precision(values, 8, 7)
    return high.astype(BF16), (values - high).astype(BF16)


def on_device(latents, targets, modulation, qkv, out, down, up):
    x, l, c = lax.axis_index("x"), lax.axis_index("l"), lax.axis_index("c")
    place = jnp.stack([x * 2 + c, l]).astype(jnp.int32)
    order = jnp.stack(
        [((x - dx) % 4) * 2 + (c ^ dc) for dc in range(2) for dx in range(4)]
    ).astype(jnp.int32)
    modulation = modulation[0]
    modded, first_part, rest_part = prologue(place, latents[0, 0], modulation, qkv, out)

    def around(values):
        along = [values] + [shift(values, "x", 4, by) for by in (1, 2, 3)]
        return along + [shift(v, "c", 2, 1) for v in along]

    pieces = around(modded)
    rest = exchange(rest_part, DP)
    first = exchange(first_part, DP)

    down_high, down_low = two_parts(down)
    down_parts = jnp.concatenate([down_high, down_low], 2)
    by_head = up.reshape(2, RANK, 3, HEADS, HEAD).transpose(0, 3, 1, 2, 4)
    by_head = jnp.pad(by_head.reshape(2, HEADS, RANK, 3 * HEAD), ((0, 0), (0, 0), (0, 0), (0, 40)))
    up_high, up_low = two_parts(by_head)
    up_parts = jnp.concatenate([up_high, up_low, up_high], 2)
    up_mine = lax.dynamic_index_in_dim(up_parts[0], place[0], 0, keepdims=False)

    other = shift(rest, "l", 2, 1)
    rest = jnp.stack([jnp.where(l == 0, rest, other), jnp.where(l == 0, other, rest)])
    qkv_second, out_first, out_second = assemble(order, around(rest))

    both = jnp.stack([latents[0, 0].reshape(16, 8, WIDTH), targets[0, 0].reshape(16, 8, WIDTH)], 1)
    both = exchange(both, SEQ)

    attended, modded_all, projected, reduced, weights = spatial(
        order, pieces, first, down_parts[0], up_mine
    )
    received = exchange(attended, SEQ)
    cosine, sine = rotation_tables()
    sent, modded_rows, low, d_projected, d_low = temporal(
        received,
        both[:, 0],
        both[:, 1],
        modulation,
        qkv_second,
        out_first,
        out_second,
        down_parts[1],
        up_parts[1],
        jnp.asarray(cosine),
        jnp.asarray(sine),
    )
    cotangent = exchange(sent, SEQ)
    late = temporal_grad(modded_rows, low, d_projected, d_low).reshape(16, 8, 1536)
    late = jnp.sum(exchange(late, SEQ), 0)
    early = spatial_back(cotangent, modded_all, projected, reduced, weights, up_mine)
    early = exchange(early.reshape(16, 8, 768), SEQ)
    early_down = jnp.sum(early[:, :, :640], 0)
    early_up = jnp.sum(early[:, :, 640:].reshape(4, 2, 2, 8, 128), 1)
    early_up = early_up.reshape(8, 8, 128).transpose(1, 0, 2).reshape(8, 1024)
    bottom_up = jnp.sum(early[:, :, 512:640].reshape(4, 2, 2, 8, 128), 1)
    bottom_up = bottom_up.reshape(8, 8, 128).transpose(1, 0, 2).reshape(8, 1024)
    bottom = place[0] * 0 + (x >= 2).astype(jnp.int32)
    early_up = jnp.where(bottom == 1, bottom_up, early_up)
    total = jnp.concatenate([early_down, early_up, late], 1)
    total = jnp.sum(spread(total, ("z",), 8), 0)
    total = jnp.sum(spread(total, ("h",), 4), 0)
    total = spread(total, SEQ, 16)
    return epilogue(total[:, :, :1664], total[:, :, 1664:])


def solution(mesh):
    inner = Mesh(mesh.devices.reshape(8, 4, 4, 2, 2), ("z", "h", "x", "l", "c"))
    in_specs = (
        P(DP, SEQ, None, None),
        P(DP, SEQ, None, None),
        P(DP, None, None, None),
        P(None, DP, None),
        P(None, DP, None),
        P(),
        P(),
    )
    return jax.shard_map(
        on_device, mesh=inner, in_specs=in_specs, out_specs=(P(), P()), check_vma=False
    )
```

time: 695 us -> 334 us (0.48)
  waiting for transfers between devices: 504 us -> 31.3 us
  blocking collectives: 12.9 us -> 122 us
  starting transfers between devices: 15.8 us -> 71.6 us
  Pallas kernels: 0 us -> 48.7 us
  matrix products: 42.2 us -> 0 us
  local copies, waits for them, and re-layouts: 80.9 us -> 46.4 us
  between operations: 14.8 us -> 1.23 us
  other arithmetic: 22.5 us -> 10.9 us
    psum x1 -> x0, waiting for transfers between devices: 273 us -> none  [on_device(): lax.psum((down_early, up_early, down_late, up_late), ('dp', 'seq'))]
    all_gather x2 -> x0, waiting for transfers between devices: 218 us -> none  [the longest x1 131 us: on_device(): lax.all_gather(query_key_value_weight, 'dp', axis=1, tiled=True)]
    all_to_all x1 -> x5, blocking collectives: 12.9 us -> 122 us  [exchange(): return lax.all_to_all(values, axes, 0, 0)]
    pallas_call x0 -> x7, Pallas kernels: none -> 48.7 us  [run(): pl.pallas_call(kernel, out_shape=out_shape, in_specs=in_specs or [vmem] *...]
    ppermute x0 -> x15, starting transfers between devices: none -> 44.6 us  [shift(): lax.ppermute(values, axis, [(i, (i + by) % count) for i in range(count)])]
    dot_general x30 -> x0, matrix products: 42.2 us -> none  [the longest x3 10.8 us: block(): jnp.dot(modded, query_key_value_weight, preferred_element_type=jnp.float32)]
    slice x4 -> x3, local copies, waits for them, and re-layouts: 27.9 us -> 0.14 us  [the longest x2 0.13 us: on_device(): return epilogue(total[:, :, :1664], total[:, :, 1664:])]
    unnamed x135 -> x66, local copies, waits for them, and re-layouts: 41.8 us -> 17.1 us
  transfers between devices with their start and end apart: 6 -> 20, of which waited for: 5 -> 4; matrix products, arithmetic and copies ran while one was open for 5% -> 12% of each run, Pallas kernels for 0% -> 5%
where the time goes in v1:
time: 334 us; the launch traced here: 332 us
  blocking collectives  122 us (37%)
  starting transfers between devices  71.6 us (21%)
  Pallas kernels  48.7 us (15%)
  local copies, waits for them, and re-layouts  46.4 us (14%)
  waiting for transfers between devices  31.3 us (9%)
  other arithmetic  10.9 us (3%)
    all_to_all x5, blocking collectives, exchange(): return lax.all_to_all(values, axes, 0, 0)  122 us
    pallas_call x7, Pallas kernels, run(): pl.pallas_call(kernel, out_shape=out_shape, in_specs=in_specs or [vmem] *...  48.7 us
    ppermute x15, starting transfers between devices, shift(): lax.ppermute(values, axis, [(i, (i + by) % count) for i in range(count)])  44.6 us
    all_to_all x5, starting transfers between devices, exchange(): return lax.all_to_all(values, axes, 0, 0)  27.1 us
    all_to_all x5, waiting for transfers between devices, exchange(): return lax.all_to_all(values, axes, 0, 0)  18.4 us
    unnamed x66, local copies, waits for them, and re-layouts  17.1 us
    ppermute x15, waiting for transfers between devices, shift(): lax.ppermute(values, axis, [(i, (i + by) % count) for i in range(count)])  13 us
    ppermute x7, local copies, waits for them, and re-layouts, shift(): lax.ppermute(values, axis, [(i, (i + by) % count) for i in range(count)])  12.5 us
  transfers between devices with their start and end apart: 20, of which 4 were waited for; matrix products, arithmetic and copies ran while one was open for 12% of the time, Pallas kernels for 5%

profile of v1, /device:TPU:1, one launch (start us, length us, event | category | flops | bytes accessed | tf_op | source)
XLA Modules:
  0.0 332.1 jit_solution(7882228946257200162)
XLA Ops:
  4.4 1.9 shard_map.104
  6.2 33.2 %all_to_all.50 = bf16[32,54,128]{2,1,0:T(8,128)(2,1)} all-to-all(bf16[32,54,128]{2,1,0:T(8,128)(2,1)S(1)} %get-tuple-element.21), channel_id=1, replica_groups=mesh['z'=8,'h'=4,'x'=4,'l'=2,'c'=2] {'z','h'}, dimensions={0} | all-to-all | bytes 884736 | tf_op jit(solution)/shard_map/all_to_all | solution.py:487
  39.4 6.4 %all-to-all-start = ((bf16[32,36,256]{2,1,0:T(8,128)(2,1)}), bf16[32,36,256]{2,1,0:T(8,128)(2,1)S(1)}, u32[]{:S(2)}, u32[]{:S(2)}) async-start(bf16[32,36,256]{2,1,0:T(8,128)(2,1)} %get-tuple-element.19), calls=%async_computation | async-start | bytes 1310720 | tf_op jit(solution)/shard_map/all_to_all | solution.py:487
  45.9 2.1 collective-permute-start.7
  47.9 3.1 collective-permute-start
  51.0 4.4 %collective-permute-start.1 = (bf16[128,1152]{1,0:T(8,128)(2,1)S(1)}, bf16[128,1152]{1,0:T(8,128)(2,1)S(1)}, u32[]{:S(2)}, u32[]{:S(2)}) collective-permute-start(bf16[128,1152]{1,0:T(8,128)(2,1)S(1)} %get-tuple-element.18.refs_0_), channel_id=1, source_target_pairs={{0,8},{4,12},{8,0},{12,4},{1,9},{5,13},{9,1},{13,5},{2,10},{6,14},... | collective-permute-start | bytes 884744 | tf_op jit(solution)/shard_map/ppermute | solution.py:495
  55.4 3.1 collective-permute-start.2
  58.5 4.2 %collective-permute-start.3 = (bf16[128,1152]{1,0:T(8,128)(2,1)S(1)}, bf16[128,1152]{1,0:T(8,128)(2,1)S(1)}, u32[]{:S(2)}, u32[]{:S(2)}) collective-permute-start(bf16[128,1152]{1,0:T(8,128)(2,1)S(1)} %get-tuple-element.18.refs_0_), channel_id=1, source_target_pairs={{0,1},{1,0},{2,3},{3,2},{4,5},{5,4},{6,7},{7,6},{8,9},{9,8},{10,11... | collective-permute-start | bytes 884744 | tf_op jit(solution)/shard_map/ppermute | solution.py:495
  63.8 2.5 copy.69
  67.8 1.8 pad_maximum_fusion.2
  69.6 1.9 collective-permute-start.4
  73.9 2.2 collective-permute-start.8
  76.2 6.4 %all-to-all-start.2 = ((bf16[16,2,8,1152]{3,2,1,0:T(8,128)(2,1)}), bf16[16,2,8,1152]{3,2,1,0:T(8,128)(2,1)}, u32[]{:S(2)}, u32[]{:S(2)}) async-start(bf16[16,2,8,1152]{3,2,1,0:T(8,128)(2,1)} %pad_maximum_fusion.2), calls=%async_computation.2 | async-start | bytes 1179648 | tf_op jit(solution)/shard_map/all_to_all | solution.py:487
  82.6 4.8 %collective-permute-start.9 = (bf16[2,32,54,128]{3,1,2,0:T(8,128)(2,1)}, bf16[2,32,54,128]{3,1,2,0:T(8,128)(2,1)}, u32[]{:S(2)}, u32[]{:S(2)}) collective-permute-start(bf16[2,32,54,128]{3,1,2,0:T(8,128)(2,1)} %copy.74), channel_id=1, source_target_pairs={{0,8},{4,12},{8,0},{12,4},{1,9},{5,13},{9,1},{13,5},{2,10},{6,14},... | collective-permute-start | bytes 2654216 | tf_op jit(solution)/shard_map/ppermute | solution.py:495
  87.4 2.8 collective-permute-start.10
  90.2 3.2 subtract_convert_fusion
  93.4 3.0 reshape.35
  96.4 3.3 copy.90
  99.7 3.5 %reshape.36 = f32[2,8,64,216]{3,2,1,0:T(8,128)} reshape(f32[2,8,64,3,72]{4,3,2,1,0:T(4,128)} %bitcast.52) | data formatting | bytes 1769472 | tf_op jit(solution)/shard_map/reshape | solution.py:523
  104.7 2.8 collective-permute-start.5
  107.7 1.9 collective-permute-start.11
  109.6 2.4 collective-permute-start.12
  112.1 10.0 %collective-permute-done.9 = bf16[2,32,54,128]{3,1,2,0:T(8,128)(2,1)} collective-permute-done((bf16[2,32,54,128]{3,1,2,0:T(8,128)(2,1)}, bf16[2,32,54,128]{3,1,2,0:T(8,128)(2,1)}, u32[]{:S(2)}, u32[]{:S(2)}) %collective-permute-start.9) | collective-permute-done | bytes 884768 | tf_op jit(solution)/shard_map/ppermute | solution.py:495
  122.1 4.2 %collective-permute-start.13 = (bf16[2,32,54,128]{3,1,2,0:T(8,128)(2,1)}, bf16[2,32,54,128]{3,1,2,0:T(8,128)(2,1)}, u32[]{:S(2)}, u32[]{:S(2)}) collective-permute-start(bf16[2,32,54,128]{3,1,2,0:T(8,128)(2,1)} %collective-permute-done.9), channel_id=1, source_target_pairs={{0,1},{1,0},{2,3},{3,2},{4,5},{5,4},{6,7},{7,6},{8,9},{9,8},{10,11... | collective-permute-start | bytes 2654216 | tf_op jit(solution)/shard_map/ppermute | solution.py:495
  126.4 2.9 collective-permute-done.10
  129.2 2.8 collective-permute-start.14
  133.0 1.9 collective-permute-start.6
  136.0 1.6 fusion.3
  140.5 8.3 %shard_map.105 = (bf16[16,64,128]{2,1,0:T(8,128)(2,1)S(1)}, bf16[8,128,1152]{2,1,0:T(8,128)(2,1)}, f32[1024,256]{1,0:T(8,128)S(1)}, bf16[1024,128]{1,0:T(8,128)(2,1)S(1)}, f32[8,128,128]{2,1,0:T(8,128)S(1)}) custom-call(s32[8]{0:T(128)S(1)} %stack.56.order, bf16[128,1152]{1,0:T(8,128)(2,1)S(1)} %copy-done.13, bf16[128,1152]{1,0:T(8,128)(2,1)S(1)} %copy-done.15, ...), custom_call_target="tpu_custom_call" | custom-call | tf_op jit(solution)/shard_map/pallas_call | solution.py:29
  151.2 5.4 %all-to-all-start.1 = ((bf16[16,64,128]{2,1,0:T(8,128)(2,1)}), bf16[16,64,128]{2,1,0:T(8,128)(2,1)S(1)}, u32[]{:S(2)}, u32[]{:S(2)}) async-start(bf16[16,64,128]{2,1,0:T(8,128)(2,1)} %copy-done.24), calls=%async_computation.1 | async-start | bytes 524288 | tf_op jit(solution)/shard_map/all_to_all | solution.py:487
  157.6 1.5 copy.78.refs_1_
  162.2 1.5 copy.81.refs_4_
  163.7 1.5 copy.82.refs_5_
  165.3 2.4 copy.83.refs_6_
  167.7 2.4 copy.84.refs_7_
  170.2 8.3 %shard_map.106 = (bf16[8,1152,256]{2,1,0:T(8,128)(2,1)}, bf16[576,1152]{1,0:T(8,128)(2,1)}, bf16[576,1152]{1,0:T(8,128)(2,1)}) custom-call(s32[8]{0:T(128)S(1)} %stack.56.order, bf16[2,32,54,128]{3,2,1,0:T(8,128)(2,1)S(1)} %pad_maximum_fusion.1.refs_0_, bf16[2,32,54,128]{3,2,1,0:T(8,128)(2,1)S(1)} %copy.78.refs_1_, ...), custom_call_target="tpu_custom_call" | custom-call | tf_op jit(solution)/shard_map/pallas_call | solution.py:29
  181.5 21.0 %shard_map.107 = (bf16[16,64,128]{2,1,0:T(8,128)(2,1)S(1)}, bf16[128,1152]{1,0:T(8,128)(2,1)S(1)}, bf16[128,128]{1,0:T(8,128)(2,1)S(1)}, f32[8,128,256]{2,1,0:T(8,128)S(1)}, bf16[128,128]{1,0:T(8,128)(2,1)S(1)}) custom-call(bf16[16,64,128]{2,1,0:T(8,128)(2,1)S(1)} %all-to-all-done.1.received, bf16[16,8,1152]{2,1,0:T(8,128)(2,1)S(1)} %get-tuple-element.55.latents, ...), custom_call_target="tpu_custom_call" | custom-call | tf_op jit(solution)/shard_map/pallas_call | solution.py:29
  203.6 12.7 %all_to_all.51.cotangent = bf16[16,64,128]{2,1,0:T(8,128)(2,1)S(1)} all-to-all(bf16[16,64,128]{2,1,0:T(8,128)(2,1)S(1)} %get-tuple-element.25), channel_id=1, replica_groups=mesh['z'=8,'h'=4,'x'=4,'l'=2,'c'=2] {'x','l','c'}, dimensions={0} | all-to-all | bytes 524288 | tf_op jit(solution)/shard_map/all_to_all | solution.py:487
  216.3 6.2 %shard_map.108 = f32[128,768]{1,0:T(8,128)} custom-call(bf16[16,64,128]{2,1,0:T(8,128)(2,1)S(1)} %all_to_all.51.cotangent, bf16[8,128,1152]{2,1,0:T(8,128)(2,1)S(1)} %copy-done, f32[1024,256]{1,0:T(8,128)S(1)} %copy-done.5, bf16[1024,128]{1,0:T(8,128)(2,1)S(1)} %copy-done.23, f32[8,128,128]{2,1,0:T(8,128)S(1)} %get-tuple-element.29.weights, ...), custom_call_target="tpu_custom_call" | custom-call | tf_op jit(solution)/shard_map/pallas_call | solution.py:29
  222.5 4.3 %all-to-all-start.5 = ((f32[16,8,768]{2,1,0:T(8,128)}), f32[16,8,768]{2,1,0:T(8,128)S(1)}, u32[]{:S(2)}, u32[]{:S(2)}) async-start(f32[16,8,768]{2,1,0:T(8,128)} %bitcast.23), calls=%async_computation.5 | async-start | bytes 786432 | tf_op jit(solution)/shard_map/all_to_all | solution.py:487
  228.4 1.6 shard_map.109
  229.9 5.4 %all-to-all-done.5 = f32[16,8,768]{2,1,0:T(8,128)S(1)} async-done(((f32[16,8,768]{2,1,0:T(8,128)}), f32[16,8,768]{2,1,0:T(8,128)S(1)}, u32[]{:S(2)}, u32[]{:S(2)}) %all-to-all-start.5) | async-done | bytes 393248 | tf_op jit(solution)/shard_map/all_to_all | solution.py:487
  235.3 4.6 %all-to-all-start.6 = ((f32[16,8,1536]{2,1,0:T(8,128)}), f32[16,8,1536]{2,1,0:T(8,128)S(1)}, u32[]{:S(2)}, u32[]{:S(2)}) async-start(f32[16,8,1536]{2,1,0:T(8,128)} %bitcast.29), calls=%async_computation.6 | async-start | bytes 1572864 | tf_op jit(solution)/shard_map/all_to_all | solution.py:487
  240.0 13.0 %all-to-all-done.6 = f32[16,8,1536]{2,1,0:T(8,128)S(1)} async-done(((f32[16,8,1536]{2,1,0:T(8,128)}), f32[16,8,1536]{2,1,0:T(8,128)S(1)}, u32[]{:S(2)}, u32[]{:S(2)}) %all-to-all-start.6) | async-done | bytes 786464 | tf_op jit(solution)/shard_map/all_to_all | solution.py:487
  253.1 28.2 %all_to_all.52 = f32[8,8,3200]{2,1,0:T(8,128)S(1)} all-to-all(f32[8,8,3200]{2,1,0:T(8,128)S(1)} %broadcast_in_dim.6), channel_id=1, replica_groups=mesh['z'=8,'h'=4,'x'=4,'l'=2,'c'=2] {'z'}, dimensions={0} | all-to-all | bytes 1638400 | tf_op jit(solution)/shard_map/all_to_all | solution.py:487
  281.3 16.8 %all_to_all.53 = f32[4,8,3200]{2,1,0:T(8,128)S(1)} all-to-all(f32[4,8,3200]{2,1,0:T(8,128)S(1)} %broadcast_in_dim.7), channel_id=1, replica_groups=mesh['z'=8,'h'=4,'x'=4,'l'=2,'c'=2] {'h'}, dimensions={0} | all-to-all | bytes 819200 | tf_op jit(solution)/shard_map/all_to_all | solution.py:487
  298.3 30.9 %all_to_all.54 = f32[16,8,3200]{2,1,0:T(8,128)S(1)} all-to-all(f32[16,8,3200]{2,1,0:T(8,128)S(1)} %broadcast_in_dim.8), channel_id=1, replica_groups=mesh['z'=8,'h'=4,'x'=4,'l'=2,'c'=2] {'x','l','c'}, dimensions={0} | all-to-all | bytes 3276800 | tf_op jit(solution)/shard_map/all_to_all | solution.py:487
  329.4 1.6 shard_map.110
  (110 shorter events, 28.9 us)
Async XLA Ops:
  1.4 38.0 %copy-start.8 = (f32[1,2,3,1152]{3,2,1,0:T(4,128)}, f32[1,2,3,1152]{3,2,1,0:T(4,128)S(1)}, u32[]{:S(2)}) copy-start(f32[1,2,3,1152]{3,2,1,0:T(4,128)S(1)} %copy.91) | copy-start | bytes 82948
  3.4 1.0 copy-start.2
  6.2 57.6 %copy-start.12 = (bf16[128,1152]{1,0:T(8,128)(2,1)}, bf16[128,1152]{1,0:T(8,128)(2,1)S(1)}, u32[]{:S(2)}) copy-start(bf16[128,1152]{1,0:T(8,128)(2,1)S(1)} %get-tuple-element.18.refs_0_) | copy-start | bytes 884740
  39.4 36.7 %all-to-all-start = ((bf16[32,36,256]{2,1,0:T(8,128)(2,1)}), bf16[32,36,256]{2,1,0:T(8,128)(2,1)S(1)}, u32[]{:S(2)}, u32[]{:S(2)}) async-start(bf16[32,36,256]{2,1,0:T(8,128)(2,1)} %get-tuple-element.19), calls=%async_computation | async-start | bytes 1310720 | tf_op jit(solution)/shard_map/all_to_all | solution.py:487
  45.9 25.7 %collective-permute-start.7 = (bf16[32,54,128]{2,1,0:T(8,128)(2,1)}, bf16[32,54,128]{2,1,0:T(8,128)(2,1)}, u32[]{:S(2)}, u32[]{:S(2)}) collective-permute-start(bf16[32,54,128]{2,1,0:T(8,128)(2,1)} %all_to_all.50), channel_id=1, source_target_pairs={{0,2},{2,0},{1,3},{3,1},{4,6},{6,4},{5,7},{7,5},{8,10},{10,8},{9,1... | collective-permute-start | bytes 1327112 | tf_op jit(solution)/shard_map/ppermute | solution.py:495
  47.9 21.7 %collective-permute-start = (bf16[128,1152]{1,0:T(8,128)(2,1)S(1)}, bf16[128,1152]{1,0:T(8,128)(2,1)S(1)}, u32[]{:S(2)}, u32[]{:S(2)}) collective-permute-start(bf16[128,1152]{1,0:T(8,128)(2,1)S(1)} %get-tuple-element.18.refs_0_), channel_id=1, source_target_pairs={{0,4},{4,8},{8,12},{12,0},{1,5},{5,9},{9,13},{13,1},{2,6},{6,10},{... | collective-permute-start | bytes 884744 | tf_op jit(solution)/shard_map/ppermute | solution.py:495
  51.0 31.5 %collective-permute-start.1 = (bf16[128,1152]{1,0:T(8,128)(2,1)S(1)}, bf16[128,1152]{1,0:T(8,128)(2,1)S(1)}, u32[]{:S(2)}, u32[]{:S(2)}) collective-permute-start(bf16[128,1152]{1,0:T(8,128)(2,1)S(1)} %get-tuple-element.18.refs_0_), channel_id=1, source_target_pairs={{0,8},{4,12},{8,0},{12,4},{1,9},{5,13},{9,1},{13,5},{2,10},{6,14},... | collective-permute-start | bytes 884744 | tf_op jit(solution)/shard_map/ppermute | solution.py:495
  55.4 31.9 %collective-permute-start.2 = (bf16[128,1152]{1,0:T(8,128)(2,1)S(1)}, bf16[128,1152]{1,0:T(8,128)(2,1)S(1)}, u32[]{:S(2)}, u32[]{:S(2)}) collective-permute-start(bf16[128,1152]{1,0:T(8,128)(2,1)S(1)} %get-tuple-element.18.refs_0_), channel_id=1, source_target_pairs={{0,12},{4,0},{8,4},{12,8},{1,13},{5,1},{9,5},{13,9},{2,14},{6,2},{... | collective-permute-start | bytes 884744 | tf_op jit(solution)/shard_map/ppermute | solution.py:495
  58.5 46.1 %collective-permute-start.3 = (bf16[128,1152]{1,0:T(8,128)(2,1)S(1)}, bf16[128,1152]{1,0:T(8,128)(2,1)S(1)}, u32[]{:S(2)}, u32[]{:S(2)}) collective-permute-start(bf16[128,1152]{1,0:T(8,128)(2,1)S(1)} %get-tuple-element.18.refs_0_), channel_id=1, source_target_pairs={{0,1},{1,0},{2,3},{3,2},{4,5},{5,4},{6,7},{7,6},{8,9},{9,8},{10,11... | collective-permute-start | bytes 884744 | tf_op jit(solution)/shard_map/ppermute | solution.py:495
  63.8 4.0 %copy-start.3 = (bf16[1,1,128,1152]{3,2,1,0:T(8,128)(2,1)S(1)}, bf16[1,1,128,1152]{3,2,1,0:T(8,128)(2,1)}, u32[]{:S(2)}) copy-start(bf16[1,1,128,1152]{3,2,1,0:T(8,128)(2,1)} %param.9) | copy-start | bytes 884740
  69.6 3.3 copy-start.14
  69.6 38.1 %collective-permute-start.4 = (bf16[128,1152]{1,0:T(8,128)(2,1)S(1)}, bf16[128,1152]{1,0:T(8,128)(2,1)}, u32[]{:S(2)}, u32[]{:S(2)}) collective-permute-start(bf16[128,1152]{1,0:T(8,128)(2,1)S(1)} %collective-permute-done.refs_1_), channel_id=1, source_target_pairs={{0,1},{1,0},{2,3},{3,2},{4,5},{5,4},{6,7},{7,6},{8,9},{9,8},{10,11... | collective-permute-start | bytes 884744 | tf_op jit(solution)/shard_map/ppermute | solution.py:495
  73.9 35.7 %collective-permute-start.8 = (bf16[2,32,54,128]{3,1,2,0:T(8,128)(2,1)}, bf16[2,32,54,128]{3,1,2,0:T(8,128)(2,1)}, u32[]{:S(2)}, u32[]{:S(2)}) collective-permute-start(bf16[2,32,54,128]{3,1,2,0:T(8,128)(2,1)} %copy.74), channel_id=1, source_target_pairs={{0,4},{4,8},{8,12},{12,0},{1,5},{5,9},{9,13},{13,1},{2,6},{6,10},{... | collective-permute-start | bytes 2654216 | tf_op jit(solution)/shard_map/ppermute | solution.py:495
  76.2 75.0 %all-to-all-start.2 = ((bf16[16,2,8,1152]{3,2,1,0:T(8,128)(2,1)}), bf16[16,2,8,1152]{3,2,1,0:T(8,128)(2,1)}, u32[]{:S(2)}, u32[]{:S(2)}) async-start(bf16[16,2,8,1152]{3,2,1,0:T(8,128)(2,1)} %pad_maximum_fusion.2), calls=%async_computation.2 | async-start | bytes 1179648 | tf_op jit(solution)/shard_map/all_to_all | solution.py:487
  82.5 22.1 %copy-start.16 = (bf16[128,1152]{1,0:T(8,128)(2,1)}, bf16[128,1152]{1,0:T(8,128)(2,1)S(1)}, u32[]{:S(2)}) copy-start(bf16[128,1152]{1,0:T(8,128)(2,1)S(1)} %collective-permute-done.1.refs_2_) | copy-start | bytes 884740
  82.6 39.6 %collective-permute-start.9 = (bf16[2,32,54,128]{3,1,2,0:T(8,128)(2,1)}, bf16[2,32,54,128]{3,1,2,0:T(8,128)(2,1)}, u32[]{:S(2)}, u32[]{:S(2)}) collective-permute-start(bf16[2,32,54,128]{3,1,2,0:T(8,128)(2,1)} %copy.74), channel_id=1, source_target_pairs={{0,8},{4,12},{8,0},{12,4},{1,9},{5,13},{9,1},{13,5},{2,10},{6,14},... | collective-permute-start | bytes 2654216 | tf_op jit(solution)/shard_map/ppermute | solution.py:495
  87.4 45.7 %copy-start.18 = (bf16[128,1152]{1,0:T(8,128)(2,1)}, bf16[128,1152]{1,0:T(8,128)(2,1)S(1)}, u32[]{:S(2)}) copy-start(bf16[128,1152]{1,0:T(8,128)(2,1)S(1)} %collective-permute-done.2.refs_3_) | copy-start | bytes 884740
  87.4 41.9 %collective-permute-start.10 = (bf16[2,32,54,128]{3,1,2,0:T(8,128)(2,1)}, bf16[2,32,54,128]{3,1,2,0:T(8,128)(2,1)}, u32[]{:S(2)}, u32[]{:S(2)}) collective-permute-start(bf16[2,32,54,128]{3,1,2,0:T(8,128)(2,1)} %copy.74), channel_id=1, source_target_pairs={{0,12},{4,0},{8,4},{12,8},{1,13},{5,1},{9,5},{13,9},{2,14},{6,2},{... | collective-permute-start | bytes 2654216 | tf_op jit(solution)/shard_map/ppermute | solution.py:495
  104.6 28.4 %copy-start.20 = (bf16[128,1152]{1,0:T(8,128)(2,1)}, bf16[128,1152]{1,0:T(8,128)(2,1)S(1)}, u32[]{:S(2)}) copy-start(bf16[128,1152]{1,0:T(8,128)(2,1)S(1)} %collective-permute-done.3.refs_4_) | copy-start | bytes 884740
  104.7 28.4 %collective-permute-start.5 = (bf16[128,1152]{1,0:T(8,128)(2,1)S(1)}, bf16[128,1152]{1,0:T(8,128)(2,1)}, u32[]{:S(2)}, u32[]{:S(2)}) collective-permute-start(bf16[128,1152]{1,0:T(8,128)(2,1)S(1)} %collective-permute-done.1.refs_2_), channel_id=1, source_target_pairs={{0,1},{1,0},{2,3},{3,2},{4,5},{5,4},{6,7},{7,6},{8,9},{9,8},{10,11... | collective-permute-start | bytes 884744 | tf_op jit(solution)/shard_map/ppermute | solution.py:495
  107.7 54.5 %collective-permute-start.11 = (bf16[2,32,54,128]{3,1,2,0:T(8,128)(2,1)}, bf16[2,32,54,128]{3,1,2,0:T(8,128)(2,1)}, u32[]{:S(2)}, u32[]{:S(2)}) collective-permute-start(bf16[2,32,54,128]{3,1,2,0:T(8,128)(2,1)} %copy.74), channel_id=1, source_target_pairs={{0,1},{1,0},{2,3},{3,2},{4,5},{5,4},{6,7},{7,6},{8,9},{9,8},{10,11... | collective-permute-start | bytes 2654216 | tf_op jit(solution)/shard_map/ppermute | solution.py:495
  109.6 54.1 %collective-permute-start.12 = (bf16[2,32,54,128]{3,1,2,0:T(8,128)(2,1)}, bf16[2,32,54,128]{3,1,2,0:T(8,128)(2,1)}, u32[]{:S(2)}, u32[]{:S(2)}) collective-permute-start(bf16[2,32,54,128]{3,1,2,0:T(8,128)(2,1)} %collective-permute-done.8), channel_id=1, source_target_pairs={{0,1},{1,0},{2,3},{3,2},{4,5},{5,4},{6,7},{7,6},{8,9},{9,8},{10,11... | collective-permute-start | bytes 2654216 | tf_op jit(solution)/shard_map/ppermute | solution.py:495
  122.1 43.2 %collective-permute-start.13 = (bf16[2,32,54,128]{3,1,2,0:T(8,128)(2,1)}, bf16[2,32,54,128]{3,1,2,0:T(8,128)(2,1)}, u32[]{:S(2)}, u32[]{:S(2)}) collective-permute-start(bf16[2,32,54,128]{3,1,2,0:T(8,128)(2,1)} %collective-permute-done.9), channel_id=1, source_target_pairs={{0,1},{1,0},{2,3},{3,2},{4,5},{5,4},{6,7},{7,6},{8,9},{9,8},{10,11... | collective-permute-start | bytes 2654216 | tf_op jit(solution)/shard_map/ppermute | solution.py:495
  129.2 38.5 %collective-permute-start.14 = (bf16[2,32,54,128]{3,1,2,0:T(8,128)(2,1)}, bf16[2,32,54,128]{3,1,2,0:T(8,128)(2,1)}, u32[]{:S(2)}, u32[]{:S(2)}) collective-permute-start(bf16[2,32,54,128]{3,1,2,0:T(8,128)(2,1)} %collective-permute-done.10), channel_id=1, source_target_pairs={{0,1},{1,0},{2,3},{3,2},{4,5},{5,4},{6,7},{7,6},{8,9},{9,8},{10,11... | collective-permute-start | bytes 2654216 | tf_op jit(solution)/shard_map/ppermute | solution.py:495
  133.0 4.6 %collective-permute-start.6 = (bf16[128,1152]{1,0:T(8,128)(2,1)S(1)}, bf16[128,1152]{1,0:T(8,128)(2,1)}, u32[]{:S(2)}, u32[]{:S(2)}) collective-permute-start(bf16[128,1152]{1,0:T(8,128)(2,1)S(1)} %collective-permute-done.2.refs_3_), channel_id=1, source_target_pairs={{0,1},{1,0},{2,3},{3,2},{4,5},{5,4},{6,7},{7,6},{8,9},{9,8},{10,11... | collective-permute-start | bytes 884744 | tf_op jit(solution)/shard_map/ppermute | solution.py:495
  136.0 1.6 copy-start.19
  136.0 1.6 copy-start.21
  137.6 1.0 copy-start.13
  138.6 1.0 copy-start.15
  139.5 1.0 copy-start.17
  148.8 1.0 copy-start.4
  151.2 27.3 %all-to-all-start.1 = ((bf16[16,64,128]{2,1,0:T(8,128)(2,1)}), bf16[16,64,128]{2,1,0:T(8,128)(2,1)S(1)}, u32[]{:S(2)}, u32[]{:S(2)}) async-start(bf16[16,64,128]{2,1,0:T(8,128)(2,1)} %copy-done.24), calls=%async_computation.1 | async-start | bytes 524288 | tf_op jit(solution)/shard_map/all_to_all | solution.py:487
  170.2 8.3 %copy-start.9 = (f32[1,2,3,1152]{3,2,1,0:T(4,128)S(1)}, f32[1,2,3,1152]{3,2,1,0:T(4,128)}, u32[]{:S(2)}) copy-start(f32[1,2,3,1152]{3,2,1,0:T(4,128)} %copy-done.8) | copy-start | bytes 82948
  178.5 1.3 copy-start.1
  179.8 0.8 copy-start.25
  180.7 0.8 copy-start.26
  181.5 34.8 %copy-start = (bf16[8,128,1152]{2,1,0:T(8,128)(2,1)S(1)}, bf16[8,128,1152]{2,1,0:T(8,128)(2,1)}, u32[]{:S(2)}) copy-start(bf16[8,128,1152]{2,1,0:T(8,128)(2,1)} %get-tuple-element.26.modded) | copy-start | bytes 7077892
  181.5 34.8 %copy-start.5 = (f32[1024,256]{1,0:T(8,128)S(1)}, f32[1024,256]{1,0:T(8,128)}, u32[]{:S(2)}) copy-start(f32[1024,256]{1,0:T(8,128)} %copy-done.4) | copy-start | bytes 3145732
  181.5 34.8 %copy-start.23 = (bf16[1024,128]{1,0:T(8,128)(2,1)S(1)}, bf16[1024,128]{1,0:T(8,128)(2,1)}, u32[]{:S(2)}) copy-start(bf16[1024,128]{1,0:T(8,128)(2,1)} %copy-done.22) | copy-start | bytes 786436
  202.5 1.1 copy-start.6
  203.6 12.7 %copy-start.10 = (bf16[128,1152]{1,0:T(8,128)(2,1)}, bf16[128,1152]{1,0:T(8,128)(2,1)S(1)}, u32[]{:S(2)}) copy-start(bf16[128,1152]{1,0:T(8,128)(2,1)S(1)} %get-tuple-element.30.modded) | copy-start | bytes 884740
  203.6 18.9 %copy-start.27 = (bf16[128,128]{1,0:T(8,128)(2,1)}, bf16[128,128]{1,0:T(8,128)(2,1)S(1)}, u32[]{:S(2)}) copy-start(bf16[128,128]{1,0:T(8,128)(2,1)S(1)} %get-tuple-element.31.reduced) | copy-start | bytes 98308
  203.6 18.9 %copy-start.29 = (bf16[128,128]{1,0:T(8,128)(2,1)}, bf16[128,128]{1,0:T(8,128)(2,1)S(1)}, u32[]{:S(2)}) copy-start(bf16[128,128]{1,0:T(8,128)(2,1)S(1)} %get-tuple-element.33.d_reduced) | copy-start | bytes 98308
  216.3 10.5 %copy-start.7 = (f32[8,128,256]{2,1,0:T(8,128)S(1)}, f32[8,128,256]{2,1,0:T(8,128)}, u32[]{:S(2)}) copy-start(f32[8,128,256]{2,1,0:T(8,128)} %copy-done.6) | copy-start | bytes 3145732
  216.3 10.5 %copy-start.11 = (bf16[128,1152]{1,0:T(8,128)(2,1)S(1)}, bf16[128,1152]{1,0:T(8,128)(2,1)}, u32[]{:S(2)}) copy-start(bf16[128,1152]{1,0:T(8,128)(2,1)} %copy-done.10) | copy-start | bytes 884740
  222.5 12.8 %all-to-all-start.5 = ((f32[16,8,768]{2,1,0:T(8,128)}), f32[16,8,768]{2,1,0:T(8,128)S(1)}, u32[]{:S(2)}, u32[]{:S(2)}) async-start(f32[16,8,768]{2,1,0:T(8,128)} %bitcast.23), calls=%async_computation.5 | async-start | bytes 786432 | tf_op jit(solution)/shard_map/all_to_all | solution.py:487
  226.8 0.8 copy-start.28
  235.3 17.6 %all-to-all-start.6 = ((f32[16,8,1536]{2,1,0:T(8,128)}), f32[16,8,1536]{2,1,0:T(8,128)S(1)}, u32[]{:S(2)}, u32[]{:S(2)}) async-start(f32[16,8,1536]{2,1,0:T(8,128)} %bitcast.29), calls=%async_computation.6 | async-start | bytes 1572864 | tf_op jit(solution)/shard_map/all_to_all | solution.py:487
  (3 other events, 2.2 us)

commit v2 on v1

v2 whole, which is shorter than its diff:
```python
import math

import jax
import jax.numpy as jnp
import numpy as np
from jax import lax
from jax.experimental import pallas as pl
from jax.experimental.pallas import tpu as pltpu
from jax.sharding import Mesh, PartitionSpec as P

WIDTH = 1152
HEADS = 8
HEAD = 72
RANK = 64
FEATURES = HEADS * HEAD
ROWS = 128
F32 = jnp.float32
BF16 = jnp.bfloat16
SCALE = 1.0 / math.sqrt(HEAD)
MIB = 1 << 20
DP = ("z", "h")
SEQ = ("x", "l", "c")


def call(kernel, out_shape, scratch=(), in_specs=None, limit=16):
    vmem = pl.BlockSpec(memory_space=pltpu.VMEM)

    def run(*operands):
        return pl.pallas_call(
            kernel,
            out_shape=out_shape,
            in_specs=in_specs or [vmem] * len(operands),
            out_specs=jax.tree.map(lambda _: vmem, out_shape),
            scratch_shapes=list(scratch),
            compiler_params=pltpu.CompilerParams(vmem_limit_bytes=limit * MIB),
        )(*operands)

    return run


def spec(space):
    return pl.BlockSpec(memory_space=space)


def dot(a, b, dims=((1,), (0,))):
    return lax.dot_general(a, b, (dims, ((), ())), preferred_element_type=F32)


NT = ((1,), (1,))
TN = ((0,), (0,))


def halves(values):
    high = values.astype(BF16)
    return high, (values - high.astype(F32)).astype(BF16)


def normalise(values):
    centred = values - jnp.mean(values, -1, keepdims=True)
    rate = lax.rsqrt(jnp.mean(centred * centred, -1, keepdims=True) + 1e-06)
    return centred * rate, rate


def lane_mask(width, dtype=F32):
    lanes = lax.broadcasted_iota(jnp.int32, (1, 128), 1)
    return (lanes < width).astype(dtype)


def split_heads(projected):
    keep = lane_mask(HEAD)
    q = projected[:, :128] * keep
    k = pltpu.roll(projected, 256 - HEAD, 1)[:, :128] * keep
    v = pltpu.roll(projected, 256 - 2 * HEAD, 1)[:, :128] * keep
    return q, k, v


def join_heads(q, k, v):
    zero = jnp.zeros_like(q)
    return (
        jnp.concatenate([q, zero], 1)
        + pltpu.roll(jnp.concatenate([k, zero], 1), HEAD, 1)
        + pltpu.roll(jnp.concatenate([v, zero], 1), 2 * HEAD, 1)
    )


def head_rate(values):
    return lax.rsqrt(jnp.sum(values * values, -1, keepdims=True) * (1.0 / HEAD) + 1e-06)


def head_norm_back(values, cotangent):
    rate = head_rate(values)
    inner = jnp.sum(cotangent * values, -1, keepdims=True) * (1.0 / HEAD)
    return rate * (cotangent - values * (rate * rate * inner))


def swap(values):
    lanes = lax.broadcasted_iota(jnp.int32, (1, 128), 1)
    return jnp.where(
        lanes < HEAD // 2,
        pltpu.roll(values, 128 - HEAD // 2, 1),
        pltpu.roll(values, HEAD // 2, 1),
    )


def softmax(scores, mask):
    weights = jnp.exp(scores * SCALE)
    if mask is not None:
        weights = weights * mask
    return weights / jnp.sum(weights, -1, keepdims=True)


def attention_back(weights, q, k, v, cotangent):
    rounded = weights.astype(BF16)
    d_v = dot(rounded, cotangent, TN).astype(BF16)
    d_weights = dot(cotangent, v, NT).astype(BF16).astype(F32)
    d_scores = weights * (d_weights - jnp.sum(d_weights * weights, -1, keepdims=True))
    d_scores = (d_scores * SCALE).astype(BF16)
    d_q = dot(d_scores, k).astype(BF16)
    d_k = dot(d_scores, q, TN).astype(BF16)
    return d_q.astype(F32), d_k.astype(F32), d_v.astype(F32)


def same_token():
    rows = lax.broadcasted_iota(jnp.int32, (ROWS, ROWS), 0)
    columns = lax.broadcasted_iota(jnp.int32, (ROWS, ROWS), 1)
    return ((rows & 7) == (columns & 7)).astype(F32)


def rotation_tables():
    row = np.arange(ROWS)
    frame = ((row // 16) % 4) * 4 + (row // 64) * 2 + (row // 8) % 2
    half = HEAD // 2
    frequency = np.exp(np.arange(half) * (-2.0 * math.log(10000.0) / HEAD))
    angle = frame[:, None] * frequency[None, :]
    cosine = np.zeros((ROWS, 128), np.float32)
    sine = np.zeros((ROWS, 128), np.float32)
    cosine[:, :half] = cosine[:, half:HEAD] = np.cos(angle)
    sine[:, :half] = -np.sin(angle)
    sine[:, half:HEAD] = np.sin(angle)
    return cosine, sine


def prologue_kernel(place, *refs):
    sources, (modded, part, first_part), held = refs[:4], refs[4:7], refs[7:11]
    rest, sems = refs[11:]
    copies = [pltpu.make_async_copy(a, b, sems.at[i]) for i, (a, b) in enumerate(zip(sources, held))]
    for copy in copies:
        copy.start()
    latents, modulation, qkv, out = held
    rest[...] = jnp.zeros_like(rest)
    copies[0].wait()
    copies[1].wait()
    normed, _ = normalise(latents[...].astype(F32))
    modded[...] = (normed * (1.0 + modulation[0, 1:2]) + modulation[0, 0:1]).astype(BF16)
    copies[2].wait()
    copies[3].wait()
    for head in range(HEADS):

        @pl.when(place[0] == head)
        def _():
            for k in range(3):
                columns = slice(k * FEATURES + head * HEAD, k * FEATURES + head * HEAD + HEAD)
                rest[0, :, k * HEAD : k * HEAD + HEAD] = qkv[0, :, columns].astype(F32)
                rest[1, :, k * HEAD : k * HEAD + HEAD] = qkv[1, :, columns].astype(F32)
            for block in range(2):
                rows = slice(18 * block, 18 * block + 18)
                rest[1, rows, 216:232] = out[block, :, 1024 + 16 * head : 1040 + 16 * head].astype(F32)
                rest[1, rows, 256:384] = out[block, :, 128 * head : 128 * head + 128].astype(F32)

    lower = place[1] == 0
    first = rest[0, :, :256].astype(BF16)
    tiles = jnp.concatenate([rest[1, :, 128 * t : 128 * t + 128] for t in range(3)], 0)
    mine = jnp.where(lower, tiles[:54], tiles[54:])
    mine = jnp.concatenate([mine, jnp.zeros((2, 128), F32)], 0).astype(BF16)
    for copy in range(32):
        part[copy] = mine
        first_part[copy, :36] = first


def prologue(place, *operands):
    return call(
        prologue_kernel,
        (
            jax.ShapeDtypeStruct((ROWS, WIDTH), BF16),
            jax.ShapeDtypeStruct((32, 56, 128), BF16),
            jax.ShapeDtypeStruct((32, 40, 256), BF16),
        ),
        [pltpu.VMEM(v.shape, v.dtype) for v in operands]
        + [pltpu.VMEM((2, 36, 384), F32), pltpu.SemaphoreType.DMA((4,))],
        [spec(pltpu.SMEM)] + [spec(pl.ANY)] * 4,
    )(place, *operands)


def adapters_kernel(down, up, down_parts, up_parts):
    for block in range(2):
        high, low = halves(down[block])
        down_parts[block, :64] = high
        down_parts[block, 64:] = low
        for head in range(HEADS):
            start = head * HEAD
            columns = [up[block, :, k * FEATURES + start : k * FEATURES + start + HEAD] for k in range(3)]
            zero = jnp.zeros((RANK, 128 - HEAD), F32)
            wide = join_heads(*[jnp.concatenate([part, zero], 1) for part in columns])
            high, low = halves(wide)
            up_parts[block, head, :64] = high
            up_parts[block, head, 64:128] = low
            up_parts[block, head, 128:] = high


def adapters(down, up):
    return call(
        adapters_kernel,
        (
            jax.ShapeDtypeStruct((2, 128, WIDTH), BF16),
            jax.ShapeDtypeStruct((2, HEADS, 192, 256), BF16),
        ),
    )(down, up)


def spatial_kernel(
    place,
    modded,
    weight,
    down,
    up,
    latents,
    targets,
    sent,
    projected,
    reduced,
    weights,
    merged,
):
    for chunk in range(32):
        merged[36 * chunk : 36 * chunk + 36, :] = weight[chunk, :36]
    sent[:, :, 1024 : 1024 + WIDTH] = latents[...].astype(F32).reshape(16, 8, WIDTH).astype(BF16)
    sent[:, :, 1024 + WIDTH :] = targets[...].astype(F32).reshape(16, 8, WIDTH).astype(BF16)
    rows = modded[...].reshape(8 * ROWS, WIDTH)
    low = dot(rows, down[0], NT)
    high, rest = halves(low[:, :64] + low[:, 64:])
    reduced[...] = jnp.concatenate([high, rest], 1)
    adapted = dot(jnp.concatenate([high, high, rest], 1), up[0, place[0]])
    projected[...] = dot(rows, merged[...]) + adapted
    for frame in range(8):
        q, k, v = split_heads(projected[frame * ROWS : frame * ROWS + ROWS])
        q = (q * head_rate(q)).astype(BF16)
        k = (k * head_rate(k)).astype(BF16)
        w = softmax(dot(q, k, NT), None)
        weights[frame] = w
        attended = dot(w.astype(BF16), v.astype(BF16)).reshape(16, 8, 128)
        sent[:, :, 128 * frame : 128 * frame + 128] = attended.astype(BF16)


def spatial(place, *operands):
    return call(
        spatial_kernel,
        (
            jax.ShapeDtypeStruct((16, 8, 1024 + 2 * WIDTH), BF16),
            jax.ShapeDtypeStruct((8 * ROWS, 256), F32),
            jax.ShapeDtypeStruct((8 * ROWS, 128), BF16),
            jax.ShapeDtypeStruct((8, ROWS, ROWS), F32),
        ),
        [pltpu.VMEM((WIDTH, 256), BF16)],
        [spec(pltpu.SMEM)] + [spec(pltpu.VMEM)] * 6,
        limit=24,
    )(place, *operands)


def spatial_back_kernel(place, cotangent, modded, projected, reduced, weights, up, grad, d_projected):
    for pair in range(4):
        rows = cotangent[:, 16 * pair : 16 * pair + 16, :].astype(F32).reshape(16, 2, 8, 128)
        for side in range(2):
            frame = 2 * pair + side
            span = slice(frame * ROWS, frame * ROWS + ROWS)
            q, k, v = split_heads(projected[span])
            q_out = (q * head_rate(q)).astype(BF16)
            k_out = (k * head_rate(k)).astype(BF16)
            d_q, d_k, d_v = attention_back(
                weights[frame],
                q_out,
                k_out,
                v.astype(BF16),
                rows[:, side].reshape(ROWS, 128).astype(BF16),
            )
            d_projected[span] = join_heads(head_norm_back(q, d_q), head_norm_back(k, d_k), d_v)
    high, rest = halves(d_projected[...])
    both = dot(reduced[...], jnp.concatenate([high, rest], 1), TN)
    grad_up = both[:64, :256] + both[64:, :256] + both[:64, 256:] + both[64:, 256:]
    head = up[0, place[0], :128]
    two = dot(high, head, NT) + dot(rest, head, NT)
    low_high, low_rest = halves(two[:, :64] + two[:, 64:])
    down = dot(
        jnp.concatenate([low_high, low_rest], 1), modded[...].reshape(8 * ROWS, WIDTH), TN
    )
    store_tiles(grad, 0, down[:64] + down[64:])
    store_tiles(grad, 9, grad_up)


def store_tiles(ref, start, values):
    for tile in range(values.shape[1] // 128):
        ref[:, start + tile, :] = values[:, 128 * tile : 128 * tile + 128]


def spatial_back(*operands):
    vmem = spec(pltpu.VMEM)
    return call(
        spatial_back_kernel,
        jax.ShapeDtypeStruct((RANK, 11, 128), F32),
        [pltpu.VMEM((8 * ROWS, 256), F32)],
        [spec(pltpu.SMEM)] + [vmem] * 6,
        limit=24,
    )(*operands)


def assemble(parts, held, sems, qkv, out_first, out_second):
    for x in range(4):
        copy = part_copy(parts, held, sems, x)
        copy.wait()
        for c in range(2):
            head = 2 * x + c
            lower, upper = held.at[4 * x + c], held.at[4 * x + 2 + c]
            main = slice(128 * head, 128 * head + 128)
            tail = slice(1024 + 16 * head, 1040 + 16 * head)
            for d in range(32):
                a = 36 * d
                qkv[head, a : a + 36, :128] = lower[d, 0:36]
                qkv[head, a : a + 18, 128:] = lower[d, 36:54]
                qkv[head, a + 18 : a + 36, 128:] = upper[d, 0:18]
                rows = slice(18 * d, 18 * d + 18)
                out_first[rows, main] = upper[d, 18:36]
                out_second[rows, main] = upper[d, 36:54]
                out_first[rows, tail] = lower[d, 36:54, 88:104]
                out_second[rows, tail] = upper[d, 0:18, 88:104]


def part_copy(parts, held, sems, x):
    span = pl.ds(4 * x, 4)
    return pltpu.make_async_copy(parts.at[span], held.at[span], sems.at[x])


def by_rows(received, columns):
    values = received[:, :, columns].astype(F32)
    frames = [x * 4 + l * 2 + c for l in range(2) for x in range(4) for c in range(2)]
    return jnp.concatenate([values[f] for f in frames], 0)


def temporal_kernel(
    received,
    modulation,
    parts,
    down,
    up,
    cosine,
    sine,
    sent,
    grad,
    wide,
    modded,
    reduced,
    d_projected,
    ups,
    projected,
    weights,
    q_all,
    k_all,
    v_all,
    held,
    qkv,
    out_first,
    out_second,
    sems,
):
    for x in range(4):
        part_copy(parts, held, sems, x).start()
    for head in range(HEADS):
        x, c = head // 2, head % 2
        rows = jnp.concatenate(
            [
                received[x * 4 + 2 * l + c, :, 128 * g : 128 * g + 128].astype(F32)
                for l in range(2)
                for g in range(8)
            ],
            0,
        )
        wide[:, HEAD * head : HEAD * head + HEAD] = rows[:, :HEAD]
    assemble(parts, held, sems, qkv, out_first, out_second)
    gate_first, gate_second = modulation[0, 2:3], modulation[1, 2:3]
    mixed = dot(wide[...].astype(BF16), out_first[...])
    middle = (by_rows(received, slice(1024, 1024 + WIDTH)) + gate_first * mixed).astype(BF16).astype(F32)
    normed, rate = normalise(middle)
    scale = 1.0 + modulation[1, 1:2]
    modded[...] = (normed * scale + modulation[1, 0:1]).astype(BF16)
    low = dot(modded[...], down[1], NT)
    high, rest = halves(low[:, :64] + low[:, 64:])
    reduced[...] = jnp.concatenate([high, rest], 1)
    three = jnp.concatenate([high, high, rest], 1)
    mask = same_token()
    for head in range(HEADS):
        both = dot(modded[...], qkv[head]) + dot(three, up[1, head])
        projected[head] = both
        q, k, v = split_heads(both)
        q = q * head_rate(q)
        k = k * head_rate(k)
        q = (q * cosine[...] + swap(q) * sine[...]).astype(BF16)
        k = (k * cosine[...] + swap(k) * sine[...]).astype(BF16)
        v = v.astype(BF16)
        w = softmax(dot(q, k, NT), mask)
        q_all[head], k_all[head], v_all[head], weights[head] = q, k, v, w
        wide[:, HEAD * head : HEAD * head + HEAD] = dot(w.astype(BF16), v)[:, :HEAD]
    mixed = dot(wide[...].astype(BF16), out_second[...])
    produced = (middle + gate_second * mixed).astype(BF16).astype(F32)
    error = ((produced - by_rows(received, slice(1024 + WIDTH, None))) / WIDTH).astype(BF16).astype(F32)
    wide[...] = dot((gate_second * error).astype(BF16), out_second[...], NT)
    d_low = jnp.zeros((ROWS, 128), F32)
    d_modded = jnp.zeros((ROWS, WIDTH), F32)
    for head in range(HEADS):
        cotangent = wide[:, HEAD * head : HEAD * head + HEAD].astype(BF16)
        cotangent = jnp.concatenate([cotangent, jnp.zeros((ROWS, 128 - HEAD), BF16)], 1)
        d_q, d_k, d_v = attention_back(
            weights[head], q_all[head], k_all[head], v_all[head], cotangent
        )
        d_q = d_q * cosine[...] - swap(d_q) * sine[...]
        d_k = d_k * cosine[...] - swap(d_k) * sine[...]
        q, k, _ = split_heads(projected[head])
        joined = join_heads(head_norm_back(q, d_q), head_norm_back(k, d_k), d_v)
        d_projected[head] = joined
        high, rest = halves(joined)
        d_low += dot(high, up[1, head, :128], NT) + dot(rest, up[1, head, :128], NT)
        d_modded += dot(high, qkv[head], NT)
    d_low = d_low[:, :64] + d_low[:, 64:]
    high, rest = halves(d_low)
    d_reduced = jnp.concatenate([high, rest], 1)
    through = dot(jnp.concatenate([high, high], 1), down[1]) + dot(rest, down[1, :64])
    d_modded = (d_modded.astype(BF16) + through.astype(BF16)).astype(F32)
    d_normed = d_modded * scale
    inner = jnp.mean(d_normed * normed, -1, keepdims=True)
    d_middle = rate * (d_normed - jnp.mean(d_normed, -1, keepdims=True) - normed * inner)
    d_middle = (error.astype(BF16) + d_middle.astype(BF16)).astype(F32)
    wide[...] = dot((gate_first * d_middle).astype(BF16), out_first[...], NT)
    for head in range(HEADS):
        x, c = head // 2, head % 2
        rows = wide[:, HEAD * head : HEAD * head + HEAD].astype(BF16)
        rows = jnp.concatenate([rows, jnp.zeros((ROWS, 128 - HEAD), BF16)], 1)
        sent[x * 4 + c] = rows[:64]
        sent[x * 4 + 2 + c] = rows[64:]
    ups[:, 1664:] = jnp.zeros((64, 128), F32)
    for head in range(HEADS):
        high, rest = halves(d_projected[head])
        both = dot(reduced[...], jnp.concatenate([high, rest], 1), TN)
        part = both[:64, :256] + both[64:, :256] + both[:64, 256:] + both[64:, 256:]
        for k in range(3):
            start = k * FEATURES + head * HEAD
            ups[:, start : start + HEAD] = part[:, k * HEAD : k * HEAD + HEAD]
    down = dot(d_reduced, modded[...], TN)
    store_tiles(grad, 0, down[:64] + down[64:])
    store_tiles(grad, 9, ups[...])


def temporal(*operands):
    return call(
        temporal_kernel,
        (
            jax.ShapeDtypeStruct((16, 64, 128), BF16),
            jax.ShapeDtypeStruct((RANK, 23, 128), F32),
        ),
        [
            pltpu.VMEM((ROWS, FEATURES), F32),
            pltpu.VMEM((ROWS, WIDTH), BF16),
            pltpu.VMEM((ROWS, 128), BF16),
            pltpu.VMEM((HEADS, ROWS, 256), F32),
            pltpu.VMEM((RANK, 1792), F32),
            pltpu.VMEM((HEADS, ROWS, 256), F32),
            pltpu.VMEM((HEADS, ROWS, ROWS), F32),
            pltpu.VMEM((HEADS, ROWS, 128), BF16),
            pltpu.VMEM((HEADS, ROWS, 128), BF16),
            pltpu.VMEM((HEADS, ROWS, 128), BF16),
            pltpu.VMEM((16, 32, 56, 128), BF16),
            pltpu.VMEM((HEADS, WIDTH, 256), BF16),
            pltpu.VMEM((FEATURES, WIDTH), BF16),
            pltpu.VMEM((FEATURES, WIDTH), BF16),
            pltpu.SemaphoreType.DMA((4,)),
        ],
        [spec(pltpu.VMEM)] * 2 + [spec(pl.ANY)] + [spec(pltpu.VMEM)] * 4,
        limit=32,
    )(*operands)


def epilogue_kernel(place, own, other, grad_down, grad_up):
    for side, ref in enumerate((own, other)):
        core = place[2] if side == 0 else 1 - place[2]
        rows = pl.ds(pl.multiple_of(core * 32, 32), 32)
        for tile in range(9):
            columns = slice(128 * tile, 128 * tile + 128)
            grad_down[0, rows, columns] = ref[:, tile, :]
            grad_down[1, rows, columns] = ref[:, 25 + tile, :]
        for head in range(HEADS):
            both = jnp.concatenate([ref[:, 9 + 2 * head, :], ref[:, 10 + 2 * head, :]], 1)
            for k in range(3):
                start = k * FEATURES + head * HEAD
                grad_up[0, rows, start : start + HEAD] = both[:, k * HEAD : k * HEAD + HEAD]
        for tile in range(13):
            grad_up[1, rows, 128 * tile : 128 * tile + 128] = ref[:, 34 + tile, :]
        grad_up[1, rows, 1664:1728] = ref[:, 47, :][:, :64]


def epilogue(place, own, other):
    vmem = spec(pltpu.VMEM)
    return call(
        epilogue_kernel,
        (
            jax.ShapeDtypeStruct((2, RANK, WIDTH), F32),
            jax.ShapeDtypeStruct((2, RANK, 3 * FEATURES), F32),
        ),
        in_specs=[spec(pltpu.SMEM), vmem, vmem],
    )(place, own, other)


def exchange(values, axes):
    return lax.all_to_all(values, axes, 0, 0)


def spread(values, axes, count):
    return exchange(jnp.broadcast_to(values[None], (count,) + values.shape), axes)


def swap_cores(values):
    return lax.ppermute(values, "c", [(0, 1), (1, 0)])


def add_cores(values, c):
    mine = lax.dynamic_slice_in_dim(values, c * 32, 32, 0)
    return mine, swap_cores(lax.dynamic_slice_in_dim(values, (1 - c) * 32, 32, 0))


def on_device(latents, targets, modulation, qkv, out, down, up):
    x, l, c = lax.axis_index("x"), lax.axis_index("l"), lax.axis_index("c")
    place = jnp.stack([x * 2 + c, l, c]).astype(jnp.int32)
    modulation = modulation[0]
    modded, part, first = prologue(place, latents[0, 0], modulation, qkv, out)
    modded = lax.all_gather(modded, ("x", "c"), axis=0, tiled=False)
    parts = lax.all_gather(exchange(part, DP), SEQ, axis=0, tiled=False)
    first = exchange(first, DP)
    down_parts, up_parts = adapters(down.transpose(0, 2, 1), up)
    sent, projected, reduced, weights = spatial(
        place, modded, first, down_parts, up_parts, latents[0, 0], targets[0, 0]
    )
    received = exchange(sent, SEQ)
    cosine, sine = rotation_tables()
    sent, late = temporal(
        received,
        modulation,
        parts,
        down_parts,
        up_parts,
        jnp.asarray(cosine),
        jnp.asarray(sine),
    )
    cotangent = exchange(sent, SEQ)
    late = sum(add_cores(late, c))
    early = spatial_back(place, cotangent, modded, projected, reduced, weights, up_parts)
    mine, other = add_cores(early, c)
    first_up, second_up = mine[:, 9:], other[:, 9:]
    total = jnp.concatenate(
        [
            mine[:, :9] + other[:, :9],
            jnp.where(c == 0, first_up, second_up),
            jnp.where(c == 0, second_up, first_up),
            late,
        ],
        1,
    )
    total = exchange(total.reshape(32, 9, 4, 128), ("z", "x")).reshape(32, 36, 128)
    ups = jnp.sum(total[:, 9:13].reshape(8, 4, 4, 128), 0).reshape(16, 128)
    total = jnp.concatenate([jnp.sum(total[:, :9], 0), ups, jnp.sum(total[:, 13:], 0)], 0)
    total = jnp.sum(spread(total, ("h", "l"), 8), 0)
    total = spread(total, ("z", "x"), 32)
    grad_down, grad_up = epilogue(place, total, swap_cores(total))
    return grad_down.transpose(0, 2, 1), grad_up


def solution(mesh):
    inner = Mesh(mesh.devices.reshape(8, 4, 4, 2, 2), ("z", "h", "x", "l", "c"))
    in_specs = (
        P(DP, SEQ, None, None),
        P(DP, SEQ, None, None),
        P(DP, None, None, None),
        P(None, DP, None),
        P(None, DP, None),
        P(),
        P(),
    )
    return jax.shard_map(
        on_device, mesh=inner, in_specs=in_specs, out_specs=(P(), P()), check_vma=False
    )
```

time: 334 us -> 254 us (0.76)
  starting transfers between devices: 71.6 us -> 22.8 us
  local copies, waits for them, and re-layouts: 46.4 us -> 23.7 us
  between operations: 1.23 us -> 14.3 us
  other arithmetic: 10.9 us -> 0.43 us
  Pallas kernels: 48.7 us -> 40.9 us
  waiting for transfers between devices: 31.3 us -> 24.9 us
  blocking collectives: 122 us -> 126 us
    ppermute x15 -> x3, starting transfers between devices: 44.6 us -> 12.4 us  [swap_cores(): return lax.ppermute(values, 'c', [(0, 1), (1, 0)])]
    all_to_all x5 -> x2, starting transfers between devices: 27.1 us -> 10.3 us  [exchange(): return lax.all_to_all(values, axes, 0, 0)]
    ppermute x7 -> x0, local copies, waits for them, and re-layouts: 12.5 us -> none  [shift(): lax.ppermute(values, axis, [(i, (i + by) % count) for i in range(count)])]
    ppermute x15 -> x3, waiting for transfers between devices: 13 us -> 2.96 us  [swap_cores(): return lax.ppermute(values, 'c', [(0, 1), (1, 0)])]
    reshape x3 -> x1, local copies, waits for them, and re-layouts: 9.83 us -> 0.38 us  [on_device(): total.reshape(32, 9, 4, 128)]
    pallas_call x7 -> x6, Pallas kernels: 48.7 us -> 40.9 us  [run(): pl.pallas_call(kernel, out_shape=out_shape, in_specs=in_specs or [vmem] *...]
    unnamed x66 -> x45, local copies, waits for them, and re-layouts: 17.1 us -> 22 us
    convert_element_type x2 -> x0, other arithmetic: 4.59 us -> none  [two_parts(): return (high.astype(BF16), (values - high).astype(BF16))]
  transfers between devices with their start and end apart: 20 -> 7, of which waited for: 4 -> 4; matrix products, arithmetic and copies ran while one was open for 12% -> 0% of each run, Pallas kernels for 5% -> 5%
where the time goes in v2:
time: 254 us; the launch traced here: 253 us
  blocking collectives  126 us (50%)
  Pallas kernels  40.9 us (16%)
  waiting for transfers between devices  24.9 us (10%)
  local copies, waits for them, and re-layouts  23.7 us (9%)
  starting transfers between devices  22.8 us (9%)
  between operations  14.3 us (6%)
    all_to_all x5, blocking collectives, exchange(): return lax.all_to_all(values, axes, 0, 0)  126 us
    pallas_call x6, Pallas kernels, run(): pl.pallas_call(kernel, out_shape=out_shape, in_specs=in_specs or [vmem] *...  40.9 us
    unnamed x45, local copies, waits for them, and re-layouts  22 us
    all_to_all x2, waiting for transfers between devices, exchange(): return lax.all_to_all(values, axes, 0, 0)  21.9 us
    ppermute x3, starting transfers between devices, swap_cores(): return lax.ppermute(values, 'c', [(0, 1), (1, 0)])  12.4 us
    all_to_all x2, starting transfers between devices, exchange(): return lax.all_to_all(values, axes, 0, 0)  10.3 us
  transfers between devices with their start and end apart: 7, of which 4 were waited for; matrix products, arithmetic and copies ran while one was open for 0% of the time, Pallas kernels for 5%

profile of v2, /device:TPU:1, one launch (start us, length us, event | category | flops | bytes accessed | tf_op | source)
XLA Modules:
  0.0 253.1 jit_solution(7827651300826563347)
XLA Ops:
  7.2 0.8 copy.39
  8.0 1.0 copy.32.refs_2_
  9.0 0.9 copy.33.refs_3_
  9.9 0.1 pad_add_fusion.place
  10.0 1.0 copy-done.3
  10.9 2.2 shard_map.104
  13.2 0.0 all-gather.7.cloned.1.call-start
  13.3 33.2 %all_to_all.35 = bf16[32,56,128]{2,1,0:T(8,128)(2,1)} all-to-all(bf16[32,56,128]{2,1,0:T(8,128)(2,1)S(1)} %get-tuple-element.20), channel_id=1, replica_groups=mesh['z'=8,'h'=4,'x'=4,'l'=2,'c'=2] {'z','h'}, dimensions={0} | all-to-all | bytes 917504 | tf_op jit(solution)/shard_map/all_to_all | solution.py:519
  46.5 6.4 %all-to-all-start = ((bf16[32,40,256]{2,1,0:T(8,128)(2,1)}), bf16[32,40,256]{2,1,0:T(8,128)(2,1)S(1)}, u32[]{:S(2)}, u32[]{:S(2)}) async-start(bf16[32,40,256]{2,1,0:T(8,128)(2,1)} %get-tuple-element.16), calls=%async_computation | async-start | bytes 1310720 | tf_op jit(solution)/shard_map/all_to_all | solution.py:519
  53.0 1.2 copy-done.7
  54.2 1.1 copy-done.10
  55.2 1.7 shard_map.105
  56.9 17.8 %all-to-all-done.weight = bf16[32,40,256]{2,1,0:T(8,128)(2,1)S(1)} async-done(((bf16[32,40,256]{2,1,0:T(8,128)(2,1)}), bf16[32,40,256]{2,1,0:T(8,128)(2,1)S(1)}, u32[]{:S(2)}, u32[]{:S(2)}) %all-to-all-start) | async-done | bytes 655392 | tf_op jit(solution)/shard_map/all_to_all | solution.py:519
  74.8 1.7 copy-done
  76.5 1.0 copy-done.15
  77.5 6.0 %shard_map.106 = (bf16[16,8,3328]{2,1,0:T(8,128)(2,1)S(1)}, f32[1024,256]{1,0:T(8,128)S(1)}, bf16[1024,128]{1,0:T(8,128)(2,1)S(1)}, f32[8,128,128]{2,1,0:T(8,128)S(1)}) custom-call(s32[3]{0:T(128)S(1)} %pad_add_fusion.place, bf16[8,128,1152]{2,1,0:T(8,128)(2,1)S(1)} %bitcast.16, bf16[32,40,256]{2,1,0:T(8,128)(2,1)S(1)} %all-to-all-done.weight, ...), custom_call_target="tpu_custom_call" | custom-call | tf_op jit(solution)/shard_map/pallas_call | solution.py:29
  83.5 1.0 copy-done.5
  84.5 0.8 copy-done.11
  85.3 0.7 copy-done.17
  86.0 29.7 %all_to_all.36.received = bf16[16,8,3328]{2,1,0:T(8,128)(2,1)S(1)} all-to-all(bf16[16,8,3328]{2,1,0:T(8,128)(2,1)S(1)} %get-tuple-element.19), channel_id=1, replica_groups=mesh['z'=8,'h'=4,'x'=4,'l'=2,'c'=2] {'x','l','c'}, dimensions={0} | all-to-all | bytes 1703936 | tf_op jit(solution)/shard_map/all_to_all | solution.py:519
  115.7 3.1 %copy-done.2 = bf16[512,56,128]{2,1,0:T(8,128)(2,1)S(1)} copy-done((bf16[512,56,128]{2,1,0:T(8,128)(2,1)S(1)}, bf16[512,56,128]{2,1,0:T(8,128)(2,1)}, u32[]{:S(2)}) %copy-start.2) | copy-done | bytes 7340056
  118.8 0.8 copy-done.14
  119.5 0.8 copy-done.19
  120.4 0.8 copy-done.20
  121.2 22.5 %shard_map.107 = (bf16[16,64,128]{2,1,0:T(8,128)(2,1)S(1)}, f32[64,23,128]{2,1,0:T(8,128)S(1)}) custom-call(bf16[16,8,3328]{2,1,0:T(8,128)(2,1)S(1)} %all_to_all.36.received, f32[2,3,1152]{2,1,0:T(4,128)S(1)} %bitcast.23, bf16[16,32,56,128]{3,2,1,0:T(8,128)(2,1)S(1)} %bitcast.18, bf16[2,128,1152]{2,1,0:T(8,128)(2,1)S(1)} %get-tuple-element.17.down, ...), custom_call_target="tpu_custom_call" | custom-call | tf_op jit(solution)/shard_map/pallas_call | solution.py:29
  143.8 0.9 copy-done.8
  144.6 0.7 copy-done.16
  145.3 3.9 %all-to-all-start.3 = ((bf16[16,64,128]{2,1,0:T(8,128)(2,1)}), bf16[16,64,128]{2,1,0:T(8,128)(2,1)S(1)}, u32[]{:S(2)}, u32[]{:S(2)}) async-start(bf16[16,64,128]{2,1,0:T(8,128)(2,1)} %copy-done.16), calls=%async_computation.3 | async-start | bytes 524288 | tf_op jit(solution)/shard_map/all_to_all | solution.py:519
  149.2 1.0 constant_dynamic-slice_fusion
  150.2 2.1 collective-permute-start.1
  152.4 4.1 %all-to-all-done.3.cotangent = bf16[16,64,128]{2,1,0:T(8,128)(2,1)S(1)} async-done(((bf16[16,64,128]{2,1,0:T(8,128)(2,1)}), bf16[16,64,128]{2,1,0:T(8,128)(2,1)S(1)}, u32[]{:S(2)}, u32[]{:S(2)}) %all-to-all-start.3) | async-done | bytes 262176 | tf_op jit(solution)/shard_map/all_to_all | solution.py:519
  156.5 1.7 copy-done.1
  158.1 1.2 copy-done.6
  159.3 0.9 copy-done.18
  160.3 6.0 %shard_map.108 = f32[64,11,128]{2,1,0:T(8,128)S(1)} custom-call(s32[3]{0:T(128)S(1)} %pad_add_fusion.place, bf16[16,64,128]{2,1,0:T(8,128)(2,1)S(1)} %all-to-all-done.3.cotangent, bf16[8,128,1152]{2,1,0:T(8,128)(2,1)S(1)} %bitcast.17, f32[1024,256]{1,0:T(8,128)S(1)} %copy-done.6, bf16[1024,128]{1,0:T(8,128)(2,1)S(1)} %copy-done.18, ...), custom_call_target="tpu_custom_call" | custom-call | tf_op jit(solution)/shard_map/pallas_call | solution.py:29
  166.4 2.9 %collective-permute-start = (f32[32,11,128]{2,1,0:T(8,128)S(1)}, f32[32,11,128]{2,1,0:T(8,128)S(1)}, u32[]{:S(2)}, u32[]{:S(2)}) collective-permute-start(f32[32,11,128]{2,1,0:T(8,128)S(1)} %constant_dynamic-slice_fusion.1), channel_id=1, source_target_pairs={{0,1},{1,0},{2,3},{3,2},{4,5},{5,4},{6,7},{7,6},{8,9},{9,8},{10,11... | collective-permute-start | bytes 540680 | tf_op jit(solution)/shard_map/ppermute | solution.py:527
  169.4 1.1 collective-permute-done
  170.5 0.1 pad_maximum_fusion
  170.7 0.1 copy.34
  170.8 0.4 copy.35
  171.2 25.3 %all_to_all.37 = f32[32,9,4,128]{3,2,1,0:T(4,128)S(1)} all-to-all(f32[32,9,4,128]{3,2,1,0:T(4,128)S(1)} %copy.35), channel_id=1, replica_groups=mesh['z'=8,'h'=4,'x'=4,'l'=2,'c'=2] {'z','x'}, dimensions={0} | all-to-all | bytes 1179648 | tf_op jit(solution)/shard_map/all_to_all | solution.py:519
  196.5 0.1 copy.36
  196.7 14.1 %all_to_all.38 = f32[8,48,128]{2,1,0:T(8,128)S(1)} all-to-all(f32[8,48,128]{2,1,0:T(8,128)S(1)} %broadcast_in_dim.4), channel_id=1, replica_groups=mesh['z'=8,'h'=4,'x'=4,'l'=2,'c'=2] {'h','l'}, dimensions={0} | all-to-all | bytes 393216 | tf_op jit(solution)/shard_map/all_to_all | solution.py:519
  210.8 0.1 broadcast_in_dim.5
  210.9 23.6 %all_to_all.39.own = f32[32,48,128]{2,1,0:T(8,128)S(1)} all-to-all(f32[32,48,128]{2,1,0:T(8,128)S(1)} %broadcast_in_dim.5), channel_id=1, replica_groups=mesh['z'=8,'h'=4,'x'=4,'l'=2,'c'=2] {'z','x'}, dimensions={0} | all-to-all | bytes 1572864 | tf_op jit(solution)/shard_map/all_to_all | solution.py:519
  234.5 7.4 %collective-permute-start.2 = (f32[32,48,128]{2,1,0:T(8,128)S(1)}, f32[32,48,128]{2,1,0:T(8,128)S(1)}, u32[]{:S(2)}, u32[]{:S(2)}) collective-permute-start(f32[32,48,128]{2,1,0:T(8,128)S(1)} %all_to_all.39.own), channel_id=1, source_target_pairs={{0,1},{1,0},{2,3},{3,2},{4,5},{5,4},{6,7},{7,6},{8,9},{9,8},{10,11... | collective-permute-start | bytes 2359304 | tf_op jit(solution)/shard_map/ppermute | solution.py:527
  242.0 1.9 collective-permute-done.2.other
  243.8 2.4 shard_map.109
  (43 shorter events, 0.4 us)
Async XLA Ops:
  7.2 67.6 %all-gather.5.cloned.1.call-start = ((), (), s32[]{:S(2)}) async-start(), calls=%async_computation.7 | async-start | bytes 2654208 | tf_op jit(solution)/shard_map/all_gather | solution.py:540
  8.0 45.0 %copy-start.13 = (f32[1,2,3,1152]{3,2,1,0:T(4,128)}, f32[1,2,3,1152]{3,2,1,0:T(4,128)S(1)}, u32[]{:S(2)}) copy-start(f32[1,2,3,1152]{3,2,1,0:T(4,128)S(1)} %copy.39) | copy-start | bytes 82948
  10.0 1.0 copy-start.3
  13.2 61.6 %copy-start.4 = (bf16[1,1,128,1152]{3,2,1,0:T(8,128)(2,1)S(1)}, bf16[1,1,128,1152]{3,2,1,0:T(8,128)(2,1)}, u32[]{:S(2)}) copy-start(bf16[1,1,128,1152]{3,2,1,0:T(8,128)(2,1)} %param.9) | copy-start | bytes 884740
  13.2 102.4 %all-gather.7.cloned.1.call-start = ((), (), s32[]{:S(2)}) async-start(), calls=%async_computation.8 | async-start | bytes 7798784 | tf_op jit(solution)/shard_map/all_gather | solution.py:541
  46.5 28.3 %all-to-all-start = ((bf16[32,40,256]{2,1,0:T(8,128)(2,1)}), bf16[32,40,256]{2,1,0:T(8,128)(2,1)S(1)}, u32[]{:S(2)}, u32[]{:S(2)}) async-start(bf16[32,40,256]{2,1,0:T(8,128)(2,1)} %get-tuple-element.16), calls=%async_computation | async-start | bytes 1310720 | tf_op jit(solution)/shard_map/all_to_all | solution.py:519
  53.0 1.2 copy-start.7
  54.2 1.1 copy-start.10
  74.8 1.7 copy-start
  76.5 1.0 copy-start.15
  83.5 1.0 copy-start.5
  84.5 0.8 copy-start.11
  85.3 0.7 copy-start.17
  115.7 3.1 %copy-start.2 = (bf16[512,56,128]{2,1,0:T(8,128)(2,1)S(1)}, bf16[512,56,128]{2,1,0:T(8,128)(2,1)}, u32[]{:S(2)}) copy-start(bf16[512,56,128]{2,1,0:T(8,128)(2,1)} %all-gather.7.cloned.1.call-done) | copy-start | bytes 22020100
  118.8 0.8 copy-start.14
  119.5 0.8 copy-start.19
  120.4 0.8 copy-start.20
  121.2 35.2 %copy-start.12 = (f32[8,128,128]{2,1,0:T(8,128)S(1)}, f32[8,128,128]{2,1,0:T(8,128)}, u32[]{:S(2)}) copy-start(f32[8,128,128]{2,1,0:T(8,128)} %copy-done.11) | copy-start | bytes 1572868
  143.7 0.9 copy-start.8
  144.6 0.7 copy-start.16
  145.3 11.1 %all-to-all-start.3 = ((bf16[16,64,128]{2,1,0:T(8,128)(2,1)}), bf16[16,64,128]{2,1,0:T(8,128)(2,1)S(1)}, u32[]{:S(2)}, u32[]{:S(2)}) async-start(bf16[16,64,128]{2,1,0:T(8,128)(2,1)} %copy-done.16), calls=%async_computation.3 | async-start | bytes 524288 | tf_op jit(solution)/shard_map/all_to_all | solution.py:519
  150.2 19.1 %collective-permute-start.1 = (f32[32,23,128]{2,1,0:T(8,128)S(1)}, f32[32,23,128]{2,1,0:T(8,128)S(1)}, u32[]{:S(2)}, u32[]{:S(2)}) collective-permute-start(f32[32,23,128]{2,1,0:T(8,128)S(1)} %constant_dynamic-slice_fusion), channel_id=1, source_target_pairs={{0,1},{1,0},{2,3},{3,2},{4,5},{5,4},{6,7},{7,6},{8,9},{9,8},{10,11... | collective-permute-start | bytes 1130504 | tf_op jit(solution)/shard_map/ppermute | solution.py:527
  156.4 1.7 copy-start.1
  158.1 1.2 copy-start.6
  159.3 0.9 copy-start.18
  160.3 9.0 %copy-start.9 = (f32[64,23,128]{2,1,0:T(8,128)S(1)}, f32[64,23,128]{2,1,0:T(8,128)}, u32[]{:S(2)}) copy-start(f32[64,23,128]{2,1,0:T(8,128)} %copy-done.8) | copy-start | bytes 2260996
  166.4 4.1 %collective-permute-start = (f32[32,11,128]{2,1,0:T(8,128)S(1)}, f32[32,11,128]{2,1,0:T(8,128)S(1)}, u32[]{:S(2)}, u32[]{:S(2)}) collective-permute-start(f32[32,11,128]{2,1,0:T(8,128)S(1)} %constant_dynamic-slice_fusion.1), channel_id=1, source_target_pairs={{0,1},{1,0},{2,3},{3,2},{4,5},{5,4},{6,7},{7,6},{8,9},{9,8},{10,11... | collective-permute-start | bytes 540680 | tf_op jit(solution)/shard_map/ppermute | solution.py:527
  234.5 9.3 %collective-permute-start.2 = (f32[32,48,128]{2,1,0:T(8,128)S(1)}, f32[32,48,128]{2,1,0:T(8,128)S(1)}, u32[]{:S(2)}, u32[]{:S(2)}) collective-permute-start(f32[32,48,128]{2,1,0:T(8,128)S(1)} %all_to_all.39.own), channel_id=1, source_target_pairs={{0,1},{1,0},{2,3},{3,2},{4,5},{5,4},{6,7},{7,6},{8,9},{9,8},{10,11... | collective-permute-start | bytes 2359304 | tf_op jit(solution)/shard_map/ppermute | solution.py:527
Sparse Core Ops, SparseCore 0:
  13.4 36.8 all-gather.4
  52.4 62.2 all-gather.6

commit v3 on v2

--- a/solution.py
+++ b/solution.py
@@ -22,17 +22,21 @@
 SEQ = ("x", "l", "c")
 
 
-def call(kernel, out_shape, scratch=(), in_specs=None, limit=16):
+def call(kernel, out_shape, scratch=(), in_specs=None, limit=20, out_space=pltpu.VMEM, us=2):
     vmem = pl.BlockSpec(memory_space=pltpu.VMEM)
+    out_spec = pl.BlockSpec(memory_space=out_space)
 
     def run(*operands):
         return pl.pallas_call(
             kernel,
             out_shape=out_shape,
             in_specs=in_specs or [vmem] * len(operands),
-            out_specs=jax.tree.map(lambda _: vmem, out_shape),
+            out_specs=jax.tree.map(lambda _: out_spec, out_shape),
             scratch_shapes=list(scratch),
             compiler_params=pltpu.CompilerParams(vmem_limit_bytes=limit * MIB),
+            cost_estimate=pl.CostEstimate(
+                flops=us * 10**9, bytes_accessed=us * 3 * 10**6, transcendentals=0
+            ),
         )(*operands)
 
     return run
@@ -40,6 +44,24 @@
 
 def spec(space):
     return pl.BlockSpec(memory_space=space)
+
+
+SMEM, VMEM, HBM = spec(pltpu.SMEM), spec(pltpu.VMEM), spec(pltpu.HBM)
+
+
+def copier(sems):
+    count = iter(range(100))
+
+    def start(source, target):
+        copy = pltpu.make_async_copy(source, target, sems.at[next(count)])
+        copy.start()
+        return copy
+
+    return start
+
+
+def like(values):
+    return pltpu.VMEM(values.shape, values.dtype)
 
 
 def dot(a, b, dims=((1,), (0,))):
@@ -97,8 +119,8 @@
     lanes = lax.broadcasted_iota(jnp.int32, (1, 128), 1)
     return jnp.where(
         lanes < HEAD // 2,
-        pltpu.roll(values, 128 - HEAD // 2, 1),
-        pltpu.roll(values, HEAD // 2, 1),
+        pltpu.roll(values, 128 - HEAD // 2, values.ndim - 1),
+        pltpu.roll(values, HEAD // 2, values.ndim - 1),
     )
 
 
@@ -141,53 +163,63 @@
 
 
 def prologue_kernel(place, *refs):
-    sources, (modded, part, first_part), held = refs[:4], refs[4:7], refs[7:11]
-    rest, sems = refs[11:]
-    copies = [pltpu.make_async_copy(a, b, sems.at[i]) for i, (a, b) in enumerate(zip(sources, held))]
-    for copy in copies:
-        copy.start()
+    sources, outs, held = refs[:4], refs[4:7], refs[7:11]
+    modded, part, first_part, rest, sems = refs[11:]
+    start = copier(sems)
+    arrivals = [start(a, b) for a, b in zip(sources, held)]
     latents, modulation, qkv, out = held
+    arrivals[0].wait()
+    arrivals[1].wait()
+    normed, _ = normalise(latents[...].astype(F32))
+    modded[...] = (normed * (1.0 + modulation[1, 0:1]) + modulation[0, 0:1]).astype(BF16)
+    finish = [start(modded, outs[0])]
     rest[...] = jnp.zeros_like(rest)
-    copies[0].wait()
-    copies[1].wait()
-    normed, _ = normalise(latents[...].astype(F32))
-    modded[...] = (normed * (1.0 + modulation[0, 1:2]) + modulation[0, 0:1]).astype(BF16)
-    copies[2].wait()
-    copies[3].wait()
+    arrivals[2].wait()
+    arrivals[3].wait()
     for head in range(HEADS):
 
         @pl.when(place[0] == head)
         def _():
             for k in range(3):
-                columns = slice(k * FEATURES + head * HEAD, k * FEATURES + head * HEAD + HEAD)
-                rest[0, :, k * HEAD : k * HEAD + HEAD] = qkv[0, :, columns].astype(F32)
-                rest[1, :, k * HEAD : k * HEAD + HEAD] = qkv[1, :, columns].astype(F32)
+                begin = k * FEATURES + head * HEAD
+                both = qkv[:, :, begin : begin + HEAD].astype(F32)
+                rest[0, :, k * HEAD : k * HEAD + HEAD] = both[:, 0]
+                rest[1, :, k * HEAD : k * HEAD + HEAD] = both[:, 1]
+            main = out[:, :, 128 * head : 128 * head + 128].astype(F32)
+            tail = out[:, :, 1024 + 16 * head : 1040 + 16 * head].astype(F32)
             for block in range(2):
                 rows = slice(18 * block, 18 * block + 18)
-                rest[1, rows, 216:232] = out[block, :, 1024 + 16 * head : 1040 + 16 * head].astype(F32)
-                rest[1, rows, 256:384] = out[block, :, 128 * head : 128 * head + 128].astype(F32)
-
-    lower = place[1] == 0
+                rest[1, rows, 216:232] = tail[:, block]
+                rest[1, rows, 256:384] = main[:, block]
+
     first = rest[0, :, :256].astype(BF16)
     tiles = jnp.concatenate([rest[1, :, 128 * t : 128 * t + 128] for t in range(3)], 0)
-    mine = jnp.where(lower, tiles[:54], tiles[54:])
+    mine = jnp.where(place[1] == 0, tiles[:54], tiles[54:])
     mine = jnp.concatenate([mine, jnp.zeros((2, 128), F32)], 0).astype(BF16)
     for copy in range(32):
         part[copy] = mine
         first_part[copy, :36] = first
+        first_part[copy, 36:] = jnp.zeros((4, 256), BF16)
+    finish += [start(part, outs[1]), start(first_part, outs[2])]
+    for copy in finish:
+        copy.wait()
 
 
 def prologue(place, *operands):
+    outs = (
+        jax.ShapeDtypeStruct((ROWS, WIDTH), BF16),
+        jax.ShapeDtypeStruct((32, 56, 128), BF16),
+        jax.ShapeDtypeStruct((32, 40, 256), BF16),
+    )
     return call(
         prologue_kernel,
-        (
-            jax.ShapeDtypeStruct((ROWS, WIDTH), BF16),
-            jax.ShapeDtypeStruct((32, 56, 128), BF16),
-            jax.ShapeDtypeStruct((32, 40, 256), BF16),
-        ),
-        [pltpu.VMEM(v.shape, v.dtype) for v in operands]
-        + [pltpu.VMEM((2, 36, 384), F32), pltpu.SemaphoreType.DMA((4,))],
-        [spec(pltpu.SMEM)] + [spec(pl.ANY)] * 4,
+        outs,
+        [like(v) for v in operands]
+        + [like(v) for v in outs]
+        + [pltpu.VMEM((2, 36, 384), F32), pltpu.SemaphoreType.DMA((7,))],
+        [SMEM] + [HBM] * 4,
+        limit=60,
+        out_space=pltpu.HBM,
     )(place, *operands)
 
 
@@ -233,8 +265,9 @@
 ):
     for chunk in range(32):
         merged[36 * chunk : 36 * chunk + 36, :] = weight[chunk, :36]
-    sent[:, :, 1024 : 1024 + WIDTH] = latents[...].astype(F32).reshape(16, 8, WIDTH).astype(BF16)
-    sent[:, :, 1024 + WIDTH :] = targets[...].astype(F32).reshape(16, 8, WIDTH).astype(BF16)
+    sent[:, :, 640 : 640 + WIDTH] = latents[...].astype(F32).reshape(16, 8, WIDTH).astype(BF16)
+    sent[:, :, 640 + WIDTH :] = targets[...].astype(F32).reshape(16, 8, WIDTH).astype(BF16)
+    sent[:, :, FEATURES:640] = jnp.zeros((16, 8, 640 - FEATURES), BF16)
     rows = modded[...].reshape(8 * ROWS, WIDTH)
     low = dot(rows, down[0], NT)
     high, rest = halves(low[:, :64] + low[:, 64:])
@@ -248,25 +281,27 @@
         w = softmax(dot(q, k, NT), None)
         weights[frame] = w
         attended = dot(w.astype(BF16), v.astype(BF16)).reshape(16, 8, 128)
-        sent[:, :, 128 * frame : 128 * frame + 128] = attended.astype(BF16)
+        sent[:, :, HEAD * frame : HEAD * frame + HEAD] = attended[:, :, :HEAD].astype(BF16)
 
 
 def spatial(place, *operands):
     return call(
         spatial_kernel,
         (
-            jax.ShapeDtypeStruct((16, 8, 1024 + 2 * WIDTH), BF16),
+            jax.ShapeDtypeStruct((16, 8, 640 + 2 * WIDTH), BF16),
             jax.ShapeDtypeStruct((8 * ROWS, 256), F32),
             jax.ShapeDtypeStruct((8 * ROWS, 128), BF16),
             jax.ShapeDtypeStruct((8, ROWS, ROWS), F32),
         ),
         [pltpu.VMEM((WIDTH, 256), BF16)],
-        [spec(pltpu.SMEM)] + [spec(pltpu.VMEM)] * 6,
-        limit=24,
+        [SMEM] + [VMEM] * 6,
+        us=8,
     )(place, *operands)
 
 
-def spatial_back_kernel(place, cotangent, modded, projected, reduced, weights, up, grad, d_projected):
+def spatial_back_kernel(
+    place, cotangent, up, modded, projected, reduced, weights, grad, d_projected
+):
     for pair in range(4):
         rows = cotangent[:, 16 * pair : 16 * pair + 16, :].astype(F32).reshape(16, 2, 8, 128)
         for side in range(2):
@@ -301,21 +336,24 @@
         ref[:, start + tile, :] = values[:, 128 * tile : 128 * tile + 128]
 
 
-def spatial_back(*operands):
-    vmem = spec(pltpu.VMEM)
+def spatial_back(place, *operands):
     return call(
         spatial_back_kernel,
         jax.ShapeDtypeStruct((RANK, 11, 128), F32),
         [pltpu.VMEM((8 * ROWS, 256), F32)],
-        [spec(pltpu.SMEM)] + [vmem] * 6,
-        limit=24,
-    )(*operands)
-
-
-def assemble(parts, held, sems, qkv, out_first, out_second):
+        [SMEM] + [VMEM] * 6,
+        us=20,
+    )(place, *operands)
+
+
+def part_copies(gathered, held, sems):
+    start = copier(sems)
+    return [start(gathered.at[pl.ds(4 * x, 4)], held.at[pl.ds(4 * x, 4)]) for x in range(4)]
+
+
+def assemble(copies, held, qkv, out_first, out_second):
     for x in range(4):
-        copy = part_copy(parts, held, sems, x)
-        copy.wait()
+        copies[x].wait()
         for c in range(2):
             head = 2 * x + c
             lower, upper = held.at[4 * x + c], held.at[4 * x + 2 + c]
@@ -333,11 +371,6 @@
                 out_second[rows, tail] = upper[d, 0:18, 88:104]
 
 
-def part_copy(parts, held, sems, x):
-    span = pl.ds(4 * x, 4)
-    return pltpu.make_async_copy(parts.at[span], held.at[span], sems.at[x])
-
-
 def by_rows(received, columns):
     values = received[:, :, columns].astype(F32)
     frames = [x * 4 + l * 2 + c for l in range(2) for x in range(4) for c in range(2)]
@@ -347,11 +380,13 @@
 def temporal_kernel(
     received,
     modulation,
-    parts,
+    gathered,
     down,
     up,
     cosine,
     sine,
+    sent_out,
+    grad_out,
     sent,
     grad,
     wide,
@@ -368,25 +403,30 @@
     qkv,
     out_first,
     out_second,
+    d_out,
+    d_v,
+    d_weights,
+    d_scores,
+    d_q,
+    d_k,
     sems,
 ):
-    for x in range(4):
-        part_copy(parts, held, sems, x).start()
+    copies = part_copies(gathered, held, sems)
     for head in range(HEADS):
         x, c = head // 2, head % 2
         rows = jnp.concatenate(
             [
-                received[x * 4 + 2 * l + c, :, 128 * g : 128 * g + 128].astype(F32)
+                received[x * 4 + 2 * l + c, :, HEAD * g : HEAD * g + HEAD].astype(F32)
                 for l in range(2)
                 for g in range(8)
             ],
             0,
         )
-        wide[:, HEAD * head : HEAD * head + HEAD] = rows[:, :HEAD]
-    assemble(parts, held, sems, qkv, out_first, out_second)
+        wide[:, HEAD * head : HEAD * head + HEAD] = rows
+    assemble(copies, held, qkv, out_first, out_second)
     gate_first, gate_second = modulation[0, 2:3], modulation[1, 2:3]
     mixed = dot(wide[...].astype(BF16), out_first[...])
-    middle = (by_rows(received, slice(1024, 1024 + WIDTH)) + gate_first * mixed).astype(BF16).astype(F32)
+    middle = (by_rows(received, slice(640, 640 + WIDTH)) + gate_first * mixed).astype(BF16).astype(F32)
     normed, rate = normalise(middle)
     scale = 1.0 + modulation[1, 1:2]
     modded[...] = (normed * scale + modulation[1, 0:1]).astype(BF16)
@@ -396,35 +436,46 @@
     three = jnp.concatenate([high, high, rest], 1)
     mask = same_token()
     for head in range(HEADS):
-        both = dot(modded[...], qkv[head]) + dot(three, up[1, head])
-        projected[head] = both
-        q, k, v = split_heads(both)
-        q = q * head_rate(q)
-        k = k * head_rate(k)
-        q = (q * cosine[...] + swap(q) * sine[...]).astype(BF16)
-        k = (k * cosine[...] + swap(k) * sine[...]).astype(BF16)
-        v = v.astype(BF16)
-        w = softmax(dot(q, k, NT), mask)
-        q_all[head], k_all[head], v_all[head], weights[head] = q, k, v, w
-        wide[:, HEAD * head : HEAD * head + HEAD] = dot(w.astype(BF16), v)[:, :HEAD]
+        projected[head] = dot(modded[...], qkv[head]) + dot(three, up[1, head])
+    q, k, v = split_heads(projected[...].reshape(HEADS * ROWS, 256))
+    q = (q * head_rate(q)).reshape(HEADS, ROWS, 128)
+    k = (k * head_rate(k)).reshape(HEADS, ROWS, 128)
+    q_all[...] = (q * cosine[...] + swap(q) * sine[...]).astype(BF16)
+    k_all[...] = (k * cosine[...] + swap(k) * sine[...]).astype(BF16)
+    v_all[...] = v.astype(BF16).reshape(HEADS, ROWS, 128)
+    for head in range(HEADS):
+        weights[head] = dot(q_all[head], k_all[head], NT)
+    weights[...] = softmax(weights[...], mask)
+    for head in range(HEADS):
+        wide[:, HEAD * head : HEAD * head + HEAD] = dot(weights[head].astype(BF16), v_all[head])[:, :HEAD]
     mixed = dot(wide[...].astype(BF16), out_second[...])
     produced = (middle + gate_second * mixed).astype(BF16).astype(F32)
-    error = ((produced - by_rows(received, slice(1024 + WIDTH, None))) / WIDTH).astype(BF16).astype(F32)
+    error = ((produced - by_rows(received, slice(640 + WIDTH, None))) / WIDTH).astype(BF16).astype(F32)
     wide[...] = dot((gate_second * error).astype(BF16), out_second[...], NT)
+    for head in range(HEADS):
+        cotangent = wide[:, HEAD * head : HEAD * head + HEAD].astype(BF16)
+        d_out[head] = jnp.concatenate([cotangent, jnp.zeros((ROWS, 128 - HEAD), BF16)], 1)
+    for head in range(HEADS):
+        d_v[head] = dot(weights[head].astype(BF16), d_out[head], TN)
+        d_weights[head] = dot(d_out[head], v_all[head], NT)
+    inner = d_weights[...].astype(BF16).astype(F32)
+    inner = weights[...] * (inner - jnp.sum(inner * weights[...], -1, keepdims=True))
+    d_scores[...] = (inner * SCALE).astype(BF16)
+    for head in range(HEADS):
+        d_q[head] = dot(d_scores[head], k_all[head])
+        d_k[head] = dot(d_scores[head], q_all[head], TN)
+    back = []
+    q, k, _ = split_heads(projected[...].reshape(HEADS * ROWS, 256))
+    for values, ref in ((q, d_q), (k, d_k)):
+        d = ref[...].astype(BF16).astype(F32)
+        d = (d * cosine[...] - swap(d) * sine[...]).reshape(HEADS * ROWS, 128)
+        back.append(head_norm_back(values, d))
+    d_val = d_v[...].astype(BF16).astype(F32).reshape(HEADS * ROWS, 128)
+    d_projected[...] = join_heads(*back, d_val).reshape(HEADS, ROWS, 256)
     d_low = jnp.zeros((ROWS, 128), F32)
     d_modded = jnp.zeros((ROWS, WIDTH), F32)
     for head in range(HEADS):
-        cotangent = wide[:, HEAD * head : HEAD * head + HEAD].astype(BF16)
-        cotangent = jnp.concatenate([cotangent, jnp.zeros((ROWS, 128 - HEAD), BF16)], 1)
-        d_q, d_k, d_v = attention_back(
-            weights[head], q_all[head], k_all[head], v_all[head], cotangent
-        )
-        d_q = d_q * cosine[...] - swap(d_q) * sine[...]
-        d_k = d_k * cosine[...] - swap(d_k) * sine[...]
-        q, k, _ = split_heads(projected[head])
-        joined = join_heads(head_norm_back(q, d_q), head_norm_back(k, d_k), d_v)
-        d_projected[head] = joined
-        high, rest = halves(joined)
+        high, rest = halves(d_projected[head])
         d_low += dot(high, up[1, head, :128], NT) + dot(rest, up[1, head, :128], NT)
         d_modded += dot(high, qkv[head], NT)
     d_low = d_low[:, :64] + d_low[:, 64:]
@@ -443,17 +494,21 @@
         rows = jnp.concatenate([rows, jnp.zeros((ROWS, 128 - HEAD), BF16)], 1)
         sent[x * 4 + c] = rows[:64]
         sent[x * 4 + 2 + c] = rows[64:]
+    start = copier(sems)
+    sent_copy = start(sent, sent_out)
     ups[:, 1664:] = jnp.zeros((64, 128), F32)
     for head in range(HEADS):
         high, rest = halves(d_projected[head])
         both = dot(reduced[...], jnp.concatenate([high, rest], 1), TN)
         part = both[:64, :256] + both[64:, :256] + both[:64, 256:] + both[64:, 256:]
         for k in range(3):
-            start = k * FEATURES + head * HEAD
-            ups[:, start : start + HEAD] = part[:, k * HEAD : k * HEAD + HEAD]
+            begin = k * FEATURES + head * HEAD
+            ups[:, begin : begin + HEAD] = part[:, k * HEAD : k * HEAD + HEAD]
     down = dot(d_reduced, modded[...], TN)
     store_tiles(grad, 0, down[:64] + down[64:])
     store_tiles(grad, 9, ups[...])
+    start(grad, grad_out).wait()
+    sent_copy.wait()
 
 
 def temporal(*operands):
@@ -464,6 +519,8 @@
             jax.ShapeDtypeStruct((RANK, 23, 128), F32),
         ),
         [
+            pltpu.VMEM((16, 64, 128), BF16),
+            pltpu.VMEM((RANK, 23, 128), F32),
             pltpu.VMEM((ROWS, FEATURES), F32),
             pltpu.VMEM((ROWS, WIDTH), BF16),
             pltpu.VMEM((ROWS, 128), BF16),
@@ -478,10 +535,18 @@
             pltpu.VMEM((HEADS, WIDTH, 256), BF16),
             pltpu.VMEM((FEATURES, WIDTH), BF16),
             pltpu.VMEM((FEATURES, WIDTH), BF16),
+            pltpu.VMEM((HEADS, ROWS, 128), BF16),
+            pltpu.VMEM((HEADS, ROWS, 128), F32),
+            pltpu.VMEM((HEADS, ROWS, ROWS), F32),
+            pltpu.VMEM((HEADS, ROWS, ROWS), BF16),
+            pltpu.VMEM((HEADS, ROWS, 128), F32),
+            pltpu.VMEM((HEADS, ROWS, 128), F32),
             pltpu.SemaphoreType.DMA((4,)),
         ],
-        [spec(pltpu.VMEM)] * 2 + [spec(pl.ANY)] + [spec(pltpu.VMEM)] * 4,
-        limit=32,
+        [VMEM] * 2 + [HBM] + [VMEM] * 4,
+        limit=60,
+        out_space=pltpu.HBM,
+        us=25,
     )(*operands)
 
 
@@ -536,9 +601,15 @@
     x, l, c = lax.axis_index("x"), lax.axis_index("l"), lax.axis_index("c")
     place = jnp.stack([x * 2 + c, l, c]).astype(jnp.int32)
     modulation = modulation[0]
-    modded, part, first = prologue(place, latents[0, 0], modulation, qkv, out)
+    modded, part, first = prologue(
+        place,
+        latents[0, 0],
+        modulation.transpose(1, 0, 2),
+        qkv.transpose(1, 0, 2),
+        out.transpose(1, 0, 2),
+    )
     modded = lax.all_gather(modded, ("x", "c"), axis=0, tiled=False)
-    parts = lax.all_gather(exchange(part, DP), SEQ, axis=0, tiled=False)
+    gathered = lax.all_gather(exchange(part, DP), SEQ, axis=0, tiled=False)
     first = exchange(first, DP)
     down_parts, up_parts = adapters(down.transpose(0, 2, 1), up)
     sent, projected, reduced, weights = spatial(
@@ -549,7 +620,7 @@
     sent, late = temporal(
         received,
         modulation,
-        parts,
+        gathered,
         down_parts,
         up_parts,
         jnp.asarray(cosine),
@@ -557,7 +628,7 @@
     )
     cotangent = exchange(sent, SEQ)
     late = sum(add_cores(late, c))
-    early = spatial_back(place, cotangent, modded, projected, reduced, weights, up_parts)
+    early = spatial_back(place, cotangent, up_parts, modded, projected, reduced, weights)
     mine, other = add_cores(early, c)
     first_up, second_up = mine[:, 9:], other[:, 9:]
     total = jnp.concatenate(

time: 254 us -> 243 us (0.957)
  local copies, waits for them, and re-layouts: 23.7 us -> 13.3 us
    unnamed x45 -> x39, local copies, waits for them, and re-layouts: 22 us -> 10.2 us
  transfers between devices with their start and end apart: 7 -> 7, of which waited for: 4 -> 3; matrix products, arithmetic and copies ran while one was open for 0% -> 1% of each run, Pallas kernels for 5% -> 6%
where the time goes in v3:
time: 243 us; the launch traced here: 242 us
  blocking collectives  124 us (51%)
  Pallas kernels  41 us (17%)
  waiting for transfers between devices  24.2 us (10%)
  starting transfers between devices  23.2 us (10%)
  between operations  14.4 us (6%)
  local copies, waits for them, and re-layouts  13.3 us (5%)
    all_to_all x5, blocking collectives, exchange(): return lax.all_to_all(values, axes, 0, 0)  124 us
    pallas_call x6, Pallas kernels, run(): pl.pallas_call(kernel, out_shape=out_shape, in_specs=in_specs or [vmem] *...  41 us
    all_to_all x2, waiting for transfers between devices, exchange(): return lax.all_to_all(values, axes, 0, 0)  22.2 us
    ppermute x3, starting transfers between devices, swap_cores(): return lax.ppermute(values, 'c', [(0, 1), (1, 0)])  12.4 us
    all_to_all x2, starting transfers between devices, exchange(): return lax.all_to_all(values, axes, 0, 0)  10.7 us
    unnamed x39, local copies, waits for them, and re-layouts  10.2 us
  transfers between devices with their start and end apart: 7, of which 3 were waited for; matrix products, arithmetic and copies ran while one was open for 1% of the time, Pallas kernels for 6%

profile of v3, /device:TPU:1, one launch (start us, length us, event | category | flops | bytes accessed | tf_op | source)
XLA Modules:
  0.0 242.1 jit_solution(3555585065972798215)
XLA Ops:
  7.2 0.0 all-gather.5.cloned.1.call-start
  7.2 0.8 copy.35
  8.0 0.6 copy.28.refs_1_
  8.6 0.7 pad_add_fusion.place
  9.3 3.3 %shard_map.104 = (bf16[128,1152]{1,0:T(8,128)(2,1)}, bf16[32,56,128]{2,1,0:T(8,128)(2,1)}, bf16[32,40,256]{2,1,0:T(8,128)(2,1)}) custom-call(s32[3]{0:T(128)} %pad_add_fusion.place, bf16[128,1152]{1,0:T(8,128)(2,1)} %bitcast.24, f32[3,2,1152]{2,1,0:T(2,128)} %copy.28.refs_1_, bf16[36,2,1728]{2,1,0:T(2,128)(2,1)} %bitcast.36, bf16[18,2,1152]{2,1,0:T(2,128)(2,1)} %bitcast.37), custom_call_target="tpu_custom_call" | custom-call | flops 2000000000 | bytes 6000000 | tf_op jit(solution)/shard_map/pallas_call | solution.py:30
  12.6 0.0 copy-start.3
  12.6 0.0 copy-start.4
  12.6 0.0 all-gather.5.cloned.1.call-update
  12.6 0.0 all-gather.7.cloned.1.call-start
  12.7 33.5 %all_to_all.35 = bf16[32,56,128]{2,1,0:T(8,128)(2,1)} all-to-all(bf16[32,56,128]{2,1,0:T(8,128)(2,1)} %get-tuple-element.20), channel_id=1, replica_groups=mesh['z'=8,'h'=4,'x'=4,'l'=2,'c'=2] {'z','h'}, dimensions={0} | all-to-all | bytes 917504 | tf_op jit(solution)/shard_map/all_to_all | solution.py:584
  46.2 0.0 all-gather.7.cloned.1.call-update
  46.2 6.5 %all-to-all-start = ((bf16[32,40,256]{2,1,0:T(8,128)(2,1)}), bf16[32,40,256]{2,1,0:T(8,128)(2,1)S(1)}, u32[]{:S(2)}, u32[]{:S(2)}) async-start(bf16[32,40,256]{2,1,0:T(8,128)(2,1)} %get-tuple-element.16), calls=%async_computation | async-start | bytes 1310720 | tf_op jit(solution)/shard_map/all_to_all | solution.py:584
  52.7 0.0 copy-done.3
  52.7 0.0 copy-start.5
  52.7 0.0 copy-start.6
  52.7 1.7 shard_map.105
  54.5 1.1 copy-done.7
  55.6 18.9 %all-to-all-done.weight = bf16[32,40,256]{2,1,0:T(8,128)(2,1)S(1)} async-done(((bf16[32,40,256]{2,1,0:T(8,128)(2,1)}), bf16[32,40,256]{2,1,0:T(8,128)(2,1)S(1)}, u32[]{:S(2)}, u32[]{:S(2)}) %all-to-all-start) | async-done | bytes 655392 | tf_op jit(solution)/shard_map/all_to_all | solution.py:584
  74.5 1.7 copy-done.1
  76.3 1.5 copy-done.8
  77.7 6.1 %shard_map.106 = (bf16[16,8,2944]{2,1,0:T(8,128)(2,1)S(1)}, f32[1024,256]{1,0:T(8,128)S(1)}, bf16[1024,128]{1,0:T(8,128)(2,1)S(1)}, f32[8,128,128]{2,1,0:T(8,128)S(1)}) custom-call(s32[3]{0:T(128)S(1)} %copy-done, bf16[8,128,1152]{2,1,0:T(8,128)(2,1)S(1)} %bitcast.21, bf16[32,40,256]{2,1,0:T(8,128)(2,1)S(1)} %all-to-all-done.weight, ...), custom_call_target="tpu_custom_call" | custom-call | flops 8000000000 | bytes 24000000 | tf_op jit(solution)/shard_map/pallas_call | solution.py:30
  83.8 1.0 copy-done.11
  84.8 0.8 copy-done.13
  85.6 0.7 copy-done.15
  86.3 27.7 %all_to_all.36.received = bf16[16,8,2944]{2,1,0:T(8,128)(2,1)} all-to-all(bf16[16,8,2944]{2,1,0:T(8,128)(2,1)S(1)} %get-tuple-element.19), channel_id=1, replica_groups=mesh['z'=8,'h'=4,'x'=4,'l'=2,'c'=2] {'x','l','c'}, dimensions={0} | all-to-all | bytes 1507328 | tf_op jit(solution)/shard_map/all_to_all | solution.py:584
  114.0 21.5 %shard_map.107 = (bf16[16,64,128]{2,1,0:T(8,128)(2,1)}, f32[64,23,128]{2,1,0:T(8,128)}) custom-call(bf16[16,8,2944]{2,1,0:T(8,128)(2,1)} %all_to_all.36.received, f32[2,3,1152]{2,1,0:T(4,128)} %bitcast.33, bf16[16,32,56,128]{3,2,1,0:T(8,128)(2,1)} %bitcast.35, bf16[2,128,1152]{2,1,0:T(8,128)(2,1)} %copy-done.10, bf16[2,8,192,256]{3,2,1,0:T(8,128)(2,1)} %copy-done.7, ...), custom_call_target="tpu_custom_call" | custom-call | flops 24999999488 | bytes 75000000 | tf_op jit(solution)/shard_map/pallas_call | solution.py:30
  135.5 4.2 %all-to-all-start.3 = ((bf16[16,64,128]{2,1,0:T(8,128)(2,1)}), bf16[16,64,128]{2,1,0:T(8,128)(2,1)S(1)}, u32[]{:S(2)}, u32[]{:S(2)}) async-start(bf16[16,64,128]{2,1,0:T(8,128)(2,1)} %get-tuple-element.21), calls=%async_computation.3 | async-start | bytes 524288 | tf_op jit(solution)/shard_map/all_to_all | solution.py:584
  139.7 1.8 constant_dynamic-slice_fusion
  141.4 2.1 collective-permute-start.1
  143.6 3.3 %all-to-all-done.3.cotangent = bf16[16,64,128]{2,1,0:T(8,128)(2,1)S(1)} async-done(((bf16[16,64,128]{2,1,0:T(8,128)(2,1)}), bf16[16,64,128]{2,1,0:T(8,128)(2,1)S(1)}, u32[]{:S(2)}, u32[]{:S(2)}) %all-to-all-start.3) | async-done | bytes 262176 | tf_op jit(solution)/shard_map/all_to_all | solution.py:584
  146.9 1.4 copy-done.9
  148.3 1.2 copy-done.12
  149.6 6.1 %shard_map.108 = f32[64,11,128]{2,1,0:T(8,128)S(1)} custom-call(s32[3]{0:T(128)S(1)} %copy-done, bf16[16,64,128]{2,1,0:T(8,128)(2,1)S(1)} %all-to-all-done.3.cotangent, bf16[2,8,192,256]{3,2,1,0:T(8,128)(2,1)S(1)} %copy-done.9, bf16[8,128,1152]{2,1,0:T(8,128)(2,1)S(1)} %bitcast.22, f32[1024,256]{1,0:T(8,128)S(1)} %copy-done.12, ...), custom_call_target="tpu_custom_call" | custom-call | flops 20000000000 | bytes 60000000 | tf_op jit(solution)/shard_map/pallas_call | solution.py:30
  155.7 2.9 %collective-permute-start = (f32[32,11,128]{2,1,0:T(8,128)S(1)}, f32[32,11,128]{2,1,0:T(8,128)S(1)}, u32[]{:S(2)}, u32[]{:S(2)}) collective-permute-start(f32[32,11,128]{2,1,0:T(8,128)S(1)} %constant_dynamic-slice_fusion.1), channel_id=1, source_target_pairs={{0,1},{1,0},{2,3},{3,2},{4,5},{5,4},{6,7},{7,6},{8,9},{9,8},{10,11... | collective-permute-start | bytes 540680 | tf_op jit(solution)/shard_map/ppermute | solution.py:592
  158.6 0.0 collective-permute-done.1
  158.6 1.1 dynamic-slice_add_fusion
  159.7 0.0 collective-permute-done
  159.8 0.1 pad_maximum_fusion
  159.9 0.1 copy.29
  160.0 0.4 copy.30
  160.4 25.1 %all_to_all.37 = f32[32,9,4,128]{3,2,1,0:T(4,128)S(1)} all-to-all(f32[32,9,4,128]{3,2,1,0:T(4,128)S(1)} %copy.30), channel_id=1, replica_groups=mesh['z'=8,'h'=4,'x'=4,'l'=2,'c'=2] {'z','x'}, dimensions={0} | all-to-all | bytes 1179648 | tf_op jit(solution)/shard_map/all_to_all | solution.py:584
  185.5 0.1 copy.31
  185.8 14.1 %all_to_all.38 = f32[8,48,128]{2,1,0:T(8,128)S(1)} all-to-all(f32[8,48,128]{2,1,0:T(8,128)S(1)} %broadcast_in_dim.4), channel_id=1, replica_groups=mesh['z'=8,'h'=4,'x'=4,'l'=2,'c'=2] {'h','l'}, dimensions={0} | all-to-all | bytes 393216 | tf_op jit(solution)/shard_map/all_to_all | solution.py:584
  199.9 0.1 broadcast_in_dim.5
  199.9 23.6 %all_to_all.39.own = f32[32,48,128]{2,1,0:T(8,128)S(1)} all-to-all(f32[32,48,128]{2,1,0:T(8,128)S(1)} %broadcast_in_dim.5), channel_id=1, replica_groups=mesh['z'=8,'h'=4,'x'=4,'l'=2,'c'=2] {'z','x'}, dimensions={0} | all-to-all | bytes 1572864 | tf_op jit(solution)/shard_map/all_to_all | solution.py:584
  223.6 7.4 %collective-permute-start.2 = (f32[32,48,128]{2,1,0:T(8,128)S(1)}, f32[32,48,128]{2,1,0:T(8,128)S(1)}, u32[]{:S(2)}, u32[]{:S(2)}) collective-permute-start(f32[32,48,128]{2,1,0:T(8,128)S(1)} %all_to_all.39.own), channel_id=1, source_target_pairs={{0,1},{1,0},{2,3},{3,2},{4,5},{5,4},{6,7},{7,6},{8,9},{9,8},{10,11... | collective-permute-start | bytes 2359304 | tf_op jit(solution)/shard_map/ppermute | solution.py:592
  231.0 1.9 collective-permute-done.2.other
  232.9 2.4 shard_map.109
  (38 shorter events, 0.3 us)
Async XLA Ops:
  7.2 67.4 %all-gather.5.cloned.1.call-start = ((), (), s32[]{:S(2)}) async-start(), calls=%async_computation.7 | async-start | bytes 2654208 | tf_op jit(solution)/shard_map/all_gather | solution.py:611
  8.0 4.6 %copy-start.18 = (f32[1,2,3,1152]{3,2,1,0:T(4,128)}, f32[1,2,3,1152]{3,2,1,0:T(4,128)S(1)}, u32[]{:S(2)}) copy-start(f32[1,2,3,1152]{3,2,1,0:T(4,128)S(1)} %copy.35) | copy-start | bytes 82948
  12.6 40.1 %copy-start.3 = (f32[2,64,1728]{2,1,0:T(8,128)S(1)}, f32[2,64,1728]{2,1,0:T(8,128)}, u32[]{:S(2)}) copy-start(f32[2,64,1728]{2,1,0:T(8,128)} %up.1) | copy-start | bytes 2654212
  12.6 40.1 %copy-start.4 = (f32[2,1152,64]{1,2,0:T(8,128)S(1)}, f32[2,1152,64]{1,2,0:T(8,128)}, u32[]{:S(2)}) copy-start(f32[2,1152,64]{1,2,0:T(8,128)} %param.14) | copy-start | bytes 1769476
  12.6 101.3 %all-gather.7.cloned.1.call-start = ((), (), s32[]{:S(2)}) async-start(), calls=%async_computation.8 | async-start | bytes 7798784 | tf_op jit(solution)/shard_map/all_gather | solution.py:612
  46.2 28.3 %all-to-all-start = ((bf16[32,40,256]{2,1,0:T(8,128)(2,1)}), bf16[32,40,256]{2,1,0:T(8,128)(2,1)S(1)}, u32[]{:S(2)}, u32[]{:S(2)}) async-start(bf16[32,40,256]{2,1,0:T(8,128)(2,1)} %get-tuple-element.16), calls=%async_computation | async-start | bytes 1310720 | tf_op jit(solution)/shard_map/all_to_all | solution.py:584
  52.7 21.8 %copy-start = (s32[3]{0:T(128)S(1)}, s32[3]{0:T(128)}, u32[]{:S(2)}) copy-start(s32[3]{0:T(128)} %pad_add_fusion.place) | copy-start | bytes 40
  52.7 21.8 %copy-start.5 = (bf16[1,1,128,1152]{3,2,1,0:T(8,128)(2,1)S(1)}, bf16[1,1,128,1152]{3,2,1,0:T(8,128)(2,1)}, u32[]{:S(2)}) copy-start(bf16[1,1,128,1152]{3,2,1,0:T(8,128)(2,1)} %param.9) | copy-start | bytes 884740
  52.7 21.8 %copy-start.6 = (bf16[1,1,128,1152]{3,2,1,0:T(8,128)(2,1)S(1)}, bf16[1,1,128,1152]{3,2,1,0:T(8,128)(2,1)}, u32[]{:S(2)}) copy-start(bf16[1,1,128,1152]{3,2,1,0:T(8,128)(2,1)} %param.10) | copy-start | bytes 884740
  54.5 1.1 copy-start.7
  55.6 28.2 %copy-start.10 = (bf16[2,128,1152]{2,1,0:T(8,128)(2,1)}, bf16[2,128,1152]{2,1,0:T(8,128)(2,1)S(1)}, u32[]{:S(2)}) copy-start(bf16[2,128,1152]{2,1,0:T(8,128)(2,1)S(1)} %get-tuple-element.17.down) | copy-start | bytes 1769476
  74.5 1.7 copy-start.1
  76.3 1.5 copy-start.8
  83.8 1.0 copy-start.11
  84.8 0.8 copy-start.13
  85.6 0.7 copy-start.15
  114.0 32.9 %copy-start.2 = (bf16[1024,1152]{1,0:T(8,128)(2,1)S(1)}, bf16[1024,1152]{1,0:T(8,128)(2,1)}, u32[]{:S(2)}) copy-start(bf16[1024,1152]{1,0:T(8,128)(2,1)} %all-gather.5.cloned.1.call-done) | copy-start | bytes 7077892
  114.0 32.9 %copy-start.14 = (f32[8,128,128]{2,1,0:T(8,128)S(1)}, f32[8,128,128]{2,1,0:T(8,128)}, u32[]{:S(2)}) copy-start(f32[8,128,128]{2,1,0:T(8,128)} %copy-done.13) | copy-start | bytes 1572868
  114.0 32.9 %copy-start.16 = (bf16[1024,128]{1,0:T(8,128)(2,1)S(1)}, bf16[1024,128]{1,0:T(8,128)(2,1)}, u32[]{:S(2)}) copy-start(bf16[1024,128]{1,0:T(8,128)(2,1)} %copy-done.15) | copy-start | bytes 786436
  135.5 11.4 %all-to-all-start.3 = ((bf16[16,64,128]{2,1,0:T(8,128)(2,1)}), bf16[16,64,128]{2,1,0:T(8,128)(2,1)S(1)}, u32[]{:S(2)}, u32[]{:S(2)}) async-start(bf16[16,64,128]{2,1,0:T(8,128)(2,1)} %get-tuple-element.21), calls=%async_computation.3 | async-start | bytes 524288 | tf_op jit(solution)/shard_map/all_to_all | solution.py:584
  141.4 17.1 %collective-permute-start.1 = (f32[32,23,128]{2,1,0:T(8,128)}, f32[32,23,128]{2,1,0:T(8,128)}, u32[]{:S(2)}, u32[]{:S(2)}) collective-permute-start(f32[32,23,128]{2,1,0:T(8,128)} %constant_dynamic-slice_fusion), channel_id=1, source_target_pairs={{0,1},{1,0},{2,3},{3,2},{4,5},{5,4},{6,7},{7,6},{8,9},{9,8},{10,11... | collective-permute-start | bytes 1130504 | tf_op jit(solution)/shard_map/ppermute | solution.py:592
  146.9 1.4 copy-start.9
  148.3 1.2 copy-start.12
  149.6 9.0 %copy-start.17 = (f32[64,23,128]{2,1,0:T(8,128)S(1)}, f32[64,23,128]{2,1,0:T(8,128)}, u32[]{:S(2)}) copy-start(f32[64,23,128]{2,1,0:T(8,128)} %get-tuple-element.25) | copy-start | bytes 2260996
  155.7 4.1 %collective-permute-start = (f32[32,11,128]{2,1,0:T(8,128)S(1)}, f32[32,11,128]{2,1,0:T(8,128)S(1)}, u32[]{:S(2)}, u32[]{:S(2)}) collective-permute-start(f32[32,11,128]{2,1,0:T(8,128)S(1)} %constant_dynamic-slice_fusion.1), channel_id=1, source_target_pairs={{0,1},{1,0},{2,3},{3,2},{4,5},{5,4},{6,7},{7,6},{8,9},{9,8},{10,11... | collective-permute-start | bytes 540680 | tf_op jit(solution)/shard_map/ppermute | solution.py:592
  223.6 9.3 %collective-permute-start.2 = (f32[32,48,128]{2,1,0:T(8,128)S(1)}, f32[32,48,128]{2,1,0:T(8,128)S(1)}, u32[]{:S(2)}, u32[]{:S(2)}) collective-permute-start(f32[32,48,128]{2,1,0:T(8,128)S(1)} %all_to_all.39.own), channel_id=1, source_target_pairs={{0,1},{1,0},{2,3},{3,2},{4,5},{5,4},{6,7},{7,6},{8,9},{9,8},{10,11... | collective-permute-start | bytes 2359304 | tf_op jit(solution)/shard_map/ppermute | solution.py:592
Sparse Core Ops, SparseCore 0:
  12.7 36.8 all-gather.4
  51.7 61.6 all-gather.6

commit v4 on v3

--- a/solution.py
+++ b/solution.py
@@ -192,14 +192,13 @@
                 rest[1, rows, 216:232] = tail[:, block]
                 rest[1, rows, 256:384] = main[:, block]
 
-    first = rest[0, :, :256].astype(BF16)
+    first = jnp.concatenate([rest[0, :, :128], rest[0, :, 128:256]], 0).astype(BF16)
     tiles = jnp.concatenate([rest[1, :, 128 * t : 128 * t + 128] for t in range(3)], 0)
     mine = jnp.where(place[1] == 0, tiles[:54], tiles[54:])
     mine = jnp.concatenate([mine, jnp.zeros((2, 128), F32)], 0).astype(BF16)
     for copy in range(32):
         part[copy] = mine
-        first_part[copy, :36] = first
-        first_part[copy, 36:] = jnp.zeros((4, 256), BF16)
+        first_part[copy] = first
     finish += [start(part, outs[1]), start(first_part, outs[2])]
     for copy in finish:
         copy.wait()
@@ -209,7 +208,7 @@
     outs = (
         jax.ShapeDtypeStruct((ROWS, WIDTH), BF16),
         jax.ShapeDtypeStruct((32, 56, 128), BF16),
-        jax.ShapeDtypeStruct((32, 40, 256), BF16),
+        jax.ShapeDtypeStruct((32, 72, 128), BF16),
     )
     return call(
         prologue_kernel,
@@ -223,34 +222,41 @@
     )(place, *operands)
 
 
-def adapters_kernel(down, up, down_parts, up_parts):
+def adapters_kernel(place, down, up, down_first, down_second, up_first, up_second, held):
     for block in range(2):
         high, low = halves(down[block])
-        down_parts[block, :64] = high
-        down_parts[block, 64:] = low
+        down_parts = down_second if block else down_first
+        down_parts[:64] = high
+        down_parts[64:] = low
         for head in range(HEADS):
             start = head * HEAD
             columns = [up[block, :, k * FEATURES + start : k * FEATURES + start + HEAD] for k in range(3)]
             zero = jnp.zeros((RANK, 128 - HEAD), F32)
             wide = join_heads(*[jnp.concatenate([part, zero], 1) for part in columns])
             high, low = halves(wide)
-            up_parts[block, head, :64] = high
-            up_parts[block, head, 64:128] = low
-            up_parts[block, head, 128:] = high
-
-
-def adapters(down, up):
+            parts = jnp.concatenate([high, low, high], 0)
+            if block == 0:
+                held[head] = parts
+            else:
+                up_second[head] = parts
+    up_first[...] = held[place[0]]
+
+
+def adapters(place, down, up):
     return call(
         adapters_kernel,
         (
-            jax.ShapeDtypeStruct((2, 128, WIDTH), BF16),
-            jax.ShapeDtypeStruct((2, HEADS, 192, 256), BF16),
+            jax.ShapeDtypeStruct((128, WIDTH), BF16),
+            jax.ShapeDtypeStruct((128, WIDTH), BF16),
+            jax.ShapeDtypeStruct((192, 256), BF16),
+            jax.ShapeDtypeStruct((HEADS, 192, 256), BF16),
         ),
-    )(down, up)
+        [pltpu.VMEM((HEADS, 192, 256), BF16)],
+        [SMEM, VMEM, VMEM],
+    )(place, down, up)
 
 
 def spatial_kernel(
-    place,
     modded,
     weight,
     down,
@@ -264,15 +270,17 @@
     merged,
 ):
     for chunk in range(32):
-        merged[36 * chunk : 36 * chunk + 36, :] = weight[chunk, :36]
+        rows = slice(36 * chunk, 36 * chunk + 36)
+        merged[rows, :128] = weight[chunk, :36]
+        merged[rows, 128:] = weight[chunk, 36:]
     sent[:, :, 640 : 640 + WIDTH] = latents[...].astype(F32).reshape(16, 8, WIDTH).astype(BF16)
     sent[:, :, 640 + WIDTH :] = targets[...].astype(F32).reshape(16, 8, WIDTH).astype(BF16)
     sent[:, :, FEATURES:640] = jnp.zeros((16, 8, 640 - FEATURES), BF16)
     rows = modded[...].reshape(8 * ROWS, WIDTH)
-    low = dot(rows, down[0], NT)
+    low = dot(rows, down[...], NT)
     high, rest = halves(low[:, :64] + low[:, 64:])
     reduced[...] = jnp.concatenate([high, rest], 1)
-    adapted = dot(jnp.concatenate([high, high, rest], 1), up[0, place[0]])
+    adapted = dot(jnp.concatenate([high, high, rest], 1), up[...])
     projected[...] = dot(rows, merged[...]) + adapted
     for frame in range(8):
         q, k, v = split_heads(projected[frame * ROWS : frame * ROWS + ROWS])
@@ -284,7 +292,7 @@
         sent[:, :, HEAD * frame : HEAD * frame + HEAD] = attended[:, :, :HEAD].astype(BF16)
 
 
-def spatial(place, *operands):
+def spatial(*operands):
     return call(
         spatial_kernel,
         (
@@ -294,13 +302,12 @@
             jax.ShapeDtypeStruct((8, ROWS, ROWS), F32),
         ),
         [pltpu.VMEM((WIDTH, 256), BF16)],
-        [SMEM] + [VMEM] * 6,
         us=8,
-    )(place, *operands)
+    )(*operands)
 
 
 def spatial_back_kernel(
-    place, cotangent, up, modded, projected, reduced, weights, grad, d_projected
+    cotangent, up, modded, projected, reduced, weights, grad, d_projected
 ):
     for pair in range(4):
         rows = cotangent[:, 16 * pair : 16 * pair + 16, :].astype(F32).reshape(16, 2, 8, 128)
@@ -321,7 +328,7 @@
     high, rest = halves(d_projected[...])
     both = dot(reduced[...], jnp.concatenate([high, rest], 1), TN)
     grad_up = both[:64, :256] + both[64:, :256] + both[:64, 256:] + both[64:, 256:]
-    head = up[0, place[0], :128]
+    head = up[:128]
     two = dot(high, head, NT) + dot(rest, head, NT)
     low_high, low_rest = halves(two[:, :64] + two[:, 64:])
     down = dot(
@@ -336,18 +343,16 @@
         ref[:, start + tile, :] = values[:, 128 * tile : 128 * tile + 128]
 
 
-def spatial_back(place, *operands):
+def spatial_back(*operands):
     return call(
         spatial_back_kernel,
         jax.ShapeDtypeStruct((RANK, 11, 128), F32),
         [pltpu.VMEM((8 * ROWS, 256), F32)],
-        [SMEM] + [VMEM] * 6,
         us=20,
-    )(place, *operands)
-
-
-def part_copies(gathered, held, sems):
-    start = copier(sems)
+    )(*operands)
+
+
+def part_copies(gathered, held, start):
     return [start(gathered.at[pl.ds(4 * x, 4)], held.at[pl.ds(4 * x, 4)]) for x in range(4)]
 
 
@@ -378,15 +383,21 @@
 
 
 def temporal_kernel(
+    gathered,
+    received_in,
+    modulation_in,
+    down_in,
+    up_in,
+    cosine_in,
+    sine_in,
+    sent_out,
+    grad_out,
     received,
     modulation,
-    gathered,
     down,
     up,
     cosine,
     sine,
-    sent_out,
-    grad_out,
     sent,
     grad,
     wide,
@@ -411,7 +422,19 @@
     d_k,
     sems,
 ):
-    copies = part_copies(gathered, held, sems)
+    start = copier(sems)
+    copies = part_copies(gathered, held, start)
+    arrivals = [
+        start(received_in, received),
+        start(modulation_in, modulation),
+        start(down_in, down),
+        start(up_in, up),
+        start(cosine_in, cosine),
+        start(sine_in, sine),
+    ]
+    assemble(copies, held, qkv, out_first, out_second)
+    for copy in arrivals:
+        copy.wait()
     for head in range(HEADS):
         x, c = head // 2, head % 2
         rows = jnp.concatenate(
@@ -423,20 +446,19 @@
             0,
         )
         wide[:, HEAD * head : HEAD * head + HEAD] = rows
-    assemble(copies, held, qkv, out_first, out_second)
-    gate_first, gate_second = modulation[0, 2:3], modulation[1, 2:3]
+    gate_first, gate_second = modulation[2, 0:1], modulation[2, 1:2]
     mixed = dot(wide[...].astype(BF16), out_first[...])
     middle = (by_rows(received, slice(640, 640 + WIDTH)) + gate_first * mixed).astype(BF16).astype(F32)
     normed, rate = normalise(middle)
     scale = 1.0 + modulation[1, 1:2]
-    modded[...] = (normed * scale + modulation[1, 0:1]).astype(BF16)
-    low = dot(modded[...], down[1], NT)
+    modded[...] = (normed * scale + modulation[0, 1:2]).astype(BF16)
+    low = dot(modded[...], down[...], NT)
     high, rest = halves(low[:, :64] + low[:, 64:])
     reduced[...] = jnp.concatenate([high, rest], 1)
     three = jnp.concatenate([high, high, rest], 1)
     mask = same_token()
     for head in range(HEADS):
-        projected[head] = dot(modded[...], qkv[head]) + dot(three, up[1, head])
+        projected[head] = dot(modded[...], qkv[head]) + dot(three, up[head])
     q, k, v = split_heads(projected[...].reshape(HEADS * ROWS, 256))
     q = (q * head_rate(q)).reshape(HEADS, ROWS, 128)
     k = (k * head_rate(k)).reshape(HEADS, ROWS, 128)
@@ -476,12 +498,12 @@
     d_modded = jnp.zeros((ROWS, WIDTH), F32)
     for head in range(HEADS):
         high, rest = halves(d_projected[head])
-        d_low += dot(high, up[1, head, :128], NT) + dot(rest, up[1, head, :128], NT)
+        d_low += dot(high, up[head, :128], NT) + dot(rest, up[head, :128], NT)
         d_modded += dot(high, qkv[head], NT)
     d_low = d_low[:, :64] + d_low[:, 64:]
     high, rest = halves(d_low)
     d_reduced = jnp.concatenate([high, rest], 1)
-    through = dot(jnp.concatenate([high, high], 1), down[1]) + dot(rest, down[1, :64])
+    through = dot(jnp.concatenate([high, high], 1), down[...]) + dot(rest, down[:64])
     d_modded = (d_modded.astype(BF16) + through.astype(BF16)).astype(F32)
     d_normed = d_modded * scale
     inner = jnp.mean(d_normed * normed, -1, keepdims=True)
@@ -494,7 +516,6 @@
         rows = jnp.concatenate([rows, jnp.zeros((ROWS, 128 - HEAD), BF16)], 1)
         sent[x * 4 + c] = rows[:64]
         sent[x * 4 + 2 + c] = rows[64:]
-    start = copier(sems)
     sent_copy = start(sent, sent_out)
     ups[:, 1664:] = jnp.zeros((64, 128), F32)
     for head in range(HEADS):
@@ -511,14 +532,15 @@
     sent_copy.wait()
 
 
-def temporal(*operands):
+def temporal(gathered, *operands):
     return call(
         temporal_kernel,
         (
             jax.ShapeDtypeStruct((16, 64, 128), BF16),
             jax.ShapeDtypeStruct((RANK, 23, 128), F32),
         ),
-        [
+        [like(v) for v in operands]
+        + [
             pltpu.VMEM((16, 64, 128), BF16),
             pltpu.VMEM((RANK, 23, 128), F32),
             pltpu.VMEM((ROWS, FEATURES), F32),
@@ -541,13 +563,13 @@
             pltpu.VMEM((HEADS, ROWS, ROWS), BF16),
             pltpu.VMEM((HEADS, ROWS, 128), F32),
             pltpu.VMEM((HEADS, ROWS, 128), F32),
-            pltpu.SemaphoreType.DMA((4,)),
+            pltpu.SemaphoreType.DMA((12,)),
         ],
-        [VMEM] * 2 + [HBM] + [VMEM] * 4,
+        [HBM] * 7,
         limit=60,
         out_space=pltpu.HBM,
         us=25,
-    )(*operands)
+    )(gathered, *operands)
 
 
 def epilogue_kernel(place, own, other, grad_down, grad_up):
@@ -600,35 +622,35 @@
 def on_device(latents, targets, modulation, qkv, out, down, up):
     x, l, c = lax.axis_index("x"), lax.axis_index("l"), lax.axis_index("c")
     place = jnp.stack([x * 2 + c, l, c]).astype(jnp.int32)
-    modulation = modulation[0]
+    modulation = modulation[0].transpose(1, 0, 2)
     modded, part, first = prologue(
         place,
         latents[0, 0],
-        modulation.transpose(1, 0, 2),
+        modulation,
         qkv.transpose(1, 0, 2),
         out.transpose(1, 0, 2),
     )
     modded = lax.all_gather(modded, ("x", "c"), axis=0, tiled=False)
     gathered = lax.all_gather(exchange(part, DP), SEQ, axis=0, tiled=False)
     first = exchange(first, DP)
-    down_parts, up_parts = adapters(down.transpose(0, 2, 1), up)
+    down_first, down_second, up_first, up_second = adapters(place, down.transpose(0, 2, 1), up)
     sent, projected, reduced, weights = spatial(
-        place, modded, first, down_parts, up_parts, latents[0, 0], targets[0, 0]
+        modded, first, down_first, up_first, latents[0, 0], targets[0, 0]
     )
     received = exchange(sent, SEQ)
     cosine, sine = rotation_tables()
     sent, late = temporal(
+        gathered,
         received,
         modulation,
-        gathered,
-        down_parts,
-        up_parts,
+        down_second,
+        up_second,
         jnp.asarray(cosine),
         jnp.asarray(sine),
     )
     cotangent = exchange(sent, SEQ)
     late = sum(add_cores(late, c))
-    early = spatial_back(place, cotangent, up_parts, modded, projected, reduced, weights)
+    early = spatial_back(cotangent, up_first, modded, projected, reduced, weights)
     mine, other = add_cores(early, c)
     first_up, second_up = mine[:, 9:], other[:, 9:]
     total = jnp.concatenate(

time: 243 us -> 240 us (0.988)
  local copies, waits for them, and re-layouts: 13.3 us -> 9.81 us
    all_gather x1, waiting for transfers between devices: 0.01 us -> 2.97 us  [on_device(): gathered = lax.all_gather(exchange(part, DP), SEQ, axis=0, tiled=False)]
    unnamed x39 -> x28, local copies, waits for them, and re-layouts: 10.2 us -> 7.38 us
  transfers between devices with their start and end apart: 7 -> 7, of which waited for: 3 -> 5; matrix products, arithmetic and copies ran while one was open for 1% -> 1% of each run, Pallas kernels for 6% -> 6%
where the time goes in v4:
time: 240 us; the launch traced here: 239 us
  blocking collectives  124 us (52%)
  Pallas kernels  39.7 us (17%)
  waiting for transfers between devices  25 us (10%)
  starting transfers between devices  24 us (10%)
  between operations  14.3 us (6%)
  local copies, waits for them, and re-layouts  9.81 us (4%)
    all_to_all x5, blocking collectives, exchange(): return lax.all_to_all(values, axes, 0, 0)  124 us
    pallas_call x6, Pallas kernels, run(): pl.pallas_call(kernel, out_shape=out_shape, in_specs=in_specs or [vmem] *...  39.7 us
    all_to_all x2, waiting for transfers between devices, exchange(): return lax.all_to_all(values, axes, 0, 0)  20.1 us
    ppermute x3, starting transfers between devices, swap_cores(): return lax.ppermute(values, 'c', [(0, 1), (1, 0)])  12.3 us
    all_to_all x2, starting transfers between devices, exchange(): return lax.all_to_all(values, axes, 0, 0)  11.6 us
    unnamed x28, local copies, waits for them, and re-layouts  7.38 us
  transfers between devices with their start and end apart: 7, of which 5 were waited for; matrix products, arithmetic and copies ran while one was open for 1% of the time, Pallas kernels for 6%

profile of v4, /device:TPU:1, one launch (start us, length us, event | category | flops | bytes accessed | tf_op | source)
XLA Modules:
  0.0 239.0 jit_solution(13923310097728851376)
XLA Ops:
  7.2 0.0 copy-start.4
  7.2 0.0 copy-start.3
  7.2 0.0 all-gather.7.cloned.1.call-start
  7.2 0.7 pad_add_fusion.place
  7.9 3.3 %shard_map.104 = (bf16[128,1152]{1,0:T(8,128)(2,1)}, bf16[32,56,128]{2,1,0:T(8,128)(2,1)}, bf16[32,72,128]{2,1,0:T(8,128)(2,1)}) custom-call(s32[3]{0:T(128)} %pad_add_fusion.place, bf16[128,1152]{1,0:T(8,128)(2,1)} %bitcast.21, f32[3,2,1152]{2,1,0:T(2,128)} %bitcast.33, bf16[36,2,1728]{2,1,0:T(2,128)(2,1)} %bitcast.31, bf16[18,2,1152]{2,1,0:T(2,128)(2,1)} %bitcast.32), custom_call_target="tpu_custom_call" | custom-call | flops 2000000000 | bytes 6000000 | tf_op jit(solution)/shard_map/pallas_call | solution.py:30
  11.3 0.0 all-gather.7.cloned.1.call-update
  11.3 0.0 all-gather.5.cloned.1.call-start
  11.3 33.4 %all_to_all.35 = bf16[32,56,128]{2,1,0:T(8,128)(2,1)} all-to-all(bf16[32,56,128]{2,1,0:T(8,128)(2,1)} %get-tuple-element.17), channel_id=1, replica_groups=mesh['z'=8,'h'=4,'x'=4,'l'=2,'c'=2] {'z','h'}, dimensions={0} | all-to-all | bytes 917504 | tf_op jit(solution)/shard_map/all_to_all | solution.py:606
  44.7 0.0 all-gather.5.cloned.1.call-update
  44.7 6.5 %all-to-all-start.1 = ((bf16[32,72,128]{2,1,0:T(8,128)(2,1)}), bf16[32,72,128]{2,1,0:T(8,128)(2,1)S(1)}, u32[]{:S(2)}, u32[]{:S(2)}) async-start(bf16[32,72,128]{2,1,0:T(8,128)(2,1)} %get-tuple-element.19), calls=%async_computation.1 | async-start | bytes 1179648 | tf_op jit(solution)/shard_map/all_to_all | solution.py:606
  51.2 0.0 copy-done.4
  51.2 0.0 copy-done.3
  51.3 0.0 copy-done
  51.3 2.3 shard_map.105
  53.5 0.0 copy-start.7
  53.6 0.9 copy-done.7
  54.4 0.7 copy-done.8
  55.2 16.7 %all-to-all-done.1.weight = bf16[32,72,128]{2,1,0:T(8,128)(2,1)S(1)} async-done(((bf16[32,72,128]{2,1,0:T(8,128)(2,1)}), bf16[32,72,128]{2,1,0:T(8,128)(2,1)S(1)}, u32[]{:S(2)}, u32[]{:S(2)}) %all-to-all-start.1) | async-done | bytes 589856 | tf_op jit(solution)/shard_map/all_to_all | solution.py:606
  71.8 0.0 copy-done.6
  71.8 1.7 copy-done.1
  73.5 5.6 %shard_map.106 = (bf16[16,8,2944]{2,1,0:T(8,128)(2,1)S(1)}, f32[1024,256]{1,0:T(8,128)S(1)}, bf16[1024,128]{1,0:T(8,128)(2,1)S(1)}, f32[8,128,128]{2,1,0:T(8,128)S(1)}) custom-call(bf16[8,128,1152]{2,1,0:T(8,128)(2,1)S(1)} %bitcast.18, bf16[32,72,128]{2,1,0:T(8,128)(2,1)S(1)} %all-to-all-done.1.weight, bf16[128,1152]{1,0:T(8,128)(2,1)S(1)} %get-tuple-element.20.down, ...), custom_call_target="tpu_custom_call" | custom-call | flops 8000000000 | bytes 24000000 | tf_op jit(solution)/shard_map/pallas_call | solution.py:30
  79.1 1.0 copy-done.9
  80.1 0.8 copy-done.11
  80.9 27.7 %all_to_all.36.received_in = bf16[16,8,2944]{2,1,0:T(8,128)(2,1)} all-to-all(bf16[16,8,2944]{2,1,0:T(8,128)(2,1)S(1)} %get-tuple-element.22), channel_id=1, replica_groups=mesh['z'=8,'h'=4,'x'=4,'l'=2,'c'=2] {'x','l','c'}, dimensions={0} | all-to-all | bytes 1507328 | tf_op jit(solution)/shard_map/all_to_all | solution.py:606
  108.7 3.0 %all-gather.5.cloned.1.call-done = bf16[512,56,128]{2,1,0:T(8,128)(2,1)} async-done(((bf16[32,56,128]{2,1,0:T(8,128)(2,1)}), bf16[512,56,128]{2,1,0:T(8,128)(2,1)}) %all-gather.5.cloned.1.call-update) | async-done | bytes 7340048 | tf_op jit(solution)/shard_map/all_gather | solution.py:634
  111.6 20.6 %shard_map.107 = (bf16[16,64,128]{2,1,0:T(8,128)(2,1)}, f32[64,23,128]{2,1,0:T(8,128)}) custom-call(bf16[16,32,56,128]{3,2,1,0:T(8,128)(2,1)} %bitcast.30, bf16[16,8,2944]{2,1,0:T(8,128)(2,1)} %all_to_all.36.received_in, f32[3,2,1152]{2,1,0:T(2,128)} %bitcast.34, bf16[128,1152]{1,0:T(8,128)(2,1)} %copy-done.8, bf16[8,192,256]{2,1,0:T(8,128)(2,1)} %copy-done.7, ...), custom_call_target="tpu_custom_call" | custom-call | flops 24999999488 | bytes 75000000 | tf_op jit(solution)/shard_map/pallas_call | solution.py:30
  132.3 5.1 %all-to-all-start.3 = ((bf16[16,64,128]{2,1,0:T(8,128)(2,1)}), bf16[16,64,128]{2,1,0:T(8,128)(2,1)S(1)}, u32[]{:S(2)}, u32[]{:S(2)}) async-start(bf16[16,64,128]{2,1,0:T(8,128)(2,1)} %get-tuple-element.25), calls=%async_computation.3 | async-start | bytes 524288 | tf_op jit(solution)/shard_map/all_to_all | solution.py:606
  137.4 1.8 constant_dynamic-slice_fusion
  139.2 2.0 collective-permute-start.1
  141.2 3.4 %all-to-all-done.3.cotangent = bf16[16,64,128]{2,1,0:T(8,128)(2,1)S(1)} async-done(((bf16[16,64,128]{2,1,0:T(8,128)(2,1)}), bf16[16,64,128]{2,1,0:T(8,128)(2,1)S(1)}, u32[]{:S(2)}, u32[]{:S(2)}) %all-to-all-start.3) | async-done | bytes 262176 | tf_op jit(solution)/shard_map/all_to_all | solution.py:606
  144.6 1.2 copy-done.10
  145.8 1.0 copy-done.12
  146.9 5.5 %shard_map.108 = f32[64,11,128]{2,1,0:T(8,128)S(1)} custom-call(bf16[16,64,128]{2,1,0:T(8,128)(2,1)S(1)} %all-to-all-done.3.cotangent, bf16[192,256]{1,0:T(8,128)(2,1)S(1)} %get-tuple-element.21.up, bf16[8,128,1152]{2,1,0:T(8,128)(2,1)S(1)} %bitcast.19, f32[1024,256]{1,0:T(8,128)S(1)} %copy-done.10, bf16[1024,128]{1,0:T(8,128)(2,1)S(1)} %get-tuple-element.27.reduced, ...), custom_call_target="tpu_custom_call" | custom-call | flops 20000000000 | bytes 60000000 | tf_op jit(solution)/shard_map/pallas_call | solution.py:30
  152.4 2.9 %collective-permute-start = (f32[32,11,128]{2,1,0:T(8,128)S(1)}, f32[32,11,128]{2,1,0:T(8,128)S(1)}, u32[]{:S(2)}, u32[]{:S(2)}) collective-permute-start(f32[32,11,128]{2,1,0:T(8,128)S(1)} %constant_dynamic-slice_fusion.1), channel_id=1, source_target_pairs={{0,1},{1,0},{2,3},{3,2},{4,5},{5,4},{6,7},{7,6},{8,9},{9,8},{10,11... | collective-permute-start | bytes 540680 | tf_op jit(solution)/shard_map/ppermute | solution.py:614
  155.3 0.0 collective-permute-done.1
  155.3 1.0 dynamic-slice_add_fusion
  156.4 0.1 collective-permute-done
  156.5 0.1 pad_maximum_fusion
  156.6 0.1 copy.19
  156.8 0.4 copy.20
  157.2 25.2 %all_to_all.37 = f32[32,9,4,128]{3,2,1,0:T(4,128)S(1)} all-to-all(f32[32,9,4,128]{3,2,1,0:T(4,128)S(1)} %copy.20), channel_id=1, replica_groups=mesh['z'=8,'h'=4,'x'=4,'l'=2,'c'=2] {'z','x'}, dimensions={0} | all-to-all | bytes 1179648 | tf_op jit(solution)/shard_map/all_to_all | solution.py:606
  182.4 0.1 copy.21
  182.6 14.1 %all_to_all.38 = f32[8,48,128]{2,1,0:T(8,128)S(1)} all-to-all(f32[8,48,128]{2,1,0:T(8,128)S(1)} %broadcast_in_dim.4), channel_id=1, replica_groups=mesh['z'=8,'h'=4,'x'=4,'l'=2,'c'=2] {'h','l'}, dimensions={0} | all-to-all | bytes 393216 | tf_op jit(solution)/shard_map/all_to_all | solution.py:606
  196.7 0.1 broadcast_in_dim.5
  196.8 23.6 %all_to_all.39.own = f32[32,48,128]{2,1,0:T(8,128)S(1)} all-to-all(f32[32,48,128]{2,1,0:T(8,128)S(1)} %broadcast_in_dim.5), channel_id=1, replica_groups=mesh['z'=8,'h'=4,'x'=4,'l'=2,'c'=2] {'z','x'}, dimensions={0} | all-to-all | bytes 1572864 | tf_op jit(solution)/shard_map/all_to_all | solution.py:606
  220.4 7.4 %collective-permute-start.2 = (f32[32,48,128]{2,1,0:T(8,128)S(1)}, f32[32,48,128]{2,1,0:T(8,128)S(1)}, u32[]{:S(2)}, u32[]{:S(2)}) collective-permute-start(f32[32,48,128]{2,1,0:T(8,128)S(1)} %all_to_all.39.own), channel_id=1, source_target_pairs={{0,1},{1,0},{2,3},{3,2},{4,5},{5,4},{6,7},{7,6},{8,9},{9,8},{10,11... | collective-permute-start | bytes 2359304 | tf_op jit(solution)/shard_map/ppermute | solution.py:614
  227.8 1.9 collective-permute-done.2.other
  229.7 2.4 shard_map.109
  (26 shorter events, 0.3 us)
Async XLA Ops:
  7.2 44.1 %copy-start.4 = (f32[2,1152,64]{1,2,0:T(8,128)S(1)}, f32[2,1152,64]{1,2,0:T(8,128)}, u32[]{:S(2)}) copy-start(f32[2,1152,64]{1,2,0:T(8,128)} %param.14) | copy-start | bytes 1769476
  7.2 44.1 %copy-start.3 = (f32[2,64,1728]{2,1,0:T(8,128)S(1)}, f32[2,64,1728]{2,1,0:T(8,128)}, u32[]{:S(2)}) copy-start(f32[2,64,1728]{2,1,0:T(8,128)} %up.1) | copy-start | bytes 2654212
  7.2 64.6 %all-gather.7.cloned.1.call-start = ((), (), s32[]{:S(2)}) async-start(), calls=%async_computation.8 | async-start | bytes 2654208 | tf_op jit(solution)/shard_map/all_gather | solution.py:633
  7.9 43.4 %copy-start = (s32[3]{0:T(128)S(1)}, s32[3]{0:T(128)}, u32[]{:S(2)}) copy-start(s32[3]{0:T(128)} %pad_add_fusion.place) | copy-start | bytes 40
  7.9 63.9 %copy-start.5 = (bf16[1,1,128,1152]{3,2,1,0:T(8,128)(2,1)S(1)}, bf16[1,1,128,1152]{3,2,1,0:T(8,128)(2,1)}, u32[]{:S(2)}) copy-start(bf16[1,1,128,1152]{3,2,1,0:T(8,128)(2,1)} %param.9) | copy-start | bytes 884740
  7.9 63.9 %copy-start.6 = (bf16[1,1,128,1152]{3,2,1,0:T(8,128)(2,1)S(1)}, bf16[1,1,128,1152]{3,2,1,0:T(8,128)(2,1)}, u32[]{:S(2)}) copy-start(bf16[1,1,128,1152]{3,2,1,0:T(8,128)(2,1)} %param.10) | copy-start | bytes 884740
  11.3 100.3 %all-gather.5.cloned.1.call-start = ((), (), s32[]{:S(2)}) async-start(), calls=%async_computation.7 | async-start | bytes 7798784 | tf_op jit(solution)/shard_map/all_gather | solution.py:634
  44.7 27.1 %all-to-all-start.1 = ((bf16[32,72,128]{2,1,0:T(8,128)(2,1)}), bf16[32,72,128]{2,1,0:T(8,128)(2,1)S(1)}, u32[]{:S(2)}, u32[]{:S(2)}) async-start(bf16[32,72,128]{2,1,0:T(8,128)(2,1)} %get-tuple-element.19), calls=%async_computation.1 | async-start | bytes 1179648 | tf_op jit(solution)/shard_map/all_to_all | solution.py:606
  53.5 0.9 copy-start.7
  54.4 0.7 copy-start.8
  71.8 1.7 copy-start.1
  79.1 1.0 copy-start.9
  80.1 0.8 copy-start.11
  111.6 32.9 %copy-start.2 = (bf16[1024,1152]{1,0:T(8,128)(2,1)S(1)}, bf16[1024,1152]{1,0:T(8,128)(2,1)}, u32[]{:S(2)}) copy-start(bf16[1024,1152]{1,0:T(8,128)(2,1)} %all-gather.7.cloned.1.call-done) | copy-start | bytes 7077892
  132.3 12.3 %all-to-all-start.3 = ((bf16[16,64,128]{2,1,0:T(8,128)(2,1)}), bf16[16,64,128]{2,1,0:T(8,128)(2,1)S(1)}, u32[]{:S(2)}, u32[]{:S(2)}) async-start(bf16[16,64,128]{2,1,0:T(8,128)(2,1)} %get-tuple-element.25), calls=%async_computation.3 | async-start | bytes 524288 | tf_op jit(solution)/shard_map/all_to_all | solution.py:606
  139.2 16.1 %collective-permute-start.1 = (f32[32,23,128]{2,1,0:T(8,128)}, f32[32,23,128]{2,1,0:T(8,128)}, u32[]{:S(2)}, u32[]{:S(2)}) collective-permute-start(f32[32,23,128]{2,1,0:T(8,128)} %constant_dynamic-slice_fusion), channel_id=1, source_target_pairs={{0,1},{1,0},{2,3},{3,2},{4,5},{5,4},{6,7},{7,6},{8,9},{9,8},{10,11... | collective-permute-start | bytes 1130504 | tf_op jit(solution)/shard_map/ppermute | solution.py:614
  144.6 1.2 copy-start.10
  145.8 1.0 copy-start.12
  146.8 8.5 %copy-start.13 = (f32[64,23,128]{2,1,0:T(8,128)S(1)}, f32[64,23,128]{2,1,0:T(8,128)}, u32[]{:S(2)}) copy-start(f32[64,23,128]{2,1,0:T(8,128)} %get-tuple-element.29) | copy-start | bytes 2260996
  152.4 4.0 %collective-permute-start = (f32[32,11,128]{2,1,0:T(8,128)S(1)}, f32[32,11,128]{2,1,0:T(8,128)S(1)}, u32[]{:S(2)}, u32[]{:S(2)}) collective-permute-start(f32[32,11,128]{2,1,0:T(8,128)S(1)} %constant_dynamic-slice_fusion.1), channel_id=1, source_target_pairs={{0,1},{1,0},{2,3},{3,2},{4,5},{5,4},{6,7},{7,6},{8,9},{9,8},{10,11... | collective-permute-start | bytes 540680 | tf_op jit(solution)/shard_map/ppermute | solution.py:614
  220.4 9.3 %collective-permute-start.2 = (f32[32,48,128]{2,1,0:T(8,128)S(1)}, f32[32,48,128]{2,1,0:T(8,128)S(1)}, u32[]{:S(2)}, u32[]{:S(2)}) collective-permute-start(f32[32,48,128]{2,1,0:T(8,128)S(1)} %all_to_all.39.own), channel_id=1, source_target_pairs={{0,1},{1,0},{2,3},{3,2},{4,5},{5,4},{6,7},{7,6},{8,9},{9,8},{10,11... | collective-permute-start | bytes 2359304 | tf_op jit(solution)/shard_map/ppermute | solution.py:614
Sparse Core Ops, SparseCore 0:
  11.4 36.8 all-gather.6
  50.4 61.1 all-gather.4

commit v5 on v4

--- a/solution.py
+++ b/solution.py
@@ -162,20 +162,37 @@
     return cosine, sine
 
 
+def modded_kernel(latents_in, modulation_in, modded_out, latents, modulation, modded, sems):
+    start = copier(sems)
+    arrivals = [start(latents_in, latents), start(modulation_in, modulation)]
+    for copy in arrivals:
+        copy.wait()
+    normed, _ = normalise(latents[...].astype(F32))
+    modded[...] = (normed * (1.0 + modulation[1, 0:1]) + modulation[0, 0:1]).astype(BF16)
+    start(modded, modded_out).wait()
+
+
+def modded_rows(*operands):
+    out = jax.ShapeDtypeStruct((ROWS, WIDTH), BF16)
+    return call(
+        modded_kernel,
+        out,
+        [like(v) for v in operands] + [like(out), pltpu.SemaphoreType.DMA((3,))],
+        [HBM] * 2,
+        limit=60,
+        out_space=pltpu.HBM,
+    )(*operands)
+
+
 def prologue_kernel(place, *refs):
-    sources, outs, held = refs[:4], refs[4:7], refs[7:11]
-    modded, part, first_part, rest, sems = refs[11:]
+    sources, outs, held = refs[:2], refs[2:4], refs[4:6]
+    part, first_part, rest, sems = refs[6:]
     start = copier(sems)
     arrivals = [start(a, b) for a, b in zip(sources, held)]
-    latents, modulation, qkv, out = held
-    arrivals[0].wait()
-    arrivals[1].wait()
-    normed, _ = normalise(latents[...].astype(F32))
-    modded[...] = (normed * (1.0 + modulation[1, 0:1]) + modulation[0, 0:1]).astype(BF16)
-    finish = [start(modded, outs[0])]
+    qkv, out = held
     rest[...] = jnp.zeros_like(rest)
-    arrivals[2].wait()
-    arrivals[3].wait()
+    for copy in arrivals:
+        copy.wait()
     for head in range(HEADS):
 
         @pl.when(place[0] == head)
@@ -199,14 +216,13 @@
     for copy in range(32):
         part[copy] = mine
         first_part[copy] = first
-    finish += [start(part, outs[1]), start(first_part, outs[2])]
+    finish = [start(part, outs[0]), start(first_part, outs[1])]
     for copy in finish:
         copy.wait()
 
 
 def prologue(place, *operands):
     outs = (
-        jax.ShapeDtypeStruct((ROWS, WIDTH), BF16),
         jax.ShapeDtypeStruct((32, 56, 128), BF16),
         jax.ShapeDtypeStruct((32, 72, 128), BF16),
     )
@@ -215,8 +231,8 @@
         outs,
         [like(v) for v in operands]
         + [like(v) for v in outs]
-        + [pltpu.VMEM((2, 36, 384), F32), pltpu.SemaphoreType.DMA((7,))],
-        [SMEM] + [HBM] * 4,
+        + [pltpu.VMEM((2, 36, 384), F32), pltpu.SemaphoreType.DMA((4,))],
+        [SMEM] + [HBM] * 2,
         limit=60,
         out_space=pltpu.HBM,
     )(place, *operands)
@@ -423,18 +439,16 @@
     sems,
 ):
     start = copier(sems)
+    received_copy = start(received_in, received)
     copies = part_copies(gathered, held, start)
     arrivals = [
-        start(received_in, received),
         start(modulation_in, modulation),
         start(down_in, down),
         start(up_in, up),
         start(cosine_in, cosine),
         start(sine_in, sine),
     ]
-    assemble(copies, held, qkv, out_first, out_second)
-    for copy in arrivals:
-        copy.wait()
+    received_copy.wait()
     for head in range(HEADS):
         x, c = head // 2, head % 2
         rows = jnp.concatenate(
@@ -446,6 +460,9 @@
             0,
         )
         wide[:, HEAD * head : HEAD * head + HEAD] = rows
+    assemble(copies, held, qkv, out_first, out_second)
+    for copy in arrivals:
+        copy.wait()
     gate_first, gate_second = modulation[2, 0:1], modulation[2, 1:2]
     mixed = dot(wide[...].astype(BF16), out_first[...])
     middle = (by_rows(received, slice(640, 640 + WIDTH)) + gate_first * mixed).astype(BF16).astype(F32)
@@ -623,13 +640,8 @@
     x, l, c = lax.axis_index("x"), lax.axis_index("l"), lax.axis_index("c")
     place = jnp.stack([x * 2 + c, l, c]).astype(jnp.int32)
     modulation = modulation[0].transpose(1, 0, 2)
-    modded, part, first = prologue(
-        place,
-        latents[0, 0],
-        modulation,
-        qkv.transpose(1, 0, 2),
-        out.transpose(1, 0, 2),
-    )
+    modded = modded_rows(latents[0, 0], modulation)
+    part, first = prologue(place, qkv.transpose(1, 0, 2), out.transpose(1, 0, 2))
     modded = lax.all_gather(modded, ("x", "c"), axis=0, tiled=False)
     gathered = lax.all_gather(exchange(part, DP), SEQ, axis=0, tiled=False)
     first = exchange(first, DP)

time: 240 us -> 239 us (level)
    pallas_call x6 -> x7, Pallas kernels: 39.7 us -> 41.4 us  [run(): pl.pallas_call(kernel, out_shape=out_shape, in_specs=in_specs or [vmem] *...]
  transfers between devices with their start and end apart: 7 -> 7, of which waited for: 5 -> 5; matrix products, arithmetic and copies ran while one was open for 1% -> 1% of each run, Pallas kernels for 6% -> 7%
where the time goes in v5:
time: 239 us; the launch traced here: 238 us
  blocking collectives  123 us (51%)
  Pallas kernels  41.4 us (17%)
  waiting for transfers between devices  24.1 us (10%)
  starting transfers between devices  23.2 us (10%)
  between operations  14.3 us (6%)
  local copies, waits for them, and re-layouts  9.79 us (4%)
    all_to_all x5, blocking collectives, exchange(): return lax.all_to_all(values, axes, 0, 0)  123 us
    pallas_call x7, Pallas kernels, run(): pl.pallas_call(kernel, out_shape=out_shape, in_specs=in_specs or [vmem] *...  41.4 us
    all_to_all x2, waiting for transfers between devices, exchange(): return lax.all_to_all(values, axes, 0, 0)  20 us
    ppermute x3, starting transfers between devices, swap_cores(): return lax.ppermute(values, 'c', [(0, 1), (1, 0)])  12.3 us
    all_to_all x2, starting transfers between devices, exchange(): return lax.all_to_all(values, axes, 0, 0)  10.8 us
    unnamed x28, local copies, waits for them, and re-layouts  7.36 us
  transfers between devices with their start and end apart: 7, of which 5 were waited for; matrix products, arithmetic and copies ran while one was open for 1% of the time, Pallas kernels for 7%

profile of v5, /device:TPU:1, one launch (start us, length us, event | category | flops | bytes accessed | tf_op | source)
XLA Modules:
  0.0 238.0 jit_solution(6017535945758398218)
XLA Ops:
  7.2 0.0 all-gather.7.cloned.1.call-start
  7.2 0.0 copy-start.3
  7.2 0.0 copy-start.4
  7.2 2.1 shard_map.105
  9.3 0.0 all-gather.7.cloned.1.call-update
  9.3 0.0 all-gather.5.cloned.1.call-start
  9.4 0.7 pad_add_fusion.place
  10.1 3.1 %shard_map.104 = (bf16[32,56,128]{2,1,0:T(8,128)(2,1)}, bf16[32,72,128]{2,1,0:T(8,128)(2,1)}) custom-call(s32[3]{0:T(128)} %pad_add_fusion.place, bf16[36,2,1728]{2,1,0:T(2,128)(2,1)} %bitcast.31, bf16[18,2,1152]{2,1,0:T(2,128)(2,1)} %bitcast.32), custom_call_target="tpu_custom_call" | custom-call | flops 2000000000 | bytes 6000000 | tf_op jit(solution)/shard_map/pallas_call | solution.py:30
  13.2 33.4 %all_to_all.35 = bf16[32,56,128]{2,1,0:T(8,128)(2,1)} all-to-all(bf16[32,56,128]{2,1,0:T(8,128)(2,1)} %get-tuple-element.16), channel_id=1, replica_groups=mesh['z'=8,'h'=4,'x'=4,'l'=2,'c'=2] {'z','h'}, dimensions={0} | all-to-all | bytes 917504 | tf_op jit(solution)/shard_map/all_to_all | solution.py:623
  46.5 0.0 all-gather.5.cloned.1.call-update
  46.6 6.5 %all-to-all-start.1 = ((bf16[32,72,128]{2,1,0:T(8,128)(2,1)}), bf16[32,72,128]{2,1,0:T(8,128)(2,1)S(1)}, u32[]{:S(2)}, u32[]{:S(2)}) async-start(bf16[32,72,128]{2,1,0:T(8,128)(2,1)} %get-tuple-element.17), calls=%async_computation.1 | async-start | bytes 1179648 | tf_op jit(solution)/shard_map/all_to_all | solution.py:623
  53.1 2.3 shard_map.106
  55.4 0.0 copy-start.7
  55.4 0.9 copy-done.7
  56.3 0.7 copy-done.8
  57.0 16.7 %all-to-all-done.1.weight = bf16[32,72,128]{2,1,0:T(8,128)(2,1)S(1)} async-done(((bf16[32,72,128]{2,1,0:T(8,128)(2,1)}), bf16[32,72,128]{2,1,0:T(8,128)(2,1)S(1)}, u32[]{:S(2)}, u32[]{:S(2)}) %all-to-all-start.1) | async-done | bytes 589856 | tf_op jit(solution)/shard_map/all_to_all | solution.py:623
  73.6 0.0 copy-done.6
  73.7 1.7 copy-done.1
  75.3 5.6 %shard_map.107 = (bf16[16,8,2944]{2,1,0:T(8,128)(2,1)S(1)}, f32[1024,256]{1,0:T(8,128)S(1)}, bf16[1024,128]{1,0:T(8,128)(2,1)S(1)}, f32[8,128,128]{2,1,0:T(8,128)S(1)}) custom-call(bf16[8,128,1152]{2,1,0:T(8,128)(2,1)S(1)} %bitcast.18, bf16[32,72,128]{2,1,0:T(8,128)(2,1)S(1)} %all-to-all-done.1.weight, bf16[128,1152]{1,0:T(8,128)(2,1)S(1)} %get-tuple-element.18.down, ...), custom_call_target="tpu_custom_call" | custom-call | flops 8000000000 | bytes 24000000 | tf_op jit(solution)/shard_map/pallas_call | solution.py:30
  80.9 1.0 copy-done.9
  81.9 0.8 copy-done.11
  82.7 27.6 %all_to_all.36.received_in = bf16[16,8,2944]{2,1,0:T(8,128)(2,1)} all-to-all(bf16[16,8,2944]{2,1,0:T(8,128)(2,1)S(1)} %get-tuple-element.20), channel_id=1, replica_groups=mesh['z'=8,'h'=4,'x'=4,'l'=2,'c'=2] {'x','l','c'}, dimensions={0} | all-to-all | bytes 1507328 | tf_op jit(solution)/shard_map/all_to_all | solution.py:623
  110.3 2.1 all-gather.5.cloned.1.call-done
  112.4 20.5 %shard_map.108 = (bf16[16,64,128]{2,1,0:T(8,128)(2,1)}, f32[64,23,128]{2,1,0:T(8,128)}) custom-call(bf16[16,32,56,128]{3,2,1,0:T(8,128)(2,1)} %bitcast.30, bf16[16,8,2944]{2,1,0:T(8,128)(2,1)} %all_to_all.36.received_in, f32[3,2,1152]{2,1,0:T(2,128)} %bitcast.34, bf16[128,1152]{1,0:T(8,128)(2,1)} %copy-done.8, bf16[8,192,256]{2,1,0:T(8,128)(2,1)} %copy-done.7, ...), custom_call_target="tpu_custom_call" | custom-call | flops 24999999488 | bytes 75000000 | tf_op jit(solution)/shard_map/pallas_call | solution.py:30
  132.9 4.3 %all-to-all-start.3 = ((bf16[16,64,128]{2,1,0:T(8,128)(2,1)}), bf16[16,64,128]{2,1,0:T(8,128)(2,1)S(1)}, u32[]{:S(2)}, u32[]{:S(2)}) async-start(bf16[16,64,128]{2,1,0:T(8,128)(2,1)} %get-tuple-element.23), calls=%async_computation.3 | async-start | bytes 524288 | tf_op jit(solution)/shard_map/all_to_all | solution.py:623
  137.2 1.8 constant_dynamic-slice_fusion
  139.0 2.0 collective-permute-start.1
  141.0 3.4 %all-to-all-done.3.cotangent = bf16[16,64,128]{2,1,0:T(8,128)(2,1)S(1)} async-done(((bf16[16,64,128]{2,1,0:T(8,128)(2,1)}), bf16[16,64,128]{2,1,0:T(8,128)(2,1)S(1)}, u32[]{:S(2)}, u32[]{:S(2)}) %all-to-all-start.3) | async-done | bytes 262176 | tf_op jit(solution)/shard_map/all_to_all | solution.py:623
  144.4 0.0 copy-done.2
  144.4 1.2 copy-done.10
  145.6 1.0 copy-done.12
  146.7 5.5 %shard_map.109 = f32[64,11,128]{2,1,0:T(8,128)S(1)} custom-call(bf16[16,64,128]{2,1,0:T(8,128)(2,1)S(1)} %all-to-all-done.3.cotangent, bf16[192,256]{1,0:T(8,128)(2,1)S(1)} %get-tuple-element.19.up, bf16[8,128,1152]{2,1,0:T(8,128)(2,1)S(1)} %bitcast.19, f32[1024,256]{1,0:T(8,128)S(1)} %copy-done.10, bf16[1024,128]{1,0:T(8,128)(2,1)S(1)} %get-tuple-element.25.reduced, ...), custom_call_target="tpu_custom_call" | custom-call | flops 20000000000 | bytes 60000000 | tf_op jit(solution)/shard_map/pallas_call | solution.py:30
  152.2 2.9 %collective-permute-start = (f32[32,11,128]{2,1,0:T(8,128)S(1)}, f32[32,11,128]{2,1,0:T(8,128)S(1)}, u32[]{:S(2)}, u32[]{:S(2)}) collective-permute-start(f32[32,11,128]{2,1,0:T(8,128)S(1)} %constant_dynamic-slice_fusion.1), channel_id=1, source_target_pairs={{0,1},{1,0},{2,3},{3,2},{4,5},{5,4},{6,7},{7,6},{8,9},{9,8},{10,11... | collective-permute-start | bytes 540680 | tf_op jit(solution)/shard_map/ppermute | solution.py:631
  155.1 0.0 collective-permute-done.1
  155.1 0.0 copy-done.13
  155.1 1.0 dynamic-slice_add_fusion
  156.2 0.1 collective-permute-done
  156.3 0.1 pad_maximum_fusion
  156.5 0.1 copy.19
  156.6 0.4 copy.20
  157.0 24.7 %all_to_all.37 = f32[32,9,4,128]{3,2,1,0:T(4,128)S(1)} all-to-all(f32[32,9,4,128]{3,2,1,0:T(4,128)S(1)} %copy.20), channel_id=1, replica_groups=mesh['z'=8,'h'=4,'x'=4,'l'=2,'c'=2] {'z','x'}, dimensions={0} | all-to-all | bytes 1179648 | tf_op jit(solution)/shard_map/all_to_all | solution.py:623
  181.7 0.1 copy.21
  181.9 13.9 %all_to_all.38 = f32[8,48,128]{2,1,0:T(8,128)S(1)} all-to-all(f32[8,48,128]{2,1,0:T(8,128)S(1)} %broadcast_in_dim.4), channel_id=1, replica_groups=mesh['z'=8,'h'=4,'x'=4,'l'=2,'c'=2] {'h','l'}, dimensions={0} | all-to-all | bytes 393216 | tf_op jit(solution)/shard_map/all_to_all | solution.py:623
  195.8 0.1 broadcast_in_dim.5
  195.9 23.6 %all_to_all.39.own = f32[32,48,128]{2,1,0:T(8,128)S(1)} all-to-all(f32[32,48,128]{2,1,0:T(8,128)S(1)} %broadcast_in_dim.5), channel_id=1, replica_groups=mesh['z'=8,'h'=4,'x'=4,'l'=2,'c'=2] {'z','x'}, dimensions={0} | all-to-all | bytes 1572864 | tf_op jit(solution)/shard_map/all_to_all | solution.py:623
  219.4 7.4 %collective-permute-start.2 = (f32[32,48,128]{2,1,0:T(8,128)S(1)}, f32[32,48,128]{2,1,0:T(8,128)S(1)}, u32[]{:S(2)}, u32[]{:S(2)}) collective-permute-start(f32[32,48,128]{2,1,0:T(8,128)S(1)} %all_to_all.39.own), channel_id=1, source_target_pairs={{0,1},{1,0},{2,3},{3,2},{4,5},{5,4},{6,7},{7,6},{8,9},{9,8},{10,11... | collective-permute-start | bytes 2359304 | tf_op jit(solution)/shard_map/ppermute | solution.py:631
  226.8 1.9 collective-permute-done.2.other
  228.7 2.4 %shard_map.110 = (f32[2,64,1152]{2,1,0:T(8,128)}, f32[2,64,1728]{2,1,0:T(8,128)}) custom-call(s32[3]{0:T(128)S(1)} %copy-done, f32[32,48,128]{2,1,0:T(8,128)S(1)} %all_to_all.39.own, f32[32,48,128]{2,1,0:T(8,128)S(1)} %collective-permute-done.2.other), custom_call_target="tpu_custom_call" | custom-call | flops 2000000000 | bytes 6000000 | tf_op jit(solution)/shard_map/pallas_call | solution.py:30
  (27 shorter events, 0.3 us)
Async XLA Ops:
  7.2 66.5 %all-gather.7.cloned.1.call-start = ((), (), s32[]{:S(2)}) async-start(), calls=%async_computation.8 | async-start | bytes 2654208 | tf_op jit(solution)/shard_map/all_gather | solution.py:645
  7.2 45.9 %copy-start.3 = (f32[2,64,1728]{2,1,0:T(8,128)S(1)}, f32[2,64,1728]{2,1,0:T(8,128)}, u32[]{:S(2)}) copy-start(f32[2,64,1728]{2,1,0:T(8,128)} %up.1) | copy-start | bytes 2654212
  7.2 45.9 %copy-start.4 = (f32[2,1152,64]{1,2,0:T(8,128)S(1)}, f32[2,1152,64]{1,2,0:T(8,128)}, u32[]{:S(2)}) copy-start(f32[2,1152,64]{1,2,0:T(8,128)} %param.14) | copy-start | bytes 1769476
  9.3 103.1 %all-gather.5.cloned.1.call-start = ((), (), s32[]{:S(2)}) async-start(), calls=%async_computation.7 | async-start | bytes 7798784 | tf_op jit(solution)/shard_map/all_gather | solution.py:646
  10.1 43.0 %copy-start = (s32[3]{0:T(128)S(1)}, s32[3]{0:T(128)}, u32[]{:S(2)}) copy-start(s32[3]{0:T(128)} %pad_add_fusion.place) | copy-start | bytes 40
  10.1 63.6 %copy-start.5 = (bf16[1,1,128,1152]{3,2,1,0:T(8,128)(2,1)S(1)}, bf16[1,1,128,1152]{3,2,1,0:T(8,128)(2,1)}, u32[]{:S(2)}) copy-start(bf16[1,1,128,1152]{3,2,1,0:T(8,128)(2,1)} %param.9) | copy-start | bytes 884740
  10.1 63.6 %copy-start.6 = (bf16[1,1,128,1152]{3,2,1,0:T(8,128)(2,1)S(1)}, bf16[1,1,128,1152]{3,2,1,0:T(8,128)(2,1)}, u32[]{:S(2)}) copy-start(bf16[1,1,128,1152]{3,2,1,0:T(8,128)(2,1)} %param.10) | copy-start | bytes 884740
  46.6 27.1 %all-to-all-start.1 = ((bf16[32,72,128]{2,1,0:T(8,128)(2,1)}), bf16[32,72,128]{2,1,0:T(8,128)(2,1)S(1)}, u32[]{:S(2)}, u32[]{:S(2)}) async-start(bf16[32,72,128]{2,1,0:T(8,128)(2,1)} %get-tuple-element.17), calls=%async_computation.1 | async-start | bytes 1179648 | tf_op jit(solution)/shard_map/all_to_all | solution.py:623
  55.4 0.9 copy-start.7
  56.3 0.7 copy-start.8
  73.6 1.7 copy-start.1
  80.9 1.0 copy-start.9
  81.9 0.8 copy-start.11
  112.4 32.0 %copy-start.2 = (bf16[1024,1152]{1,0:T(8,128)(2,1)S(1)}, bf16[1024,1152]{1,0:T(8,128)(2,1)}, u32[]{:S(2)}) copy-start(bf16[1024,1152]{1,0:T(8,128)(2,1)} %all-gather.7.cloned.1.call-done) | copy-start | bytes 7077892
  132.9 11.5 %all-to-all-start.3 = ((bf16[16,64,128]{2,1,0:T(8,128)(2,1)}), bf16[16,64,128]{2,1,0:T(8,128)(2,1)S(1)}, u32[]{:S(2)}, u32[]{:S(2)}) async-start(bf16[16,64,128]{2,1,0:T(8,128)(2,1)} %get-tuple-element.23), calls=%async_computation.3 | async-start | bytes 524288 | tf_op jit(solution)/shard_map/all_to_all | solution.py:623
  139.0 16.1 %collective-permute-start.1 = (f32[32,23,128]{2,1,0:T(8,128)}, f32[32,23,128]{2,1,0:T(8,128)}, u32[]{:S(2)}, u32[]{:S(2)}) collective-permute-start(f32[32,23,128]{2,1,0:T(8,128)} %constant_dynamic-slice_fusion), channel_id=1, source_target_pairs={{0,1},{1,0},{2,3},{3,2},{4,5},{5,4},{6,7},{7,6},{8,9},{9,8},{10,11... | collective-permute-start | bytes 1130504 | tf_op jit(solution)/shard_map/ppermute | solution.py:631
  144.4 1.2 copy-start.10
  145.6 1.0 copy-start.12
  146.7 8.5 %copy-start.13 = (f32[64,23,128]{2,1,0:T(8,128)S(1)}, f32[64,23,128]{2,1,0:T(8,128)}, u32[]{:S(2)}) copy-start(f32[64,23,128]{2,1,0:T(8,128)} %get-tuple-element.27) | copy-start | bytes 2260996
  152.2 4.0 %collective-permute-start = (f32[32,11,128]{2,1,0:T(8,128)S(1)}, f32[32,11,128]{2,1,0:T(8,128)S(1)}, u32[]{:S(2)}, u32[]{:S(2)}) collective-permute-start(f32[32,11,128]{2,1,0:T(8,128)S(1)} %constant_dynamic-slice_fusion.1), channel_id=1, source_target_pairs={{0,1},{1,0},{2,3},{3,2},{4,5},{5,4},{6,7},{7,6},{8,9},{9,8},{10,11... | collective-permute-start | bytes 540680 | tf_op jit(solution)/shard_map/ppermute | solution.py:631
  219.4 9.3 %collective-permute-start.2 = (f32[32,48,128]{2,1,0:T(8,128)S(1)}, f32[32,48,128]{2,1,0:T(8,128)S(1)}, u32[]{:S(2)}, u32[]{:S(2)}) collective-permute-start(f32[32,48,128]{2,1,0:T(8,128)S(1)} %all_to_all.39.own), channel_id=1, source_target_pairs={{0,1},{1,0},{2,3},{3,2},{4,5},{5,4},{6,7},{7,6},{8,9},{9,8},{10,11... | collective-permute-start | bytes 2359304 | tf_op jit(solution)/shard_map/ppermute | solution.py:631
Sparse Core Ops, SparseCore 0:
  10.1 36.8 all-gather.6
  49.1 63.2 all-gather.4

commit v6 on v4

--- a/solution.py
+++ b/solution.py
@@ -391,7 +391,10 @@
     cosine_in,
     sine_in,
     sent_out,
-    grad_out,
+    modded_out,
+    reduced_out,
+    d_projected_out,
+    d_reduced_out,
     received,
     modulation,
     down,
@@ -399,12 +402,11 @@
     cosine,
     sine,
     sent,
-    grad,
     wide,
     modded,
     reduced,
     d_projected,
-    ups,
+    d_reduced,
     projected,
     weights,
     q_all,
@@ -423,18 +425,16 @@
     sems,
 ):
     start = copier(sems)
+    received_copy = start(received_in, received)
     copies = part_copies(gathered, held, start)
     arrivals = [
-        start(received_in, received),
         start(modulation_in, modulation),
         start(down_in, down),
         start(up_in, up),
         start(cosine_in, cosine),
         start(sine_in, sine),
     ]
-    assemble(copies, held, qkv, out_first, out_second)
-    for copy in arrivals:
-        copy.wait()
+    received_copy.wait()
     for head in range(HEADS):
         x, c = head // 2, head % 2
         rows = jnp.concatenate(
@@ -446,6 +446,9 @@
             0,
         )
         wide[:, HEAD * head : HEAD * head + HEAD] = rows
+    assemble(copies, held, qkv, out_first, out_second)
+    for copy in arrivals:
+        copy.wait()
     gate_first, gate_second = modulation[2, 0:1], modulation[2, 1:2]
     mixed = dot(wide[...].astype(BF16), out_first[...])
     middle = (by_rows(received, slice(640, 640 + WIDTH)) + gate_first * mixed).astype(BF16).astype(F32)
@@ -455,6 +458,7 @@
     low = dot(modded[...], down[...], NT)
     high, rest = halves(low[:, :64] + low[:, 64:])
     reduced[...] = jnp.concatenate([high, rest], 1)
+    saves = [start(modded, modded_out), start(reduced, reduced_out)]
     three = jnp.concatenate([high, high, rest], 1)
     mask = same_token()
     for head in range(HEADS):
@@ -494,6 +498,7 @@
         back.append(head_norm_back(values, d))
     d_val = d_v[...].astype(BF16).astype(F32).reshape(HEADS * ROWS, 128)
     d_projected[...] = join_heads(*back, d_val).reshape(HEADS, ROWS, 256)
+    saves.append(start(d_projected, d_projected_out))
     d_low = jnp.zeros((ROWS, 128), F32)
     d_modded = jnp.zeros((ROWS, WIDTH), F32)
     for head in range(HEADS):
@@ -502,7 +507,8 @@
         d_modded += dot(high, qkv[head], NT)
     d_low = d_low[:, :64] + d_low[:, 64:]
     high, rest = halves(d_low)
-    d_reduced = jnp.concatenate([high, rest], 1)
+    d_reduced[...] = jnp.concatenate([high, rest], 1)
+    saves.append(start(d_reduced, d_reduced_out))
     through = dot(jnp.concatenate([high, high], 1), down[...]) + dot(rest, down[:64])
     d_modded = (d_modded.astype(BF16) + through.astype(BF16)).astype(F32)
     d_normed = d_modded * scale
@@ -516,20 +522,9 @@
         rows = jnp.concatenate([rows, jnp.zeros((ROWS, 128 - HEAD), BF16)], 1)
         sent[x * 4 + c] = rows[:64]
         sent[x * 4 + 2 + c] = rows[64:]
-    sent_copy = start(sent, sent_out)
-    ups[:, 1664:] = jnp.zeros((64, 128), F32)
-    for head in range(HEADS):
-        high, rest = halves(d_projected[head])
-        both = dot(reduced[...], jnp.concatenate([high, rest], 1), TN)
-        part = both[:64, :256] + both[64:, :256] + both[:64, 256:] + both[64:, 256:]
-        for k in range(3):
-            begin = k * FEATURES + head * HEAD
-            ups[:, begin : begin + HEAD] = part[:, k * HEAD : k * HEAD + HEAD]
-    down = dot(d_reduced, modded[...], TN)
-    store_tiles(grad, 0, down[:64] + down[64:])
-    store_tiles(grad, 9, ups[...])
-    start(grad, grad_out).wait()
-    sent_copy.wait()
+    saves.append(start(sent, sent_out))
+    for copy in saves:
+        copy.wait()
 
 
 def temporal(gathered, *operands):
@@ -537,17 +532,19 @@
         temporal_kernel,
         (
             jax.ShapeDtypeStruct((16, 64, 128), BF16),
-            jax.ShapeDtypeStruct((RANK, 23, 128), F32),
+            jax.ShapeDtypeStruct((ROWS, WIDTH), BF16),
+            jax.ShapeDtypeStruct((ROWS, 128), BF16),
+            jax.ShapeDtypeStruct((HEADS, ROWS, 256), F32),
+            jax.ShapeDtypeStruct((ROWS, 128), BF16),
         ),
         [like(v) for v in operands]
         + [
             pltpu.VMEM((16, 64, 128), BF16),
-            pltpu.VMEM((RANK, 23, 128), F32),
             pltpu.VMEM((ROWS, FEATURES), F32),
             pltpu.VMEM((ROWS, WIDTH), BF16),
             pltpu.VMEM((ROWS, 128), BF16),
             pltpu.VMEM((HEADS, ROWS, 256), F32),
-            pltpu.VMEM((RANK, 1792), F32),
+            pltpu.VMEM((ROWS, 128), BF16),
             pltpu.VMEM((HEADS, ROWS, 256), F32),
             pltpu.VMEM((HEADS, ROWS, ROWS), F32),
             pltpu.VMEM((HEADS, ROWS, 128), BF16),
@@ -563,13 +560,35 @@
             pltpu.VMEM((HEADS, ROWS, ROWS), BF16),
             pltpu.VMEM((HEADS, ROWS, 128), F32),
             pltpu.VMEM((HEADS, ROWS, 128), F32),
-            pltpu.SemaphoreType.DMA((12,)),
+            pltpu.SemaphoreType.DMA((16,)),
         ],
         [HBM] * 7,
-        limit=60,
+        limit=57,
         out_space=pltpu.HBM,
         us=25,
     )(gathered, *operands)
+
+
+def temporal_grad_kernel(modded, reduced, d_projected, d_reduced, grad, ups):
+    ups[:, 1664:] = jnp.zeros((64, 128), F32)
+    for head in range(HEADS):
+        high, rest = halves(d_projected[head])
+        both = dot(reduced[...], jnp.concatenate([high, rest], 1), TN)
+        part = both[:64, :256] + both[64:, :256] + both[:64, 256:] + both[64:, 256:]
+        for k in range(3):
+            begin = k * FEATURES + head * HEAD
+            ups[:, begin : begin + HEAD] = part[:, k * HEAD : k * HEAD + HEAD]
+    down = dot(d_reduced[...], modded[...], TN)
+    store_tiles(grad, 0, down[:64] + down[64:])
+    store_tiles(grad, 9, ups[...])
+
+
+def temporal_grad(*operands):
+    return call(
+        temporal_grad_kernel,
+        jax.ShapeDtypeStruct((RANK, 23, 128), F32),
+        [pltpu.VMEM((RANK, 1792), F32)],
+    )(*operands)
 
 
 def epilogue_kernel(place, own, other, grad_down, grad_up):
@@ -639,7 +658,7 @@
     )
     received = exchange(sent, SEQ)
     cosine, sine = rotation_tables()
-    sent, late = temporal(
+    sent, *saved = temporal(
         gathered,
         received,
         modulation,
@@ -649,7 +668,7 @@
         jnp.asarray(sine),
     )
     cotangent = exchange(sent, SEQ)
-    late = sum(add_cores(late, c))
+    late = sum(add_cores(temporal_grad(*saved), c))
     early = spatial_back(cotangent, up_first, modded, projected, reduced, weights)
     mine, other = add_cores(early, c)
     first_up, second_up = mine[:, 9:], other[:, 9:]

time: 240 us -> 242 us (level)
  local copies, waits for them, and re-layouts: 9.81 us -> 13.5 us
  waiting for transfers between devices: 25 us -> 21.7 us
    unnamed x28 -> x38, local copies, waits for them, and re-layouts: 7.38 us -> 12 us
    all_to_all x2, waiting for transfers between devices: 20.1 us -> 16.7 us  [exchange(): return lax.all_to_all(values, axes, 0, 0)]
    pallas_call x6 -> x7, Pallas kernels: 39.7 us -> 39.4 us  [run(): pl.pallas_call(kernel, out_shape=out_shape, in_specs=in_specs or [vmem] *...]
  transfers between devices with their start and end apart: 7 -> 7, of which waited for: 5 -> 4; matrix products, arithmetic and copies ran while one was open for 1% -> 1% of each run, Pallas kernels for 6% -> 6%
where the time goes in v6:
time: 242 us; the launch traced here: 241 us
  blocking collectives  126 us (52%)
  Pallas kernels  39.4 us (16%)
  starting transfers between devices  23.9 us (10%)
  waiting for transfers between devices  21.7 us (9%)
  between operations  14.4 us (6%)
  local copies, waits for them, and re-layouts  13.5 us (6%)
    all_to_all x5, blocking collectives, exchange(): return lax.all_to_all(values, axes, 0, 0)  126 us
    pallas_call x7, Pallas kernels, run(): pl.pallas_call(kernel, out_shape=out_shape, in_specs=in_specs or [vmem] *...  39.4 us
    all_to_all x2, waiting for transfers between devices, exchange(): return lax.all_to_all(values, axes, 0, 0)  16.7 us
    ppermute x3, starting transfers between devices, swap_cores(): return lax.ppermute(values, 'c', [(0, 1), (1, 0)])  12 us
    unnamed x38, local copies, waits for them, and re-layouts  12 us
    all_to_all x2, starting transfers between devices, exchange(): return lax.all_to_all(values, axes, 0, 0)  11.8 us
  transfers between devices with their start and end apart: 7, of which 4 were waited for; matrix products, arithmetic and copies ran while one was open for 1% of the time, Pallas kernels for 6%

profile of v6, /device:TPU:1, one launch (start us, length us, event | category | flops | bytes accessed | tf_op | source)
XLA Modules:
  0.0 241.1 jit_solution(3260455777174096284)
XLA Ops:
  7.2 0.0 all-gather.7.cloned.1.call-start
  7.2 0.6 pad_add_fusion.place
  7.8 3.3 %shard_map.104 = (bf16[128,1152]{1,0:T(8,128)(2,1)}, bf16[32,56,128]{2,1,0:T(8,128)(2,1)}, bf16[32,72,128]{2,1,0:T(8,128)(2,1)}) custom-call(s32[3]{0:T(128)} %pad_add_fusion.place, bf16[128,1152]{1,0:T(8,128)(2,1)} %bitcast.21, f32[3,2,1152]{2,1,0:T(2,128)} %bitcast.33, bf16[36,2,1728]{2,1,0:T(2,128)(2,1)} %bitcast.31, bf16[18,2,1152]{2,1,0:T(2,128)(2,1)} %bitcast.32), custom_call_target="tpu_custom_call" | custom-call | flops 2000000000 | bytes 6000000 | tf_op jit(solution)/shard_map/pallas_call | solution.py:30
  11.2 0.0 all-gather.7.cloned.1.call-update
  11.2 0.0 all-gather.5.cloned.1.call-start
  11.3 33.4 %all_to_all.35 = bf16[32,56,128]{2,1,0:T(8,128)(2,1)} all-to-all(bf16[32,56,128]{2,1,0:T(8,128)(2,1)} %get-tuple-element.20), channel_id=1, replica_groups=mesh['z'=8,'h'=4,'x'=4,'l'=2,'c'=2] {'z','h'}, dimensions={0} | all-to-all | bytes 917504 | tf_op jit(solution)/shard_map/all_to_all | solution.py:625
  44.6 0.0 all-gather.5.cloned.1.call-update
  44.7 6.5 %all-to-all-start.1 = ((bf16[32,72,128]{2,1,0:T(8,128)(2,1)}), bf16[32,72,128]{2,1,0:T(8,128)(2,1)S(1)}, u32[]{:S(2)}, u32[]{:S(2)}) async-start(bf16[32,72,128]{2,1,0:T(8,128)(2,1)} %get-tuple-element.22), calls=%async_computation.1 | async-start | bytes 1179648 | tf_op jit(solution)/shard_map/all_to_all | solution.py:625
  51.2 2.3 shard_map.105
  53.5 0.0 copy-start.8
  53.5 0.9 copy-done.8
  54.4 0.7 copy-done.10
  55.1 16.7 %all-to-all-done.1.weight = bf16[32,72,128]{2,1,0:T(8,128)(2,1)S(1)} async-done(((bf16[32,72,128]{2,1,0:T(8,128)(2,1)}), bf16[32,72,128]{2,1,0:T(8,128)(2,1)S(1)}, u32[]{:S(2)}, u32[]{:S(2)}) %all-to-all-start.1) | async-done | bytes 589856 | tf_op jit(solution)/shard_map/all_to_all | solution.py:625
  71.8 1.7 copy-done.1
  73.5 5.6 %shard_map.106 = (bf16[16,8,2944]{2,1,0:T(8,128)(2,1)S(1)}, f32[1024,256]{1,0:T(8,128)S(1)}, bf16[1024,128]{1,0:T(8,128)(2,1)S(1)}, f32[8,128,128]{2,1,0:T(8,128)S(1)}) custom-call(bf16[8,128,1152]{2,1,0:T(8,128)(2,1)S(1)} %bitcast.18, bf16[32,72,128]{2,1,0:T(8,128)(2,1)S(1)} %all-to-all-done.1.weight, bf16[128,1152]{1,0:T(8,128)(2,1)S(1)} %get-tuple-element.23.down, ...), custom_call_target="tpu_custom_call" | custom-call | flops 8000000000 | bytes 24000000 | tf_op jit(solution)/shard_map/pallas_call | solution.py:30
  79.1 1.0 copy-done.11
  80.0 0.8 copy-done.15
  80.8 27.7 %all_to_all.36.received_in = bf16[16,8,2944]{2,1,0:T(8,128)(2,1)} all-to-all(bf16[16,8,2944]{2,1,0:T(8,128)(2,1)S(1)} %get-tuple-element.25), channel_id=1, replica_groups=mesh['z'=8,'h'=4,'x'=4,'l'=2,'c'=2] {'x','l','c'}, dimensions={0} | all-to-all | bytes 1507328 | tf_op jit(solution)/shard_map/all_to_all | solution.py:625
  108.6 3.0 %all-gather.5.cloned.1.call-done = bf16[512,56,128]{2,1,0:T(8,128)(2,1)} async-done(((bf16[32,56,128]{2,1,0:T(8,128)(2,1)}), bf16[512,56,128]{2,1,0:T(8,128)(2,1)}) %all-gather.5.cloned.1.call-update) | async-done | bytes 7340048 | tf_op jit(solution)/shard_map/all_gather | solution.py:653
  111.6 19.5 %shard_map.107 = (bf16[16,64,128]{2,1,0:T(8,128)(2,1)}, bf16[128,1152]{1,0:T(8,128)(2,1)}, bf16[128,128]{1,0:T(8,128)(2,1)}, f32[8,128,256]{2,1,0:T(8,128)}, bf16[128,128]{1,0:T(8,128)(2,1)}) custom-call(bf16[16,32,56,128]{3,2,1,0:T(8,128)(2,1)} %bitcast.30, bf16[16,8,2944]{2,1,0:T(8,128)(2,1)} %all_to_all.36.received_in, f32[3,2,1152]{2,1,0:T(2,128)} %bitcast.34, ...), custom_call_target="tpu_custom_call" | custom-call | flops 24999999488 | bytes 75000000 | tf_op jit(solution)/shard_map/pallas_call | solution.py:30
  131.1 5.3 %all-to-all-start.3 = ((bf16[16,64,128]{2,1,0:T(8,128)(2,1)}), bf16[16,64,128]{2,1,0:T(8,128)(2,1)S(1)}, u32[]{:S(2)}, u32[]{:S(2)}) async-start(bf16[16,64,128]{2,1,0:T(8,128)(2,1)} %get-tuple-element.28), calls=%async_computation.3 | async-start | bytes 524288 | tf_op jit(solution)/shard_map/all_to_all | solution.py:625
  136.4 1.2 copy-done.7
  137.6 1.0 copy-done.9
  138.6 0.8 copy-done.13
  139.3 0.8 copy-done.14
  140.1 0.9 shard_map.109
  140.9 0.8 constant_dynamic-slice_fusion
  141.7 2.0 collective-permute-start.1
  143.7 0.0 all-to-all-done.3.cotangent
  143.8 1.2 copy-done.12
  145.0 1.0 copy-done.16
  146.0 0.9 copy-done.18
  147.0 5.5 %shard_map.108 = f32[64,11,128]{2,1,0:T(8,128)S(1)} custom-call(bf16[16,64,128]{2,1,0:T(8,128)(2,1)S(1)} %all-to-all-done.3.cotangent, bf16[192,256]{1,0:T(8,128)(2,1)S(1)} %get-tuple-element.24.up, bf16[8,128,1152]{2,1,0:T(8,128)(2,1)S(1)} %bitcast.19, f32[1024,256]{1,0:T(8,128)S(1)} %copy-done.12, bf16[1024,128]{1,0:T(8,128)(2,1)S(1)} %copy-done.18, ...), custom_call_target="tpu_custom_call" | custom-call | flops 20000000000 | bytes 60000000 | tf_op jit(solution)/shard_map/pallas_call | solution.py:30
  152.5 2.7 %collective-permute-start = (f32[32,11,128]{2,1,0:T(8,128)S(1)}, f32[32,11,128]{2,1,0:T(8,128)S(1)}, u32[]{:S(2)}, u32[]{:S(2)}) collective-permute-start(f32[32,11,128]{2,1,0:T(8,128)S(1)} %constant_dynamic-slice_fusion.1), channel_id=1, source_target_pairs={{0,1},{1,0},{2,3},{3,2},{4,5},{5,4},{6,7},{7,6},{8,9},{9,8},{10,11... | collective-permute-start | bytes 540680 | tf_op jit(solution)/shard_map/ppermute | solution.py:633
  155.2 0.0 collective-permute-done.1
  155.2 1.0 dynamic-slice_add_fusion
  156.3 0.1 collective-permute-done
  156.4 0.1 pad_maximum_fusion
  156.6 0.1 copy.19
  156.7 0.4 copy.20
  157.1 27.6 %all_to_all.37 = f32[32,9,4,128]{3,2,1,0:T(4,128)S(1)} all-to-all(f32[32,9,4,128]{3,2,1,0:T(4,128)S(1)} %copy.20), channel_id=1, replica_groups=mesh['z'=8,'h'=4,'x'=4,'l'=2,'c'=2] {'z','x'}, dimensions={0} | all-to-all | bytes 1179648 | tf_op jit(solution)/shard_map/all_to_all | solution.py:625
  184.7 0.1 copy.21
  185.0 14.1 %all_to_all.38 = f32[8,48,128]{2,1,0:T(8,128)S(1)} all-to-all(f32[8,48,128]{2,1,0:T(8,128)S(1)} %broadcast_in_dim.4), channel_id=1, replica_groups=mesh['z'=8,'h'=4,'x'=4,'l'=2,'c'=2] {'h','l'}, dimensions={0} | all-to-all | bytes 393216 | tf_op jit(solution)/shard_map/all_to_all | solution.py:625
  199.1 0.1 broadcast_in_dim.5
  199.1 23.5 %all_to_all.39.own = f32[32,48,128]{2,1,0:T(8,128)S(1)} all-to-all(f32[32,48,128]{2,1,0:T(8,128)S(1)} %broadcast_in_dim.5), channel_id=1, replica_groups=mesh['z'=8,'h'=4,'x'=4,'l'=2,'c'=2] {'z','x'}, dimensions={0} | all-to-all | bytes 1572864 | tf_op jit(solution)/shard_map/all_to_all | solution.py:625
  222.6 7.4 %collective-permute-start.2 = (f32[32,48,128]{2,1,0:T(8,128)S(1)}, f32[32,48,128]{2,1,0:T(8,128)S(1)}, u32[]{:S(2)}, u32[]{:S(2)}) collective-permute-start(f32[32,48,128]{2,1,0:T(8,128)S(1)} %all_to_all.39.own), channel_id=1, source_target_pairs={{0,1},{1,0},{2,3},{3,2},{4,5},{5,4},{6,7},{7,6},{8,9},{9,8},{10,11... | collective-permute-start | bytes 2359304 | tf_op jit(solution)/shard_map/ppermute | solution.py:633
  230.0 1.9 collective-permute-done.2.other
  231.9 2.4 shard_map.110
  (37 shorter events, 0.3 us)
Async XLA Ops:
  7.2 44.0 %copy-start.4 = (f32[2,1152,64]{1,2,0:T(8,128)S(1)}, f32[2,1152,64]{1,2,0:T(8,128)}, u32[]{:S(2)}) copy-start(f32[2,1152,64]{1,2,0:T(8,128)} %param.14) | copy-start | bytes 1769476
  7.2 44.0 %copy-start.3 = (f32[2,64,1728]{2,1,0:T(8,128)S(1)}, f32[2,64,1728]{2,1,0:T(8,128)}, u32[]{:S(2)}) copy-start(f32[2,64,1728]{2,1,0:T(8,128)} %up.1) | copy-start | bytes 2654212
  7.2 64.6 %all-gather.7.cloned.1.call-start = ((), (), s32[]{:S(2)}) async-start(), calls=%async_computation.8 | async-start | bytes 2654208 | tf_op jit(solution)/shard_map/all_gather | solution.py:652
  7.8 43.4 %copy-start = (s32[3]{0:T(128)S(1)}, s32[3]{0:T(128)}, u32[]{:S(2)}) copy-start(s32[3]{0:T(128)} %pad_add_fusion.place) | copy-start | bytes 40
  7.8 63.9 %copy-start.5 = (bf16[1,1,128,1152]{3,2,1,0:T(8,128)(2,1)S(1)}, bf16[1,1,128,1152]{3,2,1,0:T(8,128)(2,1)}, u32[]{:S(2)}) copy-start(bf16[1,1,128,1152]{3,2,1,0:T(8,128)(2,1)} %param.9) | copy-start | bytes 884740
  7.8 63.9 %copy-start.6 = (bf16[1,1,128,1152]{3,2,1,0:T(8,128)(2,1)S(1)}, bf16[1,1,128,1152]{3,2,1,0:T(8,128)(2,1)}, u32[]{:S(2)}) copy-start(bf16[1,1,128,1152]{3,2,1,0:T(8,128)(2,1)} %param.10) | copy-start | bytes 884740
  11.2 100.3 %all-gather.5.cloned.1.call-start = ((), (), s32[]{:S(2)}) async-start(), calls=%async_computation.7 | async-start | bytes 7798784 | tf_op jit(solution)/shard_map/all_gather | solution.py:653
  44.7 27.1 %all-to-all-start.1 = ((bf16[32,72,128]{2,1,0:T(8,128)(2,1)}), bf16[32,72,128]{2,1,0:T(8,128)(2,1)S(1)}, u32[]{:S(2)}, u32[]{:S(2)}) async-start(bf16[32,72,128]{2,1,0:T(8,128)(2,1)} %get-tuple-element.22), calls=%async_computation.1 | async-start | bytes 1179648 | tf_op jit(solution)/shard_map/all_to_all | solution.py:625
  53.5 0.9 copy-start.8
  54.4 0.7 copy-start.10
  71.8 1.7 copy-start.1
  79.1 1.0 copy-start.11
  80.0 0.8 copy-start.15
  80.8 30.7 %copy-start.17 = (bf16[1024,128]{1,0:T(8,128)(2,1)}, bf16[1024,128]{1,0:T(8,128)(2,1)S(1)}, u32[]{:S(2)}) copy-start(bf16[1024,128]{1,0:T(8,128)(2,1)S(1)} %get-tuple-element.30.reduced) | copy-start | bytes 786436
  131.1 12.7 %copy-start.2 = (bf16[1024,1152]{1,0:T(8,128)(2,1)S(1)}, bf16[1024,1152]{1,0:T(8,128)(2,1)}, u32[]{:S(2)}) copy-start(bf16[1024,1152]{1,0:T(8,128)(2,1)} %all-gather.7.cloned.1.call-done) | copy-start | bytes 7077892
  131.1 12.7 %all-to-all-start.3 = ((bf16[16,64,128]{2,1,0:T(8,128)(2,1)}), bf16[16,64,128]{2,1,0:T(8,128)(2,1)S(1)}, u32[]{:S(2)}, u32[]{:S(2)}) async-start(bf16[16,64,128]{2,1,0:T(8,128)(2,1)} %get-tuple-element.28), calls=%async_computation.3 | async-start | bytes 524288 | tf_op jit(solution)/shard_map/all_to_all | solution.py:625
  136.4 1.2 copy-start.7
  137.6 1.0 copy-start.9
  138.6 0.8 copy-start.13
  139.3 0.8 copy-start.14
  141.7 13.5 %collective-permute-start.1 = (f32[32,23,128]{2,1,0:T(8,128)}, f32[32,23,128]{2,1,0:T(8,128)}, u32[]{:S(2)}, u32[]{:S(2)}) collective-permute-start(f32[32,23,128]{2,1,0:T(8,128)} %constant_dynamic-slice_fusion), channel_id=1, source_target_pairs={{0,1},{1,0},{2,3},{3,2},{4,5},{5,4},{6,7},{7,6},{8,9},{9,8},{10,11... | collective-permute-start | bytes 1130504 | tf_op jit(solution)/shard_map/ppermute | solution.py:633
  143.8 1.2 copy-start.12
  145.0 1.0 copy-start.16
  146.0 0.9 copy-start.18
  152.5 3.8 %collective-permute-start = (f32[32,11,128]{2,1,0:T(8,128)S(1)}, f32[32,11,128]{2,1,0:T(8,128)S(1)}, u32[]{:S(2)}, u32[]{:S(2)}) collective-permute-start(f32[32,11,128]{2,1,0:T(8,128)S(1)} %constant_dynamic-slice_fusion.1), channel_id=1, source_target_pairs={{0,1},{1,0},{2,3},{3,2},{4,5},{5,4},{6,7},{7,6},{8,9},{9,8},{10,11... | collective-permute-start | bytes 540680 | tf_op jit(solution)/shard_map/ppermute | solution.py:633
  222.6 9.3 %collective-permute-start.2 = (f32[32,48,128]{2,1,0:T(8,128)S(1)}, f32[32,48,128]{2,1,0:T(8,128)S(1)}, u32[]{:S(2)}, u32[]{:S(2)}) collective-permute-start(f32[32,48,128]{2,1,0:T(8,128)S(1)} %all_to_all.39.own), channel_id=1, source_target_pairs={{0,1},{1,0},{2,3},{3,2},{4,5},{5,4},{6,7},{7,6},{8,9},{9,8},{10,11... | collective-permute-start | bytes 2359304 | tf_op jit(solution)/shard_map/ppermute | solution.py:633
Sparse Core Ops, SparseCore 0:
  11.3 36.8 all-gather.6
  50.3 61.1 all-gather.4
